TPU v7x, 32 devices: a whole 2x2x4 slice. The times are simulated.
32 devices in a mesh: ta: 4 (over y, core), gz: 4 (over z), xy: 2 (over x).
Axes of the slice: x: 2, y: 2, z: 4, core: 2. Of those that a mesh axis runs over, the one named last changes fastest.
Arguments:
- right_side: float32 [2, 3, 16, 16, 8, 16], P(None, None, 'ta', 'gz', 'xy'), may hold values from -6 to 6
- links: bfloat16 [3, 3, 16, 16, 8, 256], P(None, None, 'ta', 'gz', 'xy'), may hold values from -0.59765625 to 0.59765625
- block_inverse: bfloat16 [48, 8, 8, 4, 768], P(None, 'ta', 'gz', 'xy')
- near_fine: bfloat16 [24, 8, 8, 4, 768], P(None, 'ta', 'gz', 'xy'), may hold values from -0.875 to 0.875
- mid_stencil: bfloat16 [9, 24, 8, 8, 4, 384], P(None, None, 'ta', 'gz', 'xy')
- mid_jacobi: bfloat16 [24, 8, 8, 4, 384], P(None, 'ta', 'gz', 'xy')
- near_mid: bfloat16 [48, 4, 4, 2, 3072], P(None, 'ta', 'gz', 'xy'), may hold values from -0.3125 to 0.3125
- coarse_stencil: bfloat16 [9, 2, 4, 4, 2, 192, 48], P(None, None, 'ta', 'gz', 'xy')
- coarse_jacobi: bfloat16 [2, 4, 4, 2, 192, 48], P(None, 'ta', 'gz', 'xy')
Outputs:
- solution: float32 [2, 3, 16, 16, 8, 16], P(None, None, 'ta', 'gz', 'xy')
- residual: float32 [2, 3, 16, 16, 8, 16], P(None, None, 'ta', 'gz', 'xy')
All inputs are finite; a program needn't handle non-finite values.
Results may differ from a plain program's by a relative error of at most 0.0003.
Values may be sent and summed in bfloat16 or wider, within the bound.
No kernel may reach another device: no remote copies, remote signals or barrier semaphores. Data moves between devices by JAX's collectives and lax.ppermute only.
A program may use at most 256 MiB of HBM per device.

v0:
```python
import jax
import jax.numpy as jnp
from jax import lax
from jax.sharding import PartitionSpec as P
import jax.experimental.pallas as pl
from jax.experimental.pallas import tpu as pltpu

SWEEPS = 4
CYCLES = 2
F32 = jnp.float32
BF16 = jnp.bfloat16
HIGHEST = lax.Precision.HIGHEST
LANE_BITS = (64, 32, 16)
ROW_BITS = (4, 2, 1)
VMEM_BYTES = 24 << 20


class Site:
    def __init__(self):
        self.lane = lax.broadcasted_iota(jnp.int32, (8, 128), 1)
        self.row = lax.broadcasted_iota(jnp.int32, (8, 128), 0)
        self.by = self.lane & 7

    def lane_bit(self, d):
        return (self.lane & d) != 0

    def row_bit(self, d):
        return (self.row & d) != 0

    def first(self, direction):
        return ((self.lane & LANE_BITS[direction]) | (self.row & ROW_BITS[direction])) == 0

    def last(self, direction):
        return self.lane_bit(LANE_BITS[direction]) & self.row_bit(ROW_BITS[direction])


def left(x, s):
    s = s % 128
    return pltpu.roll(x, (128 - s) % 128, 1) if s else x


def up(x, s):
    s = s % 8
    return pltpu.roll(x, (8 - s) % 8, 0) if s else x


def flip_lane(site, x, d):
    if d == 64:
        return left(x, 64)
    return jnp.where(site.lane_bit(d), left(x, -d), left(x, d))


def flip_row(site, x, d):
    if d == 4:
        return up(x, 4)
    return jnp.where(site.row_bit(d), up(x, -d), up(x, d))


def cyclic(site, x, direction, sign):
    d = LANE_BITS[direction]
    flipped = flip_lane(site, x, d)
    both = flip_row(site, flipped, ROW_BITS[direction])
    if sign > 0:
        return jnp.where(site.lane_bit(d), both, flipped)
    return jnp.where(site.lane_bit(d), flipped, both)


def by_roll(site, x, base, q):
    moved = left(x, base + q)
    if q == 0:
        return moved
    if q > 0:
        return jnp.where(site.by >= 8 - q, left(x, base + q - 8), moved)
    return jnp.where(site.by < -q, left(x, base + q + 8), moved)


def shift_y(site, x, n):
    found = []
    for c in (0, 1):
        c_new = (c + n) % 2
        q = (c + n - c_new) // 2
        found.append(by_roll(site, x, 8 * (c_new - c), q))
    return jnp.where(site.lane_bit(8), found[1], found[0])


def link(links_ref, mu, kind, part, r, c):
    return links_ref[((mu * 2 + kind) * 2 + part) * 9 + r * 3 + c]


def link_apply(links_ref, mu, kind, field):
    out = [None] * 6
    for r in range(3):
        re = im = None
        for c in range(3):
            g_re = link(links_ref, mu, kind, 0, r, c)
            g_im = link(links_ref, mu, kind, 1, r, c)
            a = g_re * field[c] - g_im * field[3 + c]
            b = g_re * field[3 + c] + g_im * field[c]
            re = a if re is None else re + a
            im = b if im is None else im + b
        out[r] = re
        out[3 + r] = im
    return out


def link_adjoint(links_ref, mu, kind, field):
    out = [None] * 6
    for c in range(3):
        re = im = None
        for r in range(3):
            g_re = link(links_ref, mu, kind, 0, r, c)
            g_im = link(links_ref, mu, kind, 1, r, c)
            a = g_re * field[r] + g_im * field[3 + r]
            b = g_re * field[3 + r] - g_im * field[r]
            re = a if re is None else re + a
            im = b if im is None else im + b
        out[c] = re
        out[3 + c] = im
    return out


def add(xs, ys):
    return [x + y for x, y in zip(xs, ys)]


def sub(xs, ys):
    return [x - y for x, y in zip(xs, ys)]


def fine_send(site, links_ref, field, acc_ref, sent_refs):
    acc = list(field)
    for kind, reach in ((0, 1), (1, 3)):
        acc = add(acc, link_apply(links_ref, 3, kind, [shift_y(site, x, reach) for x in field]))
        back = link_adjoint(links_ref, 3, kind, field)
        acc = sub(acc, [shift_y(site, x, -reach) for x in back])
    for direction in range(3):
        near = [cyclic(site, x, direction, -1) for x in link_adjoint(links_ref, direction, 0, field)]
        far = link_adjoint(links_ref, direction, 1, field)
        first, last = site.first(direction), site.last(direction)
        ref, base = sent_refs[direction]
        for i in range(6):
            ref[base + i] = jnp.where(first, near[i], far[i])
        acc = [
            a - jnp.where(first, 0.0, n) - jnp.where(last, cyclic(site, f, direction, 1), 0.0)
            for a, n, f in zip(acc, near, far)
        ]
    for i in range(6):
        acc_ref[i] = acc[i]


def fine_receive(site, links_ref, field, acc, ahead, behind):
    out = acc
    for direction in range(3):
        first, last = site.first(direction), site.last(direction)
        nxt = ahead[direction]
        one = [cyclic(site, jnp.where(first, n, x), direction, 1) for n, x in zip(nxt, field)]
        out = add(out, link_apply(links_ref, direction, 0, one))
        three = [cyclic(site, jnp.where(last, x, n), direction, -1) for n, x in zip(nxt, field)]
        out = add(out, link_apply(links_ref, direction, 1, three))
        out = [
            o - jnp.where(first, b, 0.0) - jnp.where(last, 0.0, cyclic(site, b, direction, 1))
            for o, b in zip(out, behind[direction])
        ]
    return out


def merge(site, d, a, b):
    bit = site.lane_bit(d)
    return jnp.where(bit, b, a) + left(jnp.where(bit, a, b), d)


def tree(site, leaf, base, n):
    if n == 2:
        a, b = leaf(base)
    else:
        a = tree(site, leaf, base, n // 2)
        b = tree(site, leaf, base + n // 2, n // 2)
    return [merge(site, 4 * n, x, y) for x, y in zip(a, b)]


def two_rows(ref, o):
    return ref[pl.ds(o * 8, 16), :].astype(F32)


def dot_tiles(block, row, x):
    total = None
    for j, v in enumerate(x):
        term = block[row : row + 8, 128 * j : 128 * j + 128] * v
        total = term if total is None else total + term
    return total


def pair_leaf(terms):
    def leaf(o):
        sums = [[None, None], [None, None]]
        for ref, base, x_re, x_im in terms:
            block = two_rows(ref, base + o)
            for h in range(2):
                for p, x in enumerate((x_re, x_im)):
                    t = dot_tiles(block, 8 * h, x)
                    sums[h][p] = t if sums[h][p] is None else sums[h][p] + t
        return sums

    return leaf


def fine_matrix(site, ref, field):
    x_re = field[:3] + [-x for x in field[3:]]
    x_im = field[3:] + field[:3]
    out = [tree(site, pair_leaf([(ref, 0, x_re, x_im)]), 16 * c, 16) for c in range(3)]
    return [o[0] for o in out] + [o[1] for o in out]


def mid_gather(site, terms):
    leaf = pair_leaf(terms)
    eight = [tree(site, leaf, 8 * j, 8) for j in range(3)]
    return [
        merge(site, 64, eight[0][0], eight[1][0]),
        merge(site, 64, eight[2][0], eight[0][1]),
        merge(site, 64, eight[1][1], eight[2][1]),
    ]


def swap_parts(site, v):
    low = jnp.logical_not(site.lane_bit(64))
    r = [left(x, 64) for x in v]
    return [jnp.where(low, r[1], r[2]), jnp.where(low, r[2], r[0]), jnp.where(low, r[0], r[1])]


def im_negated(site, v):
    return [v[0], jnp.where(site.lane_bit(64), -v[1], v[1]), -v[2]]


def mid_x(site, v):
    return im_negated(site, v), swap_parts(site, v)


def mid_x_conj(site, v):
    return v, im_negated(site, swap_parts(site, v))


def restrict_fine(site, near_ref, field):
    x_im = field[3:] + [-x for x in field[:3]]
    return mid_gather(site, [(near_ref, 0, field, x_im)])


def mid_matrix(site, ref, v):
    x_re, x_im = mid_x(site, v)
    return mid_gather(site, [(ref, 0, x_re, x_im)])


def mid_stencil_apply(site, ref, v, ahead, behind):
    shifted = [v]
    for direction in range(3):
        d = ROW_BITS[direction]
        bit = site.row_bit(d)
        shifted.append([flip_row(site, jnp.where(bit, x, n), d) for x, n in zip(v, ahead[direction])])
        shifted.append([flip_row(site, jnp.where(bit, n, x), d) for x, n in zip(v, behind[direction])])
    shifted.append([by_roll(site, x, 0, 1) for x in v])
    shifted.append([by_roll(site, x, 0, -1) for x in v])
    return mid_gather(site, [(ref, 24 * k) + mid_x(site, s) for k, s in enumerate(shifted)])


def spread(site, v, ref):
    def down(x, base, d):
        if d == 4:
            ref[base] = x
            return
        bit = site.lane_bit(d)
        r = left(x, d)
        down(jnp.where(bit, r, x), base, d // 2)
        down(jnp.where(bit, x, r), base + d // 8, d // 2)

    for j, x in enumerate(v):
        down(x, 16 * j, 64)


def prolong_fine(site, near_ref, v, spread_ref):
    spread(site, v, spread_ref)
    a, b = [0.0] * 6, [0.0] * 6
    for o in range(0, 24, 2):
        block = two_rows(near_ref, o)
        for h in range(2):
            y_re, y_im = spread_ref[o + h], spread_ref[24 + o + h]
            for j in range(6):
                n = block[8 * h : 8 * h + 8, 128 * j : 128 * j + 128]
                a[j] = a[j] + n * y_re
                b[j] = b[j] + n * y_im
    return [a[j] - b[3 + j] for j in range(3)] + [a[3 + j] + b[j] for j in range(3)]


def iota2(shape, axis):
    return lax.broadcasted_iota(jnp.int32, shape, axis)


def pick_y(part):
    row, lane = iota2((8, 128), 0), iota2((8, 128), 1)
    return (row == part * 4 + ((lane & 7) >> 1)).astype(F32)


def restrict_mid(site, near_ref, v, tile_ref):
    x_re, x_im = mid_x_conj(site, v)
    for o in range(0, 48, 2):
        block = two_rows(near_ref, o)
        for h in range(2):
            tile_ref[0, pl.ds(8 * (o + h), 8), :] = dot_tiles(block, 8 * h, x_re)
            tile_ref[1, pl.ds(8 * (o + h), 8), :] = dot_tiles(block, 8 * h, x_im)
    dims = (((1,), (1,)), ((), ()))
    z = None
    for p in range(2):
        t = lax.dot_general(pick_y(p), tile_ref[p], dims, precision=HIGHEST, preferred_element_type=F32)
        z = t if z is None else z + t
    select = ((iota2((384, 48), 0) >> 3) == iota2((384, 48), 1)).astype(F32)
    return jnp.dot(z, select, precision=HIGHEST, preferred_element_type=F32)


def prolong_mid(site, near_ref, y3, row_ref):
    dims = (((0,), (0,)), ((), ()))
    for p in range(2):
        row_ref[p] = lax.dot_general(y3, pick_y(p), dims, precision=HIGHEST, preferred_element_type=F32)
    a, b = [0.0] * 3, [0.0] * 3
    for o in range(0, 48, 2):
        block = two_rows(near_ref, o)
        for h in range(2):
            y_re = jnp.broadcast_to(row_ref[0, pl.ds(o + h, 1), :], (8, 128))
            y_im = jnp.broadcast_to(row_ref[1, pl.ds(o + h, 1), :], (8, 128))
            for j in range(3):
                n = block[8 * h : 8 * h + 8, 128 * j : 128 * j + 128]
                a[j] = a[j] + n * y_re
                b[j] = b[j] + n * y_im
    return add(a, swap_parts(site, [-x for x in im_negated_keep(site, b)]))


def im_negated_keep(site, v):
    return [-v[0], jnp.where(site.lane_bit(64), v[1], -v[1]), v[2]]


def coarse_rows(v):
    high = v.astype(BF16).astype(F32)
    return jnp.concatenate([high, v - high], axis=0).astype(BF16)


def coarse_matrix(terms):
    row = iota2((8, 48), 0)
    total = None
    for ref, base, v in terms:
        turned = jnp.where(row < 4, -up(v, 4), up(v, 4))
        for a, x in enumerate((v, turned)):
            t = jnp.dot(coarse_rows(x), ref[pl.ds(base + 48 * a, 48), :], preferred_element_type=F32)
            total = t if total is None else total + t
    both = total[:8] + total[8:]
    out = None
    for y in range(4):
        t = jnp.where((row & 3) == y, both[:, 48 * y : 48 * y + 48], 0.0)
        out = t if out is None else out + t
    return out


def coarse_stencil_apply(ref, v, ahead, behind):
    y = iota2((8, 48), 0) & 3
    shifted = [v]
    for direction in range(3):
        shifted += [ahead[direction], behind[direction]]
    shifted.append(jnp.where(y == 3, up(v, -3), up(v, 1)))
    shifted.append(jnp.where(y == 0, up(v, 3), up(v, -1)))
    return coarse_matrix([(ref, 96 * k, s) for k, s in enumerate(shifted)])


def load(ref, n, base=0):
    return [ref[base + i] for i in range(n)]


def store(ref, values, base=0):
    for i, x in enumerate(values):
        ref[base + i] = x


def finish_fine(site, links_ref, solution, sol_ref, acc_ref, pt_ref, pz_ref, mx_ref):
    store(sol_ref, solution)
    store(mx_ref, solution)
    fine_send(site, links_ref, solution, acc_ref, ((pt_ref, 0), (pz_ref, 0), (mx_ref, 6)))


def begin_fine(site, links_ref, refs):
    sol_ref, acc_ref, nz, bz, nt, bt, mx = refs
    solution = load(sol_ref, 6)
    ahead = [load(nt, 6), load(nz, 6), load(mx, 6)]
    behind = [load(bt, 6), load(bz, 6), load(mx, 6, 6)]
    return solution, fine_receive(site, links_ref, solution, load(acc_ref, 6), ahead, behind)


def kernel_first(links_ref, block_ref, rhs_ref, *outs):
    site = Site()
    solution = fine_matrix(site, block_ref, load(rhs_ref, 6))
    finish_fine(site, links_ref, solution, *outs)


def kernel_smooth(links_ref, block_ref, rhs_ref, *refs):
    site = Site()
    solution, applied = begin_fine(site, links_ref, refs[:7])
    residual = sub(load(rhs_ref, 6), applied)
    solution = add(solution, fine_matrix(site, block_ref, residual))
    finish_fine(site, links_ref, solution, *refs[7:])


def kernel_last(links_ref, rhs_ref, *refs):
    site = Site()
    _, applied = begin_fine(site, links_ref, refs[:7])
    store(refs[7], sub(load(rhs_ref, 6), applied))


def kernel_restrict(links_ref, near_ref, jacobi_ref, rhs_ref, *refs):
    site = Site()
    _, applied = begin_fine(site, links_ref, refs[:7])
    residual = sub(load(rhs_ref, 6), applied)
    mid_res = restrict_fine(site, near_ref, residual)
    store(refs[7], mid_res)
    store(refs[8], mid_matrix(site, jacobi_ref, mid_res))


def neighbours(refs, get):
    nz, bz, nt, bt = refs[:4]
    nx = refs[4]
    bx = refs[-1]
    ahead = [get(nt), get(nz), get(nx)]
    return ahead, [get(bt), get(bz), get(bx)]


def kernel_mid_down(stencil_ref, near_ref, jacobi_ref, res_ref, sol_ref, *refs):
    site = Site()
    around, (r3_ref, y3_ref, tile_ref) = refs[:-3], refs[-3:]
    ahead, behind = neighbours(around, lambda r: load(r, 3))
    applied = mid_stencil_apply(site, stencil_ref, load(sol_ref, 3), ahead, behind)
    r3 = restrict_mid(site, near_ref, sub(load(res_ref, 3), applied), tile_ref)
    r3_ref[...] = r3
    y3_ref[...] = coarse_matrix([(jacobi_ref, 0, r3)])


def sweep(stencil_ref, jacobi_ref, r3_ref, y3_ref, around):
    ahead, behind = neighbours(around, lambda r: r[...])
    y3 = y3_ref[...]
    rest = r3_ref[...] - coarse_stencil_apply(stencil_ref, y3, ahead, behind)
    return y3 + coarse_matrix([(jacobi_ref, 0, rest)])


def kernel_sweep(stencil_ref, jacobi_ref, r3_ref, y3_ref, *refs):
    refs[-1][...] = sweep(stencil_ref, jacobi_ref, r3_ref, y3_ref, refs[:-1])


def kernel_sweep_up(stencil_ref, jacobi_ref, near_ref, y2_ref, r3_ref, y3_ref, *refs):
    site = Site()
    around, (out_ref, row_ref) = refs[:-2], refs[-2:]
    y3 = sweep(stencil_ref, jacobi_ref, r3_ref, y3_ref, around)
    store(out_ref, add(load(y2_ref, 3), prolong_mid(site, near_ref, y3, row_ref)))


def kernel_mid_up(links_ref, stencil_ref, jacobi_ref, near_ref, old_ref, res_ref, y2_ref, *refs):
    site = Site()
    around, outs, spread_ref = refs[:-6], refs[-6:-1], refs[-1]
    ahead, behind = neighbours(around, lambda r: load(r, 3))
    y2 = load(y2_ref, 3)
    rest = sub(load(res_ref, 3), mid_stencil_apply(site, stencil_ref, y2, ahead, behind))
    y2 = add(y2, mid_matrix(site, jacobi_ref, rest))
    solution = add(load(old_ref, 6), prolong_fine(site, near_ref, y2, spread_ref))
    finish_fine(site, links_ref, solution, *outs)


def call(kernel, outs, scratch, *args):
    return pl.pallas_call(
        kernel,
        out_shape=[jax.ShapeDtypeStruct(s, F32) for s in outs],
        scratch_shapes=[pltpu.VMEM(s, F32) for s in scratch],
        compiler_params=pltpu.CompilerParams(vmem_limit_bytes=VMEM_BYTES),
        name=kernel.__name__,
    )(*args)


def from_behind(block, axis, distance):
    n = lax.axis_size(axis)
    return lax.ppermute(block, axis, [((i - distance) % n, i) for i in range(n)])


def exchange(v):
    around = [
        from_behind(v, "gz", -1),
        from_behind(v, "gz", 1),
        from_behind(v, "ta", -1),
        from_behind(v, "ta", 1),
        from_behind(v, "xy", -1),
    ]
    if lax.axis_size("xy") > 2:
        around.append(from_behind(v, "xy", 1))
    return around


def exchange_fine(sol, acc, pt, pz, mx):
    if lax.axis_size("xy") == 2:
        moved = from_behind(mx, "xy", 1)
    else:
        moved = jnp.concatenate([from_behind(mx[:6], "xy", -1), from_behind(mx[6:], "xy", 1)])
    return [
        sol,
        acc,
        from_behind(sol, "gz", -1),
        from_behind(pz, "gz", 1),
        from_behind(sol, "ta", -1),
        from_behind(pt, "ta", 1),
        moved,
    ]


TILE6 = (6, 8, 128)
FINE_OUT = [TILE6, TILE6, TILE6, TILE6, (12, 8, 128)]


def to_tiles(field):
    folded = field.reshape(6, 2, 2, 2, 2, 2, 2, 8, 2)
    return folded.transpose(0, 1, 3, 5, 2, 4, 6, 8, 7).reshape(TILE6)


def from_tiles(tiles, shape):
    folded = tiles.reshape(6, 2, 2, 2, 2, 2, 2, 2, 8)
    return folded.transpose(0, 1, 4, 2, 5, 3, 6, 8, 7).reshape(shape)


def link_tiles(links):
    folded = links.reshape(9, 2, 2, 2, 2, 2, 2, 16, 8, 2)
    tiles = folded.transpose(7, 0, 1, 3, 5, 2, 4, 6, 9, 8).reshape(4, 36, 8, 128).astype(F32)
    lane = lax.iota(jnp.int32, 128)
    ct, cz, cx = (lane >> 6) & 1, (lane >> 5) & 1, (lane >> 4) & 1
    odd = jnp.stack([0 * ct, ct, ct ^ cz, ct ^ cz ^ cx]).astype(F32)
    return (tiles * (0.5 - odd)[:, None, None, :]).reshape(144, 8, 128)


def local(
    right_side,
    links,
    block_inverse,
    near_fine,
    mid_stencil,
    mid_jacobi,
    near_mid,
    coarse_stencil,
    coarse_jacobi,
):
    g = link_tiles(links)
    rhs = to_tiles(right_side)
    block = block_inverse.reshape(384, 768)
    near1 = near_fine.reshape(192, 768)
    stencil2 = mid_stencil.reshape(1728, 384)
    jacobi2 = mid_jacobi.reshape(192, 384)
    near2 = near_mid.reshape(48, 48, 8, 2, 4).transpose(0, 2, 1, 4, 3).reshape(384, 384)
    stencil3 = jnp.swapaxes(coarse_stencil, 5, 6).reshape(864, 192)
    jacobi3 = jnp.swapaxes(coarse_jacobi, 4, 5).reshape(96, 192)
    mid = (3, 8, 128)
    coarse = (8, 48)

    state = call(kernel_first, FINE_OUT, [], g, block, rhs)
    for cycle_no in range(CYCLES):
        r2, y2 = call(kernel_restrict, [mid, mid], [], g, near1, jacobi2, rhs, *exchange_fine(*state))
        r3, y3 = call(
            kernel_mid_down, [coarse, coarse], [(2, 384, 128)], stencil2, near2, jacobi3, r2, y2, *exchange(y2)
        )
        for _ in range(SWEEPS - 1):
            (y3,) = call(kernel_sweep, [coarse], [], stencil3, jacobi3, r3, y3, *exchange(y3))
        (y2,) = call(
            kernel_sweep_up, [mid], [(2, 48, 128)], stencil3, jacobi3, near2, y2, r3, y3, *exchange(y3)
        )
        state = call(
            kernel_mid_up, FINE_OUT, [(48, 8, 128)], g, stencil2, jacobi2, near1, state[0], r2, y2, *exchange(y2)
        )
        state = call(kernel_smooth, FINE_OUT, [], g, block, rhs, *exchange_fine(*state))
        if cycle_no < CYCLES - 1:
            state = call(kernel_smooth, FINE_OUT, [], g, block, rhs, *exchange_fine(*state))
    (residual,) = call(kernel_last, [TILE6], [], g, rhs, *exchange_fine(*state))
    return from_tiles(state[0], right_side.shape), from_tiles(residual, right_side.shape)


def solution(mesh):
    return jax.shard_map(
        local,
        mesh=mesh,
        in_specs=(
            P(None, None, "ta", "gz", "xy", None),
            P(None, None, "ta", "gz", "xy", None),
            P(None, "ta", "gz", "xy", None),
            P(None, "ta", "gz", "xy", None),
            P(None, None, "ta", "gz", "xy", None),
            P(None, "ta", "gz", "xy", None),
            P(None, "ta", "gz", "xy", None),
            P(None, None, "ta", "gz", "xy", None, None),
            P(None, "ta", "gz", "xy", None, None),
        ),
        out_specs=(P(None, None, "ta", "gz", "xy", None), P(None, None, "ta", "gz", "xy", None)),
        check_vma=False,
    )
```

profile of v0, /device:TPU:0, one launch (start us, length us, event | category | flops | bytes accessed | tf_op | source)
XLA Modules:
  0.0 308.6 jit_solution(9714867572028000076)
XLA Ops:
  0.7 39.4 %reshape.133 = f32[9,2,2,2,2,2,2,16,8,2]{9,8,7,6,5,4,3,2,1,0:T(8,128)} reshape(bf16[3,3,4,4,4,256]{5,4,3,2,1,0:T(4,128)(2,1)} %param.10) | data formatting | bytes 884736 | tf_op jit(solution)/shard_map/convert_element_type | solution.py:528
  40.1 57.6 %copy.30 = f32[16,9,2,2,2,2,2,2,2,8]{9,8,7,6,5,4,3,2,1,0:T(2,128)} copy(f32[16,9,2,2,2,2,2,2,2,8]{8,9,0,7,4,6,3,5,2,1:T(8,128)} %bitcast.42) | data formatting | bytes 1179648 | tf_op jit(solution)/shard_map/convert_element_type | solution.py:528
  97.6 13.2 %reshape.134 = f32[144,8,128]{2,1,0:T(8,128)S(1)} reshape(f32[16,9,2,2,2,2,2,2,2,8]{9,8,7,6,5,4,3,2,1,0:T(2,128)} %copy.30) | data formatting | bytes 1179648 | tf_op jit(solution)/shard_map/convert_element_type | solution.py:528
  118.8 3.6 %collective-permute-start = (f32[6,8,128]{2,1,0:T(8,128)S(1)}, f32[6,8,128]{2,1,0:T(8,128)S(1)}, u32[]{:S(2)}, u32[]{:S(2)}) collective-permute-start(f32[6,8,128]{2,1,0:T(8,128)S(1)} %get-tuple-element.40.refs_0_.old_ref), channel_id=1, source_target_pairs={{2,0},{4,2},{6,4},{0,6},{3,1},{5,3},{7,5},{1,7},{10,8},{12,10},{14... | collective-permute-start | bytes 73736 | tf_op jit(solution)/shard_map/ppermute | solution.py:480
  125.0 3.4 %collective-permute-done.1.refs_3_ = f32[6,8,128]{2,1,0:T(8,128)S(1)} collective-permute-done((f32[6,8,128]{2,1,0:T(8,128)S(1)}, f32[6,8,128]{2,1,0:T(8,128)S(1)}, u32[]{:S(2)}, u32[]{:S(2)}) %collective-permute-start.1) | collective-permute-done | bytes 24608 | tf_op jit(solution)/shard_map/ppermute | solution.py:480
  133.1 3.2 %reshape.121.stencil_ref = bf16[1728,384]{1,0:T(8,128)(2,1)S(1)} reshape(bf16[9,24,2,2,2,384]{5,4,3,2,1,0:T(2,128)(2,1)} %param.13) | data formatting | bytes 2654208 | tf_op jit(solution)/shard_map/reshape | solution.py:550
  138.5 4.8 %copy.21 = bf16[48,8,48,4,2]{1,0,4,3,2:T(8,128)(2,1)} copy(bf16[48,8,48,4,2]{0,3,4,1,2:T(4,128)(2,1)} %bitcast.43) | data formatting | bytes 589824 | tf_op jit(solution)/shard_map/transpose | solution.py:552
  143.2 7.1 %reshape.127 = bf16[384,384]{0,1:T(8,128)(2,1)} reshape(bf16[48,8,48,4,2]{1,0,4,3,2:T(8,128)(2,1)} %copy.21) | data formatting | bytes 589824 | tf_op jit(solution)/shard_map/reshape | solution.py:552
  155.1 3.3 %collective-permute-start.10 = (f32[8,48]{1,0:T(8,128)S(1)}, f32[8,48]{1,0:T(8,128)S(1)}, u32[]{:S(2)}, u32[]{:S(2)}) collective-permute-start(f32[8,48]{1,0:T(8,128)S(1)} %get-tuple-element.48.y3_ref), channel_id=1, source_target_pairs={{2,0},{4,2},{6,4},{0,6},{3,1},{5,3},{7,5},{1,7},{10,8},{12,10},{14... | collective-permute-start | bytes 4616 | tf_op jit(solution)/shard_map/ppermute | solution.py:480
  160.6 3.1 %collective-permute-done.11.refs_1_ = f32[8,48]{1,0:T(8,128)S(1)} collective-permute-done((f32[8,48]{1,0:T(8,128)S(1)}, f32[8,48]{1,0:T(8,128)S(1)}, u32[]{:S(2)}, u32[]{:S(2)}) %collective-permute-start.11) | collective-permute-done | bytes 1568 | tf_op jit(solution)/shard_map/ppermute | solution.py:480
  169.6 3.3 %collective-permute-done.16.refs_1_ = f32[8,48]{1,0:T(8,128)S(1)} collective-permute-done((f32[8,48]{1,0:T(8,128)S(1)}, f32[8,48]{1,0:T(8,128)S(1)}, u32[]{:S(2)}, u32[]{:S(2)}) %collective-permute-start.16) | collective-permute-done | bytes 1568 | tf_op jit(solution)/shard_map/ppermute | solution.py:480
  178.0 3.4 %collective-permute-done.21.refs_1_ = f32[8,48]{1,0:T(8,128)S(1)} collective-permute-done((f32[8,48]{1,0:T(8,128)S(1)}, f32[8,48]{1,0:T(8,128)S(1)}, u32[]{:S(2)}, u32[]{:S(2)}) %collective-permute-start.21) | collective-permute-done | bytes 1568 | tf_op jit(solution)/shard_map/ppermute | solution.py:480
  186.4 3.4 %collective-permute-done.26.refs_1_ = f32[8,48]{1,0:T(8,128)S(1)} collective-permute-done((f32[8,48]{1,0:T(8,128)S(1)}, f32[8,48]{1,0:T(8,128)S(1)}, u32[]{:S(2)}, u32[]{:S(2)}) %collective-permute-start.26) | collective-permute-done | bytes 1568 | tf_op jit(solution)/shard_map/ppermute | solution.py:480
  196.8 3.5 %collective-permute-done.31.refs_1_ = f32[3,8,128]{2,1,0:T(8,128)S(1)} collective-permute-done((f32[3,8,128]{2,1,0:T(8,128)S(1)}, f32[3,8,128]{2,1,0:T(8,128)S(1)}, u32[]{:S(2)}, u32[]{:S(2)}) %collective-permute-start.31) | collective-permute-done | bytes 12320 | tf_op jit(solution)/shard_map/ppermute | solution.py:480
  209.3 4.1 %collective-permute-done.36.refs_3_ = f32[6,8,128]{2,1,0:T(8,128)S(1)} collective-permute-done((f32[6,8,128]{2,1,0:T(8,128)S(1)}, f32[6,8,128]{2,1,0:T(8,128)S(1)}, u32[]{:S(2)}, u32[]{:S(2)}) %collective-permute-start.36) | collective-permute-done | bytes 24608 | tf_op jit(solution)/shard_map/ppermute | solution.py:480
  218.7 3.2 %collective-permute-done.41.refs_3_ = f32[6,8,128]{2,1,0:T(8,128)S(1)} collective-permute-done((f32[6,8,128]{2,1,0:T(8,128)S(1)}, f32[6,8,128]{2,1,0:T(8,128)S(1)}, u32[]{:S(2)}, u32[]{:S(2)}) %collective-permute-start.41) | collective-permute-done | bytes 24608 | tf_op jit(solution)/shard_map/ppermute | solution.py:480
  228.2 3.2 %collective-permute-done.46.refs_3_ = f32[6,8,128]{2,1,0:T(8,128)S(1)} collective-permute-done((f32[6,8,128]{2,1,0:T(8,128)S(1)}, f32[6,8,128]{2,1,0:T(8,128)S(1)}, u32[]{:S(2)}, u32[]{:S(2)}) %collective-permute-start.46) | collective-permute-done | bytes 24608 | tf_op jit(solution)/shard_map/ppermute | solution.py:480
  236.1 3.2 %collective-permute-done.51.refs_1_ = f32[3,8,128]{2,1,0:T(8,128)S(1)} collective-permute-done((f32[3,8,128]{2,1,0:T(8,128)S(1)}, f32[3,8,128]{2,1,0:T(8,128)S(1)}, u32[]{:S(2)}, u32[]{:S(2)}) %collective-permute-start.51) | collective-permute-done | bytes 12320 | tf_op jit(solution)/shard_map/ppermute | solution.py:480
  245.1 4.1 %collective-permute-done.56.refs_1_ = f32[8,48]{1,0:T(8,128)S(1)} collective-permute-done((f32[8,48]{1,0:T(8,128)S(1)}, f32[8,48]{1,0:T(8,128)S(1)}, u32[]{:S(2)}, u32[]{:S(2)}) %collective-permute-start.56) | collective-permute-done | bytes 1568 | tf_op jit(solution)/shard_map/ppermute | solution.py:480
  253.5 4.1 %collective-permute-done.61.refs_1_ = f32[8,48]{1,0:T(8,128)S(1)} collective-permute-done((f32[8,48]{1,0:T(8,128)S(1)}, f32[8,48]{1,0:T(8,128)S(1)}, u32[]{:S(2)}, u32[]{:S(2)}) %collective-permute-start.61) | collective-permute-done | bytes 1568 | tf_op jit(solution)/shard_map/ppermute | solution.py:480
  261.9 4.1 %collective-permute-done.66.refs_1_ = f32[8,48]{1,0:T(8,128)S(1)} collective-permute-done((f32[8,48]{1,0:T(8,128)S(1)}, f32[8,48]{1,0:T(8,128)S(1)}, u32[]{:S(2)}, u32[]{:S(2)}) %collective-permute-start.66) | collective-permute-done | bytes 1568 | tf_op jit(solution)/shard_map/ppermute | solution.py:480
  270.4 4.1 %collective-permute-done.71.refs_1_ = f32[8,48]{1,0:T(8,128)S(1)} collective-permute-done((f32[8,48]{1,0:T(8,128)S(1)}, f32[8,48]{1,0:T(8,128)S(1)}, u32[]{:S(2)}, u32[]{:S(2)}) %collective-permute-start.71) | collective-permute-done | bytes 1568 | tf_op jit(solution)/shard_map/ppermute | solution.py:480
  279.3 4.1 %collective-permute-done.76.refs_1_ = f32[3,8,128]{2,1,0:T(8,128)S(1)} collective-permute-done((f32[3,8,128]{2,1,0:T(8,128)S(1)}, f32[3,8,128]{2,1,0:T(8,128)S(1)}, u32[]{:S(2)}, u32[]{:S(2)}) %collective-permute-start.76) | collective-permute-done | bytes 12320 | tf_op jit(solution)/shard_map/ppermute | solution.py:480
  289.8 4.1 %collective-permute-done.81.refs_3_ = f32[6,8,128]{2,1,0:T(8,128)S(1)} collective-permute-done((f32[6,8,128]{2,1,0:T(8,128)S(1)}, f32[6,8,128]{2,1,0:T(8,128)S(1)}, u32[]{:S(2)}, u32[]{:S(2)}) %collective-permute-start.81) | collective-permute-done | bytes 24608 | tf_op jit(solution)/shard_map/ppermute | solution.py:480
  (231 shorter events, 116.9 us)
Async XLA Ops:
  115.8 12.6 %collective-permute-start.4 = (f32[12,8,128]{2,1,0:T(8,128)S(1)}, f32[12,8,128]{2,1,0:T(8,128)S(1)}, u32[]{:S(2)}, u32[]{:S(2)}) collective-permute-start(f32[12,8,128]{2,1,0:T(8,128)S(1)} %get-tuple-element.44), channel_id=1, source_target_pairs={{1,0},{0,1},{3,2},{2,3},{5,4},{4,5},{7,6},{6,7},{9,8},{8,9},{11,10... | collective-permute-start | bytes 147464 | tf_op jit(solution)/shard_map/ppermute | solution.py:480
  118.8 6.2 %collective-permute-start = (f32[6,8,128]{2,1,0:T(8,128)S(1)}, f32[6,8,128]{2,1,0:T(8,128)S(1)}, u32[]{:S(2)}, u32[]{:S(2)}) collective-permute-start(f32[6,8,128]{2,1,0:T(8,128)S(1)} %get-tuple-element.40.refs_0_.old_ref), channel_id=1, source_target_pairs={{2,0},{4,2},{6,4},{0,6},{3,1},{5,3},{7,5},{1,7},{10,8},{12,10},{14... | collective-permute-start | bytes 73736 | tf_op jit(solution)/shard_map/ppermute | solution.py:480
  122.4 6.0 %collective-permute-start.2 = (f32[6,8,128]{2,1,0:T(8,128)S(1)}, f32[6,8,128]{2,1,0:T(8,128)S(1)}, u32[]{:S(2)}, u32[]{:S(2)}) collective-permute-start(f32[6,8,128]{2,1,0:T(8,128)S(1)} %get-tuple-element.40.refs_0_.old_ref), channel_id=1, source_target_pairs={{8,0},{16,8},{24,16},{0,24},{9,1},{17,9},{25,17},{1,25},{10,2},{18... | collective-permute-start | bytes 73736 | tf_op jit(solution)/shard_map/ppermute | solution.py:480
  122.8 5.6 %collective-permute-start.3 = (f32[6,8,128]{2,1,0:T(8,128)S(1)}, f32[6,8,128]{2,1,0:T(8,128)S(1)}, u32[]{:S(2)}, u32[]{:S(2)}) collective-permute-start(f32[6,8,128]{2,1,0:T(8,128)S(1)} %get-tuple-element.43), channel_id=1, source_target_pairs={{24,0},{0,8},{8,16},{16,24},{25,1},{1,9},{9,17},{17,25},{26,2},{2,... | collective-permute-start | bytes 73736 | tf_op jit(solution)/shard_map/ppermute | solution.py:480
  129.9 21.6 %collective-permute-start.5 = (f32[3,8,128]{2,1,0:T(8,128)}, f32[3,8,128]{2,1,0:T(8,128)}, u32[]{:S(2)}, u32[]{:S(2)}) collective-permute-start(f32[3,8,128]{2,1,0:T(8,128)} %get-tuple-element.46.sol_ref.y2_ref), channel_id=1, source_target_pairs={{2,0},{4,2},{6,4},{0,6},{3,1},{5,3},{7,5},{1,7},{10,8},{12,10},{14... | collective-permute-start | bytes 36872 | tf_op jit(solution)/shard_map/ppermute | solution.py:480
  131.4 20.2 %collective-permute-start.6 = (f32[3,8,128]{2,1,0:T(8,128)}, f32[3,8,128]{2,1,0:T(8,128)}, u32[]{:S(2)}, u32[]{:S(2)}) collective-permute-start(f32[3,8,128]{2,1,0:T(8,128)} %get-tuple-element.46.sol_ref.y2_ref), channel_id=1, source_target_pairs={{6,0},{0,2},{2,4},{4,6},{7,1},{1,3},{3,5},{5,7},{14,8},{8,10},{10,... | collective-permute-start | bytes 36872 | tf_op jit(solution)/shard_map/ppermute | solution.py:480
  132.0 19.6 %collective-permute-start.7 = (f32[3,8,128]{2,1,0:T(8,128)}, f32[3,8,128]{2,1,0:T(8,128)}, u32[]{:S(2)}, u32[]{:S(2)}) collective-permute-start(f32[3,8,128]{2,1,0:T(8,128)} %get-tuple-element.46.sol_ref.y2_ref), channel_id=1, source_target_pairs={{8,0},{16,8},{24,16},{0,24},{9,1},{17,9},{25,17},{1,25},{10,2},{18... | collective-permute-start | bytes 36872 | tf_op jit(solution)/shard_map/ppermute | solution.py:480
  132.0 19.6 %collective-permute-start.8 = (f32[3,8,128]{2,1,0:T(8,128)}, f32[3,8,128]{2,1,0:T(8,128)}, u32[]{:S(2)}, u32[]{:S(2)}) collective-permute-start(f32[3,8,128]{2,1,0:T(8,128)} %get-tuple-element.46.sol_ref.y2_ref), channel_id=1, source_target_pairs={{24,0},{0,8},{8,16},{16,24},{25,1},{1,9},{9,17},{17,25},{26,2},{2,... | collective-permute-start | bytes 36872 | tf_op jit(solution)/shard_map/ppermute | solution.py:480
  132.5 19.1 %collective-permute-start.9 = (f32[3,8,128]{2,1,0:T(8,128)}, f32[3,8,128]{2,1,0:T(8,128)}, u32[]{:S(2)}, u32[]{:S(2)}) collective-permute-start(f32[3,8,128]{2,1,0:T(8,128)} %get-tuple-element.46.sol_ref.y2_ref), channel_id=1, source_target_pairs={{1,0},{0,1},{3,2},{2,3},{5,4},{4,5},{7,6},{6,7},{9,8},{8,9},{11,10... | collective-permute-start | bytes 36872 | tf_op jit(solution)/shard_map/ppermute | solution.py:480
  203.7 9.7 %collective-permute-start.39 = (f32[12,8,128]{2,1,0:T(8,128)S(1)}, f32[12,8,128]{2,1,0:T(8,128)S(1)}, u32[]{:S(2)}, u32[]{:S(2)}) collective-permute-start(f32[12,8,128]{2,1,0:T(8,128)S(1)} %get-tuple-element.53), channel_id=1, source_target_pairs={{1,0},{0,1},{3,2},{2,3},{5,4},{4,5},{7,6},{6,7},{9,8},{8,9},{11,10... | collective-permute-start | bytes 147464 | tf_op jit(solution)/shard_map/ppermute | solution.py:480
  207.8 5.6 %collective-permute-start.37 = (f32[6,8,128]{2,1,0:T(8,128)S(1)}, f32[6,8,128]{2,1,0:T(8,128)S(1)}, u32[]{:S(2)}, u32[]{:S(2)}) collective-permute-start(f32[6,8,128]{2,1,0:T(8,128)S(1)} %get-tuple-element.49.refs_0_), channel_id=1, source_target_pairs={{8,0},{16,8},{24,16},{0,24},{9,1},{17,9},{25,17},{1,25},{10,2},{18... | collective-permute-start | bytes 73736 | tf_op jit(solution)/shard_map/ppermute | solution.py:480
  207.8 5.6 %collective-permute-start.36 = (f32[6,8,128]{2,1,0:T(8,128)S(1)}, f32[6,8,128]{2,1,0:T(8,128)S(1)}, u32[]{:S(2)}, u32[]{:S(2)}) collective-permute-start(f32[6,8,128]{2,1,0:T(8,128)S(1)} %get-tuple-element.51), channel_id=1, source_target_pairs={{6,0},{0,2},{2,4},{4,6},{7,1},{1,3},{3,5},{5,7},{14,8},{8,10},{10,... | collective-permute-start | bytes 73736 | tf_op jit(solution)/shard_map/ppermute | solution.py:480
  207.8 5.6 %collective-permute-start.38 = (f32[6,8,128]{2,1,0:T(8,128)S(1)}, f32[6,8,128]{2,1,0:T(8,128)S(1)}, u32[]{:S(2)}, u32[]{:S(2)}) collective-permute-start(f32[6,8,128]{2,1,0:T(8,128)S(1)} %get-tuple-element.52), channel_id=1, source_target_pairs={{24,0},{0,8},{8,16},{16,24},{25,1},{1,9},{9,17},{17,25},{26,2},{2,... | collective-permute-start | bytes 73736 | tf_op jit(solution)/shard_map/ppermute | solution.py:480
  214.3 7.7 %collective-permute-start.44 = (f32[12,8,128]{2,1,0:T(8,128)S(1)}, f32[12,8,128]{2,1,0:T(8,128)S(1)}, u32[]{:S(2)}, u32[]{:S(2)}) collective-permute-start(f32[12,8,128]{2,1,0:T(8,128)S(1)} %get-tuple-element.58), channel_id=1, source_target_pairs={{1,0},{0,1},{3,2},{2,3},{5,4},{4,5},{7,6},{6,7},{9,8},{8,9},{11,10... | collective-permute-start | bytes 147464 | tf_op jit(solution)/shard_map/ppermute | solution.py:480
  216.3 5.6 %collective-permute-start.42 = (f32[6,8,128]{2,1,0:T(8,128)S(1)}, f32[6,8,128]{2,1,0:T(8,128)S(1)}, u32[]{:S(2)}, u32[]{:S(2)}) collective-permute-start(f32[6,8,128]{2,1,0:T(8,128)S(1)} %get-tuple-element.54.refs_0_), channel_id=1, source_target_pairs={{8,0},{16,8},{24,16},{0,24},{9,1},{17,9},{25,17},{1,25},{10,2},{18... | collective-permute-start | bytes 73736 | tf_op jit(solution)/shard_map/ppermute | solution.py:480
  216.3 5.6 %collective-permute-start.41 = (f32[6,8,128]{2,1,0:T(8,128)S(1)}, f32[6,8,128]{2,1,0:T(8,128)S(1)}, u32[]{:S(2)}, u32[]{:S(2)}) collective-permute-start(f32[6,8,128]{2,1,0:T(8,128)S(1)} %get-tuple-element.56), channel_id=1, source_target_pairs={{6,0},{0,2},{2,4},{4,6},{7,1},{1,3},{3,5},{5,7},{14,8},{8,10},{10,... | collective-permute-start | bytes 73736 | tf_op jit(solution)/shard_map/ppermute | solution.py:480
  222.8 8.6 %collective-permute-start.49 = (f32[12,8,128]{2,1,0:T(8,128)S(1)}, f32[12,8,128]{2,1,0:T(8,128)S(1)}, u32[]{:S(2)}, u32[]{:S(2)}) collective-permute-start(f32[12,8,128]{2,1,0:T(8,128)S(1)} %get-tuple-element.63), channel_id=1, source_target_pairs={{1,0},{0,1},{3,2},{2,3},{5,4},{4,5},{7,6},{6,7},{9,8},{8,9},{11,10... | collective-permute-start | bytes 147464 | tf_op jit(solution)/shard_map/ppermute | solution.py:480
  225.8 5.6 %collective-permute-start.47 = (f32[6,8,128]{2,1,0:T(8,128)S(1)}, f32[6,8,128]{2,1,0:T(8,128)S(1)}, u32[]{:S(2)}, u32[]{:S(2)}) collective-permute-start(f32[6,8,128]{2,1,0:T(8,128)S(1)} %get-tuple-element.59.refs_0_.old_ref), channel_id=1, source_target_pairs={{8,0},{16,8},{24,16},{0,24},{9,1},{17,9},{25,17},{1,25},{10,2},{18... | collective-permute-start | bytes 73736 | tf_op jit(solution)/shard_map/ppermute | solution.py:480
  285.2 8.8 %collective-permute-start.84 = (f32[12,8,128]{2,1,0:T(8,128)S(1)}, f32[12,8,128]{2,1,0:T(8,128)S(1)}, u32[]{:S(2)}, u32[]{:S(2)}) collective-permute-start(f32[12,8,128]{2,1,0:T(8,128)S(1)} %get-tuple-element.72), channel_id=1, source_target_pairs={{1,0},{0,1},{3,2},{2,3},{5,4},{4,5},{7,6},{6,7},{9,8},{8,9},{11,10... | collective-permute-start | bytes 147464 | tf_op jit(solution)/shard_map/ppermute | solution.py:480
  288.3 5.6 %collective-permute-start.82 = (f32[6,8,128]{2,1,0:T(8,128)S(1)}, f32[6,8,128]{2,1,0:T(8,128)S(1)}, u32[]{:S(2)}, u32[]{:S(2)}) collective-permute-start(f32[6,8,128]{2,1,0:T(8,128)S(1)} %get-tuple-element.68.refs_0_), channel_id=1, source_target_pairs={{8,0},{16,8},{24,16},{0,24},{9,1},{17,9},{25,17},{1,25},{10,2},{18... | collective-permute-start | bytes 73736 | tf_op jit(solution)/shard_map/ppermute | solution.py:480
  288.3 5.6 %collective-permute-start.83 = (f32[6,8,128]{2,1,0:T(8,128)S(1)}, f32[6,8,128]{2,1,0:T(8,128)S(1)}, u32[]{:S(2)}, u32[]{:S(2)}) collective-permute-start(f32[6,8,128]{2,1,0:T(8,128)S(1)} %get-tuple-element.71), channel_id=1, source_target_pairs={{24,0},{0,8},{8,16},{16,24},{25,1},{1,9},{9,17},{17,25},{26,2},{2,... | collective-permute-start | bytes 73736 | tf_op jit(solution)/shard_map/ppermute | solution.py:480
  294.8 8.6 %collective-permute-start.89 = (f32[12,8,128]{2,1,0:T(8,128)S(1)}, f32[12,8,128]{2,1,0:T(8,128)S(1)}, u32[]{:S(2)}, u32[]{:S(2)}) collective-permute-start(f32[12,8,128]{2,1,0:T(8,128)S(1)} %get-tuple-element.77), channel_id=1, source_target_pairs={{1,0},{0,1},{3,2},{2,3},{5,4},{4,5},{7,6},{6,7},{9,8},{8,9},{11,10... | collective-permute-start | bytes 147464 | tf_op jit(solution)/shard_map/ppermute | solution.py:480
  296.4 6.5 %collective-permute-start.85 = (f32[6,8,128]{2,1,0:T(8,128)S(1)}, f32[6,8,128]{2,1,0:T(8,128)S(1)}, u32[]{:S(2)}, u32[]{:S(2)}) collective-permute-start(f32[6,8,128]{2,1,0:T(8,128)S(1)} %get-tuple-element.73.refs_0_), channel_id=1, source_target_pairs={{2,0},{4,2},{6,4},{0,6},{3,1},{5,3},{7,5},{1,7},{10,8},{12,10},{14... | collective-permute-start | bytes 73736 | tf_op jit(solution)/shard_map/ppermute | solution.py:480
  297.8 5.6 %collective-permute-start.87 = (f32[6,8,128]{2,1,0:T(8,128)S(1)}, f32[6,8,128]{2,1,0:T(8,128)S(1)}, u32[]{:S(2)}, u32[]{:S(2)}) collective-permute-start(f32[6,8,128]{2,1,0:T(8,128)S(1)} %get-tuple-element.73.refs_0_), channel_id=1, source_target_pairs={{8,0},{16,8},{24,16},{0,24},{9,1},{17,9},{25,17},{1,25},{10,2},{18... | collective-permute-start | bytes 73736 | tf_op jit(solution)/shard_map/ppermute | solution.py:480
  (79 other events, 486.1 us)
where the time goes:
time: 310 us; the launch traced here: 309 us
  local copies, waits for them, and re-layouts  148 us (48%)
  starting transfers between devices  73.7 us (24%)
  waiting for transfers between devices  66.5 us (21%)
  Pallas kernels  19.3 us (6%)
    convert_element_type x3, local copies, waits for them, and re-layouts, link_tiles(): folded.transpose(7, 0, 1, 3, 5, 2, 4, 6, 9, 8).reshape(4, 36, 8, 128)  110 us
    ppermute x90, starting transfers between devices, from_behind(): lax.ppermute(block, axis, [((i - distance) % n, i) for i in range(n)])  73.7 us
    ppermute x90, waiting for transfers between devices, from_behind(): lax.ppermute(block, axis, [((i - distance) % n, i) for i in range(n)])  66.5 us
    pallas_call x19, Pallas kernels, call(): pl.pallas_call(kernel, out_shape=[jax.ShapeDtypeStruct(s, F32) for s in o...  19.3 us
    unnamed x30, local copies, waits for them, and re-layouts  11.3 us
    reshape x2, local copies, waits for them, and re-layouts, local(): near_mid.reshape(48, 48, 8, 2, 4).transpose(0, 2, 1, 4, 3).reshape(384, 384)  8.31 us
  transfers between devices with their start and end apart: 90, of which 27 were waited for; matrix products, arithmetic and copies ran while one was open for 8% of the time, Pallas kernels for 0%

commit v1 on v0

--- a/solution.py
+++ b/solution.py
@@ -127,25 +127,25 @@
     return [x - y for x, y in zip(xs, ys)]
 
 
-def fine_send(site, links_ref, field, acc_ref, sent_refs):
+def fine_send(site, links_ref, field, acc_ref):
     acc = list(field)
     for kind, reach in ((0, 1), (1, 3)):
         acc = add(acc, link_apply(links_ref, 3, kind, [shift_y(site, x, reach) for x in field]))
         back = link_adjoint(links_ref, 3, kind, field)
         acc = sub(acc, [shift_y(site, x, -reach) for x in back])
+    sent = []
     for direction in range(3):
         near = [cyclic(site, x, direction, -1) for x in link_adjoint(links_ref, direction, 0, field)]
         far = link_adjoint(links_ref, direction, 1, field)
         first, last = site.first(direction), site.last(direction)
-        ref, base = sent_refs[direction]
-        for i in range(6):
-            ref[base + i] = jnp.where(first, near[i], far[i])
+        sent.append([jnp.where(first, n, f) for n, f in zip(near, far)])
         acc = [
             a - jnp.where(first, 0.0, n) - jnp.where(last, cyclic(site, f, direction, 1), 0.0)
             for a, n, f in zip(acc, near, far)
         ]
     for i in range(6):
         acc_ref[i] = acc[i]
+    return sent
 
 
 def fine_receive(site, links_ref, field, acc, ahead, behind):
@@ -295,44 +295,109 @@
 
 def pick_y(part):
     row, lane = iota2((8, 128), 0), iota2((8, 128), 1)
-    return (row == part * 4 + ((lane & 7) >> 1)).astype(F32)
+    return (row == part * 4 + (lane & 3)).astype(F32)
+
+
+def permute_eight(site, x, source):
+    out = x
+    for move in sorted({s - i for i, s in enumerate(source)} - {0}):
+        hit = None
+        for i, s in enumerate(source):
+            if s - i == move:
+                hit = (site.by == i) if hit is None else hit | (site.by == i)
+        out = jnp.where(hit, left(x, move), out)
+    return out
+
+
+SPLIT_Y = (0, 2, 4, 6, 1, 3, 5, 7)
+JOIN_Y = (0, 4, 1, 5, 2, 6, 3, 7)
+
+
+def total_rows(x):
+    for d in (4, 2, 1):
+        x = x + up(x, d)
+    return x
+
+
+def widen(site, v):
+    own = ((site.lane >> 3) & 7) == site.row
+    half = site.lane_bit(64) == site.lane_bit(8)
+    found = []
+
+    def down(x, d):
+        if d == 8:
+            x = jnp.where(half, x, flip_lane(site, x, 8))
+            found.append(total_rows(jnp.where(own, x, 0.0)))
+            return
+        bit = site.lane_bit(d)
+        r = left(x, d)
+        down(jnp.where(bit, r, x), d // 2)
+        down(jnp.where(bit, x, r), d // 2)
+
+    for x in v:
+        down(permute_eight(site, x, SPLIT_Y), 64)
+    return found
+
+
+def narrow(site, tiles):
+    own = ((site.lane >> 3) & 7) == site.row
+    same = site.lane_bit(64) == site.lane_bit(8)
+
+    def fold(d, a, b):
+        bit = site.lane_bit(d)
+        return jnp.where(bit, b, a) + flip_lane(site, jnp.where(bit, a, b), d)
+
+    out = []
+    for q in range(0, 24, 8):
+        t = [jnp.where(own, total_rows(x), 0.0) for x in tiles[q : q + 8]]
+        t = [fold(8, t[i], t[i + 4]) for i in range(4)]
+        t = [fold(32, t[i], t[i + 2]) for i in range(2)]
+        x = fold(16, t[0], t[1])
+        x = jnp.where(same, x, jnp.where(site.lane_bit(64), left(x, -56), left(x, 56)))
+        out.append(permute_eight(site, x, JOIN_Y))
+    return out
 
 
 def restrict_mid(site, near_ref, v, tile_ref):
-    x_re, x_im = mid_x_conj(site, v)
-    for o in range(0, 48, 2):
-        block = two_rows(near_ref, o)
+    x = widen(site, v)
+    x_im = x[12:] + [-t for t in x[:12]]
+    for o in range(0, 48, 16):
+        re = [None, None]
+        im = [None, None]
+        for j in range(24):
+            n = near_ref[pl.ds(o, 16), pl.ds(128 * j, 128)].astype(F32)
+            for h in range(2):
+                block = n[8 * h : 8 * h + 8]
+                a, b = block * x[j], block * x_im[j]
+                re[h] = a if re[h] is None else re[h] + a
+                im[h] = b if im[h] is None else im[h] + b
         for h in range(2):
-            tile_ref[0, pl.ds(8 * (o + h), 8), :] = dot_tiles(block, 8 * h, x_re)
-            tile_ref[1, pl.ds(8 * (o + h), 8), :] = dot_tiles(block, 8 * h, x_im)
+            tile_ref[0, pl.ds(o + 8 * h, 8), :] = re[h]
+            tile_ref[1, pl.ds(o + 8 * h, 8), :] = im[h]
     dims = (((1,), (1,)), ((), ()))
     z = None
     for p in range(2):
         t = lax.dot_general(pick_y(p), tile_ref[p], dims, precision=HIGHEST, preferred_element_type=F32)
         z = t if z is None else z + t
-    select = ((iota2((384, 48), 0) >> 3) == iota2((384, 48), 1)).astype(F32)
-    return jnp.dot(z, select, precision=HIGHEST, preferred_element_type=F32)
+    return z
 
 
 def prolong_mid(site, near_ref, y3, row_ref):
     dims = (((0,), (0,)), ((), ()))
     for p in range(2):
         row_ref[p] = lax.dot_general(y3, pick_y(p), dims, precision=HIGHEST, preferred_element_type=F32)
-    a, b = [0.0] * 3, [0.0] * 3
-    for o in range(0, 48, 2):
-        block = two_rows(near_ref, o)
-        for h in range(2):
-            y_re = jnp.broadcast_to(row_ref[0, pl.ds(o + h, 1), :], (8, 128))
-            y_im = jnp.broadcast_to(row_ref[1, pl.ds(o + h, 1), :], (8, 128))
-            for j in range(3):
-                n = block[8 * h : 8 * h + 8, 128 * j : 128 * j + 128]
-                a[j] = a[j] + n * y_re
-                b[j] = b[j] + n * y_im
-    return add(a, swap_parts(site, [-x for x in im_negated_keep(site, b)]))
-
-
-def im_negated_keep(site, v):
-    return [-v[0], jnp.where(site.lane_bit(64), v[1], -v[1]), v[2]]
+    a, b = [None] * 24, [None] * 24
+    for j in range(24):
+        for o in range(0, 48, 16):
+            n = near_ref[pl.ds(o, 16), pl.ds(128 * j, 128)].astype(F32)
+            for h in range(2):
+                block = n[8 * h : 8 * h + 8]
+                s = block * row_ref[0, pl.ds(o + 8 * h, 8), :]
+                t = block * row_ref[1, pl.ds(o + 8 * h, 8), :]
+                a[j] = s if a[j] is None else a[j] + s
+                b[j] = t if b[j] is None else b[j] + t
+    tiles = [a[j] - b[12 + j] for j in range(12)] + [a[12 + j] + b[j] for j in range(12)]
+    return narrow(site, tiles)
 
 
 def coarse_rows(v):
@@ -375,24 +440,119 @@
         ref[base + i] = x
 
 
-def finish_fine(site, links_ref, solution, sol_ref, acc_ref, pt_ref, pz_ref, mx_ref):
+def is_odd(axis):
+    return lax.rem(lax.axis_index(axis), 2) == 1
+
+
+def finish_fine(site, links_ref, solution, sol_ref, acc_ref, z0_ref, z1_ref, t0_ref, t1_ref, x_ref):
     store(sol_ref, solution)
-    store(mx_ref, solution)
-    fine_send(site, links_ref, solution, acc_ref, ((pt_ref, 0), (pz_ref, 0), (mx_ref, 6)))
+    store(x_ref, solution)
+    back_t, back_z, back_x = fine_send(site, links_ref, solution, acc_ref)
+    store(x_ref, back_x, 6)
+    for axis, back, ref0, ref1 in (("gz", back_z, z0_ref, z1_ref), ("ta", back_t, t0_ref, t1_ref)):
+        odd = is_odd(axis)
+        store(ref0, [jnp.where(odd, s, b) for s, b in zip(solution, back)])
+        store(ref1, [jnp.where(odd, b, s) for s, b in zip(solution, back)])
+
+
+def by_parity(axis, zero, one):
+    odd = is_odd(axis)
+    ahead = [jnp.where(odd, b, a) for a, b in zip(zero, one)]
+    return ahead, [jnp.where(odd, a, b) for a, b in zip(zero, one)]
 
 
 def begin_fine(site, links_ref, refs):
-    sol_ref, acc_ref, nz, bz, nt, bt, mx = refs
+    sol_ref, acc_ref, z1, t1, x, z0, t0 = refs
     solution = load(sol_ref, 6)
-    ahead = [load(nt, 6), load(nz, 6), load(mx, 6)]
-    behind = [load(bt, 6), load(bz, 6), load(mx, 6, 6)]
+    ahead_t, behind_t = by_parity("ta", load(t0, 6), load(t1, 6))
+    ahead_z, behind_z = by_parity("gz", load(z0, 6), load(z1, 6))
+    ahead = [ahead_t, ahead_z, load(x, 6)]
+    behind = [behind_t, behind_z, load(x, 6, 6)]
     return solution, fine_receive(site, links_ref, solution, load(acc_ref, 6), ahead, behind)
 
 
-def kernel_first(links_ref, block_ref, rhs_ref, *outs):
+def row_order(transposed):
+    m, n = iota2((64, 64), 0), iota2((64, 64), 1)
+    if transposed:
+        m, n = n, m
+    bit = lambda v, k: (v >> k) & 1
+    fine = (
+        (bit(m, 2) << 5) | (bit(m, 5) << 4) | (bit(m, 1) << 3) | (bit(m, 4) << 2) | (bit(m, 0) << 1) | bit(m, 3)
+    )
+    return n == fine
+
+
+def y_order(rows, columns, transposed):
+    m, n = iota2((rows, columns), 0), iota2((rows, columns), 1)
+    if transposed:
+        m, n = n, m
+    fine = (((n & 7) << 1) | ((n >> 3) & 1)) | (n & 112)
+    return m == (fine & (min(rows, columns) - 1))
+
+
+def exact_dot(a, b):
+    return jnp.dot(a, b, precision=HIGHEST, preferred_element_type=F32)
+
+
+def prepare_links(site, links_ref, g_ref):
+    rows = row_order(False).astype(BF16)
+    lanes = y_order(128, 128, False).astype(BF16)
+    signs = [jnp.full((8, 128), 0.5, F32)]
+    for d in LANE_BITS:
+        signs.append(jnp.where(site.lane_bit(d), -signs[-1], signs[-1]))
+    for rc in range(9):
+        block = links_ref[pl.ds(64 * rc, 64), :]
+        block = jnp.dot(rows, block, preferred_element_type=F32).astype(BF16)
+        for h in range(2):
+            half = jnp.dot(block[:, 128 * h : 128 * h + 128], lanes, preferred_element_type=F32)
+            v = [half[8 * w : 8 * w + 8] for w in range(8)]
+            for d, k in zip(LANE_BITS, (4, 2, 1)):
+                bit = site.lane_bit(d)
+                for w in range(8):
+                    if not w & k:
+                        lo, hi = v[w], v[w | k]
+                        v[w] = jnp.where(bit, left(hi, -d), lo)
+                        v[w | k] = jnp.where(bit, hi, left(lo, d))
+            for m in range(8):
+                g_ref[(8 * h + m) * 9 + rc] = v[m] * signs[2 * h + m // 4]
+
+
+def gather_fine(site, field_ref):
+    rows = row_order(False).astype(F32)
+    lanes = y_order(16, 128, False).astype(F32)
+    group = site.lane >> 4
+    out = []
+    for p in range(2):
+        for c in range(3):
+            parts = [field_ref[p, c, t, z] for t in range(4) for z in range(4)]
+            spread_out = exact_dot(rows, exact_dot(jnp.concatenate(parts, axis=0), lanes))
+            total = spread_out[:8]
+            for w in range(1, 8):
+                total = jnp.where(group == w, spread_out[8 * w : 8 * w + 8], total)
+            out.append(total)
+    return out
+
+
+def scatter_fine(site, field, out_ref):
+    rows = row_order(True).astype(F32)
+    lanes = y_order(128, 16, True).astype(F32)
+    group = site.lane >> 4
+    for p in range(2):
+        for c in range(3):
+            x = field[3 * p + c]
+            tall = jnp.concatenate([jnp.where(group == w, x, 0.0) for w in range(8)], axis=0)
+            value = exact_dot(rows, exact_dot(tall, lanes))
+            for t in range(4):
+                for z in range(4):
+                    out_ref[p, c, t, z] = value[16 * t + 4 * z : 16 * t + 4 * z + 4]
+
+
+def kernel_first(links_ref, block_ref, source_ref, g_ref, rhs_ref, *outs):
     site = Site()
-    solution = fine_matrix(site, block_ref, load(rhs_ref, 6))
-    finish_fine(site, links_ref, solution, *outs)
+    rhs = gather_fine(site, source_ref)
+    store(rhs_ref, rhs)
+    prepare_links(site, links_ref, g_ref)
+    finish_fine(site, g_ref, fine_matrix(site, block_ref, rhs), *outs)
 
 
 def kernel_smooth(links_ref, block_ref, rhs_ref, *refs):
@@ -405,8 +565,9 @@
 
 def kernel_last(links_ref, rhs_ref, *refs):
     site = Site()
-    _, applied = begin_fine(site, links_ref, refs[:7])
-    store(refs[7], sub(load(rhs_ref, 6), applied))
+    solution, applied = begin_fine(site, links_ref, refs[:7])
+    scatter_fine(site, solution, refs[7])
+    scatter_fine(site, sub(load(rhs_ref, 6), applied), refs[8])
 
 
 def kernel_restrict(links_ref, near_ref, jacobi_ref, rhs_ref, *refs):
@@ -419,11 +580,10 @@
 
 
 def neighbours(refs, get):
-    nz, bz, nt, bt = refs[:4]
-    nx = refs[4]
-    bx = refs[-1]
-    ahead = [get(nt), get(nz), get(nx)]
-    return ahead, [get(bt), get(bz), get(bx)]
+    z1, t1, nx, z0, t0 = refs[:5]
+    ahead_t, behind_t = by_parity("ta", get(t0), get(t1))
+    ahead_z, behind_z = by_parity("gz", get(z0), get(z1))
+    return [ahead_t, ahead_z, get(nx)], [behind_t, behind_z, get(refs[-1] if len(refs) > 5 else nx)]
 
 
 def kernel_mid_down(stencil_ref, near_ref, jacobi_ref, res_ref, sol_ref, *refs):
@@ -437,7 +597,8 @@
 
 
 def sweep(stencil_ref, jacobi_ref, r3_ref, y3_ref, around):
-    ahead, behind = neighbours(around, lambda r: r[...])
+    ahead, behind = neighbours(around, lambda r: [r[...]])
+    ahead, behind = [x[0] for x in ahead], [x[0] for x in behind]
     y3 = y3_ref[...]
     rest = r3_ref[...] - coarse_stencil_apply(stencil_ref, y3, ahead, behind)
     return y3 + coarse_matrix([(jacobi_ref, 0, rest)])
@@ -456,7 +617,7 @@
 
 def kernel_mid_up(links_ref, stencil_ref, jacobi_ref, near_ref, old_ref, res_ref, y2_ref, *refs):
     site = Site()
-    around, outs, spread_ref = refs[:-6], refs[-6:-1], refs[-1]
+    around, outs, spread_ref = refs[:-8], refs[-8:-1], refs[-1]
     ahead, behind = neighbours(around, lambda r: load(r, 3))
     y2 = load(y2_ref, 3)
     rest = sub(load(res_ref, 3), mid_stencil_apply(site, stencil_ref, y2, ahead, behind))
@@ -480,56 +641,32 @@
     return lax.ppermute(block, axis, [((i - distance) % n, i) for i in range(n)])
 
 
+def swap(block, axis, phase):
+    n = lax.axis_size(axis)
+    return lax.ppermute(block, axis, [(i, (((i + phase) ^ 1) - phase) % n) for i in range(n)])
+
+
 def exchange(v):
-    around = [
-        from_behind(v, "gz", -1),
-        from_behind(v, "gz", 1),
-        from_behind(v, "ta", -1),
-        from_behind(v, "ta", 1),
-        from_behind(v, "xy", -1),
-    ]
-    if lax.axis_size("xy") > 2:
-        around.append(from_behind(v, "xy", 1))
-    return around
-
-
-def exchange_fine(sol, acc, pt, pz, mx):
+    z1 = swap(v, "gz", 1)
+    t1 = swap(v, "ta", 1)
+    x = from_behind(v, "xy", -1)
+    z0 = swap(v, "gz", 0)
+    t0 = swap(v, "ta", 0)
+    return [z1, t1, x, z0, t0] + ([from_behind(v, "xy", 1)] if lax.axis_size("xy") > 2 else [])
+
+
+def exchange_fine(sol, acc, z0, z1, t0, t1, x):
+    z1 = swap(z1, "gz", 1)
+    t1 = swap(t1, "ta", 1)
     if lax.axis_size("xy") == 2:
-        moved = from_behind(mx, "xy", 1)
+        x = from_behind(x, "xy", 1)
     else:
-        moved = jnp.concatenate([from_behind(mx[:6], "xy", -1), from_behind(mx[6:], "xy", 1)])
-    return [
-        sol,
-        acc,
-        from_behind(sol, "gz", -1),
-        from_behind(pz, "gz", 1),
-        from_behind(sol, "ta", -1),
-        from_behind(pt, "ta", 1),
-        moved,
-    ]
+        x = jnp.concatenate([from_behind(x[:6], "xy", -1), from_behind(x[6:], "xy", 1)])
+    return [sol, acc, z1, t1, x, swap(z0, "gz", 0), swap(t0, "ta", 0)]
 
 
 TILE6 = (6, 8, 128)
-FINE_OUT = [TILE6, TILE6, TILE6, TILE6, (12, 8, 128)]
-
-
-def to_tiles(field):
-    folded = field.reshape(6, 2, 2, 2, 2, 2, 2, 8, 2)
-    return folded.transpose(0, 1, 3, 5, 2, 4, 6, 8, 7).reshape(TILE6)
-
-
-def from_tiles(tiles, shape):
-    folded = tiles.reshape(6, 2, 2, 2, 2, 2, 2, 2, 8)
-    return folded.transpose(0, 1, 4, 2, 5, 3, 6, 8, 7).reshape(shape)
-
-
-def link_tiles(links):
-    folded = links.reshape(9, 2, 2, 2, 2, 2, 2, 16, 8, 2)
-    tiles = folded.transpose(7, 0, 1, 3, 5, 2, 4, 6, 9, 8).reshape(4, 36, 8, 128).astype(F32)
-    lane = lax.iota(jnp.int32, 128)
-    ct, cz, cx = (lane >> 6) & 1, (lane >> 5) & 1, (lane >> 4) & 1
-    odd = jnp.stack([0 * ct, ct, ct ^ cz, ct ^ cz ^ cx]).astype(F32)
-    return (tiles * (0.5 - odd)[:, None, None, :]).reshape(144, 8, 128)
+FINE_OUT = [TILE6] * 6 + [(12, 8, 128)]
 
 
 def local(
@@ -543,23 +680,22 @@
     coarse_stencil,
     coarse_jacobi,
 ):
-    g = link_tiles(links)
-    rhs = to_tiles(right_side)
+    links_flat = links.reshape(576, 256)
     block = block_inverse.reshape(384, 768)
     near1 = near_fine.reshape(192, 768)
     stencil2 = mid_stencil.reshape(1728, 384)
     jacobi2 = mid_jacobi.reshape(192, 384)
-    near2 = near_mid.reshape(48, 48, 8, 2, 4).transpose(0, 2, 1, 4, 3).reshape(384, 384)
+    near2 = near_mid.reshape(near_mid.shape[0], near_mid.shape[4])
     stencil3 = jnp.swapaxes(coarse_stencil, 5, 6).reshape(864, 192)
     jacobi3 = jnp.swapaxes(coarse_jacobi, 4, 5).reshape(96, 192)
     mid = (3, 8, 128)
     coarse = (8, 48)
 
-    state = call(kernel_first, FINE_OUT, [], g, block, rhs)
+    g, rhs, *state = call(kernel_first, [(144, 8, 128), TILE6] + FINE_OUT, [], links_flat, block, right_side)
     for cycle_no in range(CYCLES):
         r2, y2 = call(kernel_restrict, [mid, mid], [], g, near1, jacobi2, rhs, *exchange_fine(*state))
         r3, y3 = call(
-            kernel_mid_down, [coarse, coarse], [(2, 384, 128)], stencil2, near2, jacobi3, r2, y2, *exchange(y2)
+            kernel_mid_down, [coarse, coarse], [(2, 48, 128)], stencil2, near2, jacobi3, r2, y2, *exchange(y2)
         )
         for _ in range(SWEEPS - 1):
             (y3,) = call(kernel_sweep, [coarse], [], stencil3, jacobi3, r3, y3, *exchange(y3))
@@ -572,8 +708,7 @@
         state = call(kernel_smooth, FINE_OUT, [], g, block, rhs, *exchange_fine(*state))
         if cycle_no < CYCLES - 1:
             state = call(kernel_smooth, FINE_OUT, [], g, block, rhs, *exchange_fine(*state))
-    (residual,) = call(kernel_last, [TILE6], [], g, rhs, *exchange_fine(*state))
-    return from_tiles(state[0], right_side.shape), from_tiles(residual, right_side.shape)
+    return call(kernel_last, [right_side.shape] * 2, [], g, rhs, *exchange_fine(*state))
 
 
 def solution(mesh):

time: 310 us -> 162 us (0.52)
  local copies, waits for them, and re-layouts: 148 us -> 6.7 us
  waiting for transfers between devices: 66.5 us -> 56.8 us
  Pallas kernels: 19.3 us -> 23 us
    convert_element_type x3 -> x0, local copies, waits for them, and re-layouts: 110 us -> none  [link_tiles(): folded.transpose(7, 0, 1, 3, 5, 2, 4, 6, 9, 8).reshape(4, 36, 8, 128)]
    ppermute x90 -> x18, waiting for transfers between devices: 66.5 us -> 0.63 us  [from_behind(): lax.ppermute(block, axis, [((i - distance) % n, i) for i in range(n)])]
    ppermute x0 -> x72, waiting for transfers between devices: none -> 56.2 us  [swap(): lax.ppermute(block, axis, [(i, ((i + phase ^ 1) - phase) % n) for i in ra...]
    ppermute x0 -> x72, starting transfers between devices: none -> 54 us  [swap(): lax.ppermute(block, axis, [(i, ((i + phase ^ 1) - phase) % n) for i in ra...]
    ppermute x90 -> x18, starting transfers between devices: 73.7 us -> 20.7 us  [from_behind(): lax.ppermute(block, axis, [((i - distance) % n, i) for i in range(n)])]
    reshape x10 -> x1, local copies, waits for them, and re-layouts: 14.7 us -> 1.08 us  [local(): links_flat = links.reshape(576, 256)]
    unnamed x30 -> x12, local copies, waits for them, and re-layouts: 11.3 us -> 0.03 us
    transpose x2 -> x0, local copies, waits for them, and re-layouts: 6.12 us -> none  [the longest x1 4.77 us: local(): near_mid.reshape(48, 48, 8, 2, 4).transpose(0, 2, 1, 4, 3).reshape(384, 384)]
  transfers between devices with their start and end apart: 90 -> 90, of which waited for: 27 -> 42; matrix products, arithmetic and copies ran while one was open for 8% -> 2% of each run, Pallas kernels for 0% -> 0%
where the time goes in v1:
time: 162 us
  starting transfers between devices  74.7 us (46%)
  waiting for transfers between devices  56.8 us (35%)
  Pallas kernels  23 us (14%)
  local copies, waits for them, and re-layouts  6.7 us (4%)
    ppermute x72, waiting for transfers between devices, swap(): lax.ppermute(block, axis, [(i, ((i + phase ^ 1) - phase) % n) for i in ra...  56.2 us
    ppermute x72, starting transfers between devices, swap(): lax.ppermute(block, axis, [(i, ((i + phase ^ 1) - phase) % n) for i in ra...  54 us
    pallas_call x19, Pallas kernels, call(): pl.pallas_call(kernel, out_shape=[jax.ShapeDtypeStruct(s, F32) for s in o...  23 us
    ppermute x18, starting transfers between devices, from_behind(): lax.ppermute(block, axis, [((i - distance) % n, i) for i in range(n)])  20.7 us
    reshape x1, local copies, waits for them, and re-layouts, local(): stencil2 = mid_stencil.reshape(1728, 384)  3.4 us
  transfers between devices with their start and end apart: 90, of which 42 were waited for; matrix products, arithmetic and copies ran while one was open for 2% of the time, Pallas kernels for 0%

profile of v1, /device:TPU:0, one launch (start us, length us, event | category | flops | bytes accessed | tf_op | source)
XLA Modules:
  0.0 162.2 jit_solution(11622882329148007423)
XLA Ops:
  1.7 2.0 %reshape.29.block_ref = bf16[384,768]{1,0:T(8,128)(2,1)S(1)} reshape(bf16[48,2,2,2,768]{4,3,2,1,0:T(2,128)(2,1)} %param.11) | data formatting | bytes 1179648 | tf_op jit(solution)/shard_map/reshape | solution.py:684
  3.8 2.1 %kernel_first.1 = (f32[144,8,128]{2,1,0:T(8,128)S(1)}, f32[6,8,128]{2,1,0:T(8,128)S(1)}, f32[6,8,128]{2,1,0:T(8,128)S(1)}, f32[6,8,128]{2,1,0:T(8,128)S(1)}, f32...) custom-call(bf16[576,256]{1,0:T(8,128)(2,1)S(1)} %reshape.28.links_r, ...), custom_call_target="tpu_custom_call" | custom-call | tf_op jit(solution)/shard_map/kernel_first/pallas_call | solution.py:630
  5.9 3.0 %collective-permute-start.2 = (f32[12,8,128]{2,1,0:T(8,128)S(1)}, f32[12,8,128]{2,1,0:T(8,128)S(1)}, u32[]{:S(2)}, u32[]{:S(2)}) collective-permute-start(f32[12,8,128]{2,1,0:T(8,128)S(1)} %get-tuple-element.60), channel_id=1, source_target_pairs={{1,0},{0,1},{3,2},{2,3},{5,4},{4,5},{7,6},{6,7},{9,8},{8,9},{11,10... | collective-permute-start | bytes 147464 | tf_op jit(solution)/shard_map/ppermute | solution.py:641
  8.9 3.6 %collective-permute-start = (f32[6,8,128]{2,1,0:T(8,128)S(1)}, f32[6,8,128]{2,1,0:T(8,128)S(1)}, u32[]{:S(2)}, u32[]{:S(2)}) collective-permute-start(f32[6,8,128]{2,1,0:T(8,128)S(1)} %get-tuple-element.58), channel_id=1, source_target_pairs={{0,6},{2,4},{4,2},{6,0},{1,7},{3,5},{5,3},{7,1},{8,14},{10,12},{12... | collective-permute-start | bytes 73736 | tf_op jit(solution)/shard_map/ppermute | solution.py:646
  21.2 3.4 %reshape.30.stencil_ref = bf16[1728,384]{1,0:T(8,128)(2,1)S(1)} reshape(bf16[9,24,2,2,2,384]{5,4,3,2,1,0:T(2,128)(2,1)} %param.13) | data formatting | bytes 2654208 | tf_op jit(solution)/shard_map/reshape | solution.py:686
  32.2 2.4 %collective-permute-done.10.refs_0_ = f32[8,48]{1,0:T(8,128)S(1)} collective-permute-done((f32[8,48]{1,0:T(8,128)S(1)}, f32[8,48]{1,0:T(8,128)S(1)}, u32[]{:S(2)}, u32[]{:S(2)}) %collective-permute-start.10) | collective-permute-done | bytes 1568 | tf_op jit(solution)/shard_map/ppermute | solution.py:646
  38.7 3.3 %collective-permute-done.15.refs_0_ = f32[8,48]{1,0:T(8,128)S(1)} collective-permute-done((f32[8,48]{1,0:T(8,128)S(1)}, f32[8,48]{1,0:T(8,128)S(1)}, u32[]{:S(2)}, u32[]{:S(2)}) %collective-permute-start.15) | collective-permute-done | bytes 1568 | tf_op jit(solution)/shard_map/ppermute | solution.py:646
  47.2 2.9 %collective-permute-done.20.refs_0_ = f32[8,48]{1,0:T(8,128)S(1)} collective-permute-done((f32[8,48]{1,0:T(8,128)S(1)}, f32[8,48]{1,0:T(8,128)S(1)}, u32[]{:S(2)}, u32[]{:S(2)}) %collective-permute-start.20) | collective-permute-done | bytes 1568 | tf_op jit(solution)/shard_map/ppermute | solution.py:646
  54.3 3.3 %collective-permute-done.25.refs_0_ = f32[8,48]{1,0:T(8,128)S(1)} collective-permute-done((f32[8,48]{1,0:T(8,128)S(1)}, f32[8,48]{1,0:T(8,128)S(1)}, u32[]{:S(2)}, u32[]{:S(2)}) %collective-permute-start.25) | collective-permute-done | bytes 1568 | tf_op jit(solution)/shard_map/ppermute | solution.py:646
  63.8 2.8 %collective-permute-done.30.refs_0_ = f32[3,8,128]{2,1,0:T(8,128)S(1)} collective-permute-done((f32[3,8,128]{2,1,0:T(8,128)S(1)}, f32[3,8,128]{2,1,0:T(8,128)S(1)}, u32[]{:S(2)}, u32[]{:S(2)}) %collective-permute-start.30) | collective-permute-done | bytes 12320 | tf_op jit(solution)/shard_map/ppermute | solution.py:646
  72.1 2.5 %collective-permute-done.35.refs_2_ = f32[6,8,128]{2,1,0:T(8,128)S(1)} collective-permute-done((f32[6,8,128]{2,1,0:T(8,128)S(1)}, f32[6,8,128]{2,1,0:T(8,128)S(1)}, u32[]{:S(2)}, u32[]{:S(2)}) %collective-permute-start.35) | collective-permute-done | bytes 24608 | tf_op jit(solution)/shard_map/ppermute | solution.py:646
  80.7 2.3 %collective-permute-done.40.refs_2_ = f32[6,8,128]{2,1,0:T(8,128)S(1)} collective-permute-done((f32[6,8,128]{2,1,0:T(8,128)S(1)}, f32[6,8,128]{2,1,0:T(8,128)S(1)}, u32[]{:S(2)}, u32[]{:S(2)}) %collective-permute-start.40) | collective-permute-done | bytes 24608 | tf_op jit(solution)/shard_map/ppermute | solution.py:646
  88.3 2.6 %collective-permute-done.45.refs_2_ = f32[6,8,128]{2,1,0:T(8,128)S(1)} collective-permute-done((f32[6,8,128]{2,1,0:T(8,128)S(1)}, f32[6,8,128]{2,1,0:T(8,128)S(1)}, u32[]{:S(2)}, u32[]{:S(2)}) %collective-permute-start.45) | collective-permute-done | bytes 24608 | tf_op jit(solution)/shard_map/ppermute | solution.py:646
  97.3 3.0 %collective-permute-done.50.refs_0_ = f32[3,8,128]{2,1,0:T(8,128)S(1)} collective-permute-done((f32[3,8,128]{2,1,0:T(8,128)S(1)}, f32[3,8,128]{2,1,0:T(8,128)S(1)}, u32[]{:S(2)}, u32[]{:S(2)}) %collective-permute-start.50) | collective-permute-done | bytes 12320 | tf_op jit(solution)/shard_map/ppermute | solution.py:646
  105.7 3.0 %collective-permute-done.55.refs_0_ = f32[8,48]{1,0:T(8,128)S(1)} collective-permute-done((f32[8,48]{1,0:T(8,128)S(1)}, f32[8,48]{1,0:T(8,128)S(1)}, u32[]{:S(2)}, u32[]{:S(2)}) %collective-permute-start.55) | collective-permute-done | bytes 1568 | tf_op jit(solution)/shard_map/ppermute | solution.py:646
  113.9 3.3 %collective-permute-done.60.refs_0_ = f32[8,48]{1,0:T(8,128)S(1)} collective-permute-done((f32[8,48]{1,0:T(8,128)S(1)}, f32[8,48]{1,0:T(8,128)S(1)}, u32[]{:S(2)}, u32[]{:S(2)}) %collective-permute-start.60) | collective-permute-done | bytes 1568 | tf_op jit(solution)/shard_map/ppermute | solution.py:646
  118.9 2.0 %collective-permute-start.65 = (f32[8,48]{1,0:T(8,128)S(1)}, f32[8,48]{1,0:T(8,128)S(1)}, u32[]{:S(2)}, u32[]{:S(2)}) collective-permute-start(f32[8,48]{1,0:T(8,128)S(1)} %kernel_sweep.10.y3_ref), channel_id=1, source_target_pairs={{0,6},{2,4},{4,2},{6,0},{1,7},{3,5},{5,3},{7,1},{8,14},{10,12},{12... | collective-permute-start | bytes 4616 | tf_op jit(solution)/shard_map/ppermute | solution.py:646
  121.3 3.0 %collective-permute-done.65.refs_0_ = f32[8,48]{1,0:T(8,128)S(1)} collective-permute-done((f32[8,48]{1,0:T(8,128)S(1)}, f32[8,48]{1,0:T(8,128)S(1)}, u32[]{:S(2)}, u32[]{:S(2)}) %collective-permute-start.65) | collective-permute-done | bytes 1568 | tf_op jit(solution)/shard_map/ppermute | solution.py:646
  129.4 3.3 %collective-permute-done.70.refs_0_ = f32[8,48]{1,0:T(8,128)S(1)} collective-permute-done((f32[8,48]{1,0:T(8,128)S(1)}, f32[8,48]{1,0:T(8,128)S(1)}, u32[]{:S(2)}, u32[]{:S(2)}) %collective-permute-start.70) | collective-permute-done | bytes 1568 | tf_op jit(solution)/shard_map/ppermute | solution.py:646
  137.9 2.9 %collective-permute-done.75.refs_0_ = f32[3,8,128]{2,1,0:T(8,128)S(1)} collective-permute-done((f32[3,8,128]{2,1,0:T(8,128)S(1)}, f32[3,8,128]{2,1,0:T(8,128)S(1)}, u32[]{:S(2)}, u32[]{:S(2)}) %collective-permute-start.75) | collective-permute-done | bytes 12320 | tf_op jit(solution)/shard_map/ppermute | solution.py:646
  147.4 2.6 %collective-permute-done.80.refs_2_ = f32[6,8,128]{2,1,0:T(8,128)S(1)} collective-permute-done((f32[6,8,128]{2,1,0:T(8,128)S(1)}, f32[6,8,128]{2,1,0:T(8,128)S(1)}, u32[]{:S(2)}, u32[]{:S(2)}) %collective-permute-start.80) | collective-permute-done | bytes 24608 | tf_op jit(solution)/shard_map/ppermute | solution.py:646
  151.9 2.0 %collective-permute-start.85 = (f32[6,8,128]{2,1,0:T(8,128)S(1)}, f32[6,8,128]{2,1,0:T(8,128)S(1)}, u32[]{:S(2)}, u32[]{:S(2)}) collective-permute-start(f32[6,8,128]{2,1,0:T(8,128)S(1)} %get-tuple-element.101), channel_id=1, source_target_pairs={{0,6},{2,4},{4,2},{6,0},{1,7},{3,5},{5,3},{7,1},{8,14},{10,12},{12... | collective-permute-start | bytes 73736 | tf_op jit(solution)/shard_map/ppermute | solution.py:646
  155.0 2.5 %collective-permute-done.85.refs_2_ = f32[6,8,128]{2,1,0:T(8,128)S(1)} collective-permute-done((f32[6,8,128]{2,1,0:T(8,128)S(1)}, f32[6,8,128]{2,1,0:T(8,128)S(1)}, u32[]{:S(2)}, u32[]{:S(2)}) %collective-permute-start.85) | collective-permute-done | bytes 24608 | tf_op jit(solution)/shard_map/ppermute | solution.py:646
  158.1 4.0 %kernel_last.1 = (f32[2,3,4,4,4,16]{5,4,3,2,1,0:T(4,128)}, f32[2,3,4,4,4,16]{5,4,3,2,1,0:T(4,128)}) custom-call(f32[144,8,128]{2,1,0:T(8,128)S(1)} %get-tuple-element.54.links_ref, f32[6,8,128]{2,1,0:T(8,128)S(1)} %get-tuple-element.55.rhs_ref, f32[6,8,128]{2,1,0:T(8,128)S(1)} %get-tuple-element.99.refs_0_, f32[6,8,128]{2,1,0:T(8,128)S(1)} %get-tuple-element.100.refs_1_, ...), custom_call_target="tpu_custom_call" | custom-call | tf_op jit(solution)/shard_map/kernel_last/pallas_call | solution.py:630
  (192 shorter events, 93.1 us)
Async XLA Ops:
  5.9 10.8 %collective-permute-start.2 = (f32[12,8,128]{2,1,0:T(8,128)S(1)}, f32[12,8,128]{2,1,0:T(8,128)S(1)}, u32[]{:S(2)}, u32[]{:S(2)}) collective-permute-start(f32[12,8,128]{2,1,0:T(8,128)S(1)} %get-tuple-element.60), channel_id=1, source_target_pairs={{1,0},{0,1},{3,2},{2,3},{5,4},{4,5},{7,6},{6,7},{9,8},{8,9},{11,10... | collective-permute-start | bytes 147464 | tf_op jit(solution)/shard_map/ppermute | solution.py:641
  8.9 5.6 %collective-permute-start = (f32[6,8,128]{2,1,0:T(8,128)S(1)}, f32[6,8,128]{2,1,0:T(8,128)S(1)}, u32[]{:S(2)}, u32[]{:S(2)}) collective-permute-start(f32[6,8,128]{2,1,0:T(8,128)S(1)} %get-tuple-element.58), channel_id=1, source_target_pairs={{0,6},{2,4},{4,2},{6,0},{1,7},{3,5},{5,3},{7,1},{8,14},{10,12},{12... | collective-permute-start | bytes 73736 | tf_op jit(solution)/shard_map/ppermute | solution.py:646
  17.7 7.0 %collective-permute-start.9 = (f32[3,8,128]{2,1,0:T(8,128)S(1)}, f32[3,8,128]{2,1,0:T(8,128)S(1)}, u32[]{:S(2)}, u32[]{:S(2)}) collective-permute-start(f32[3,8,128]{2,1,0:T(8,128)S(1)} %get-tuple-element.64.sol_ref.y2_ref), channel_id=1, source_target_pairs={{0,8},{8,0},{16,24},{24,16},{1,9},{9,1},{17,25},{25,17},{2,10},{10... | collective-permute-start | bytes 36872 | tf_op jit(solution)/shard_map/ppermute | solution.py:646
  17.8 6.8 %collective-permute-start.8 = (f32[3,8,128]{2,1,0:T(8,128)S(1)}, f32[3,8,128]{2,1,0:T(8,128)S(1)}, u32[]{:S(2)}, u32[]{:S(2)}) collective-permute-start(f32[3,8,128]{2,1,0:T(8,128)S(1)} %get-tuple-element.64.sol_ref.y2_ref), channel_id=1, source_target_pairs={{0,2},{2,0},{4,6},{6,4},{1,3},{3,1},{5,7},{7,5},{8,10},{10,8},{12,... | collective-permute-start | bytes 36872 | tf_op jit(solution)/shard_map/ppermute | solution.py:646
  18.1 6.6 %collective-permute-start.7 = (f32[3,8,128]{2,1,0:T(8,128)S(1)}, f32[3,8,128]{2,1,0:T(8,128)S(1)}, u32[]{:S(2)}, u32[]{:S(2)}) collective-permute-start(f32[3,8,128]{2,1,0:T(8,128)S(1)} %get-tuple-element.64.sol_ref.y2_ref), channel_id=1, source_target_pairs={{1,0},{0,1},{3,2},{2,3},{5,4},{4,5},{7,6},{6,7},{9,8},{8,9},{11,10... | collective-permute-start | bytes 36872 | tf_op jit(solution)/shard_map/ppermute | solution.py:641
  18.6 6.1 %collective-permute-start.6 = (f32[3,8,128]{2,1,0:T(8,128)S(1)}, f32[3,8,128]{2,1,0:T(8,128)S(1)}, u32[]{:S(2)}, u32[]{:S(2)}) collective-permute-start(f32[3,8,128]{2,1,0:T(8,128)S(1)} %get-tuple-element.64.sol_ref.y2_ref), channel_id=1, source_target_pairs={{0,24},{8,16},{16,8},{24,0},{1,25},{9,17},{17,9},{25,1},{2,26},{10... | collective-permute-start | bytes 36872 | tf_op jit(solution)/shard_map/ppermute | solution.py:646
  19.4 5.5 %collective-permute-start.5 = (f32[3,8,128]{2,1,0:T(8,128)S(1)}, f32[3,8,128]{2,1,0:T(8,128)S(1)}, u32[]{:S(2)}, u32[]{:S(2)}) collective-permute-start(f32[3,8,128]{2,1,0:T(8,128)S(1)} %get-tuple-element.64.sol_ref.y2_ref), channel_id=1, source_target_pairs={{0,6},{2,4},{4,2},{6,0},{1,7},{3,5},{5,3},{7,1},{8,14},{10,12},{12... | collective-permute-start | bytes 36872 | tf_op jit(solution)/shard_map/ppermute | solution.py:646
  36.7 5.4 %collective-permute-start.15 = (f32[8,48]{1,0:T(8,128)S(1)}, f32[8,48]{1,0:T(8,128)S(1)}, u32[]{:S(2)}, u32[]{:S(2)}) collective-permute-start(f32[8,48]{1,0:T(8,128)S(1)} %kernel_sweep.6.y3_ref), channel_id=1, source_target_pairs={{0,6},{2,4},{4,2},{6,0},{1,7},{3,5},{5,3},{7,1},{8,14},{10,12},{12... | collective-permute-start | bytes 4616 | tf_op jit(solution)/shard_map/ppermute | solution.py:646
  44.7 5.4 %collective-permute-start.20 = (f32[8,48]{1,0:T(8,128)S(1)}, f32[8,48]{1,0:T(8,128)S(1)}, u32[]{:S(2)}, u32[]{:S(2)}) collective-permute-start(f32[8,48]{1,0:T(8,128)S(1)} %kernel_sweep.7.y3_ref), channel_id=1, source_target_pairs={{0,6},{2,4},{4,2},{6,0},{1,7},{3,5},{5,3},{7,1},{8,14},{10,12},{12... | collective-permute-start | bytes 4616 | tf_op jit(solution)/shard_map/ppermute | solution.py:646
  61.1 5.5 %collective-permute-start.30 = (f32[3,8,128]{2,1,0:T(8,128)S(1)}, f32[3,8,128]{2,1,0:T(8,128)S(1)}, u32[]{:S(2)}, u32[]{:S(2)}) collective-permute-start(f32[3,8,128]{2,1,0:T(8,128)S(1)} %kernel_sweep_up.2.y2_ref), channel_id=1, source_target_pairs={{0,6},{2,4},{4,2},{6,0},{1,7},{3,5},{5,3},{7,1},{8,14},{10,12},{12... | collective-permute-start | bytes 36872 | tf_op jit(solution)/shard_map/ppermute | solution.py:646
  68.4 6.6 %collective-permute-start.37 = (f32[12,8,128]{2,1,0:T(8,128)S(1)}, f32[12,8,128]{2,1,0:T(8,128)S(1)}, u32[]{:S(2)}, u32[]{:S(2)}) collective-permute-start(f32[12,8,128]{2,1,0:T(8,128)S(1)} %get-tuple-element.71), channel_id=1, source_target_pairs={{1,0},{0,1},{3,2},{2,3},{5,4},{4,5},{7,6},{6,7},{9,8},{8,9},{11,10... | collective-permute-start | bytes 147464 | tf_op jit(solution)/shard_map/ppermute | solution.py:641
  69.0 5.6 %collective-permute-start.35 = (f32[6,8,128]{2,1,0:T(8,128)S(1)}, f32[6,8,128]{2,1,0:T(8,128)S(1)}, u32[]{:S(2)}, u32[]{:S(2)}) collective-permute-start(f32[6,8,128]{2,1,0:T(8,128)S(1)} %get-tuple-element.69), channel_id=1, source_target_pairs={{0,6},{2,4},{4,2},{6,0},{1,7},{3,5},{5,3},{7,1},{8,14},{10,12},{12... | collective-permute-start | bytes 73736 | tf_op jit(solution)/shard_map/ppermute | solution.py:646
  75.9 8.0 %collective-permute-start.42 = (f32[12,8,128]{2,1,0:T(8,128)S(1)}, f32[12,8,128]{2,1,0:T(8,128)S(1)}, u32[]{:S(2)}, u32[]{:S(2)}) collective-permute-start(f32[12,8,128]{2,1,0:T(8,128)S(1)} %get-tuple-element.78), channel_id=1, source_target_pairs={{1,0},{0,1},{3,2},{2,3},{5,4},{4,5},{7,6},{6,7},{9,8},{8,9},{11,10... | collective-permute-start | bytes 147464 | tf_op jit(solution)/shard_map/ppermute | solution.py:641
  77.4 5.6 %collective-permute-start.40 = (f32[6,8,128]{2,1,0:T(8,128)S(1)}, f32[6,8,128]{2,1,0:T(8,128)S(1)}, u32[]{:S(2)}, u32[]{:S(2)}) collective-permute-start(f32[6,8,128]{2,1,0:T(8,128)S(1)} %get-tuple-element.76), channel_id=1, source_target_pairs={{0,6},{2,4},{4,2},{6,0},{1,7},{3,5},{5,3},{7,1},{8,14},{10,12},{12... | collective-permute-start | bytes 73736 | tf_op jit(solution)/shard_map/ppermute | solution.py:646
  84.7 6.8 %collective-permute-start.47 = (f32[12,8,128]{2,1,0:T(8,128)S(1)}, f32[12,8,128]{2,1,0:T(8,128)S(1)}, u32[]{:S(2)}, u32[]{:S(2)}) collective-permute-start(f32[12,8,128]{2,1,0:T(8,128)S(1)} %get-tuple-element.85), channel_id=1, source_target_pairs={{1,0},{0,1},{3,2},{2,3},{5,4},{4,5},{7,6},{6,7},{9,8},{8,9},{11,10... | collective-permute-start | bytes 147464 | tf_op jit(solution)/shard_map/ppermute | solution.py:641
  85.3 5.6 %collective-permute-start.45 = (f32[6,8,128]{2,1,0:T(8,128)S(1)}, f32[6,8,128]{2,1,0:T(8,128)S(1)}, u32[]{:S(2)}, u32[]{:S(2)}) collective-permute-start(f32[6,8,128]{2,1,0:T(8,128)S(1)} %get-tuple-element.83), channel_id=1, source_target_pairs={{0,6},{2,4},{4,2},{6,0},{1,7},{3,5},{5,3},{7,1},{8,14},{10,12},{12... | collective-permute-start | bytes 73736 | tf_op jit(solution)/shard_map/ppermute | solution.py:646
  94.8 5.5 %collective-permute-start.50 = (f32[3,8,128]{2,1,0:T(8,128)S(1)}, f32[3,8,128]{2,1,0:T(8,128)S(1)}, u32[]{:S(2)}, u32[]{:S(2)}) collective-permute-start(f32[3,8,128]{2,1,0:T(8,128)S(1)} %get-tuple-element.89.sol_ref.y2_ref), channel_id=1, source_target_pairs={{0,6},{2,4},{4,2},{6,0},{1,7},{3,5},{5,3},{7,1},{8,14},{10,12},{12... | collective-permute-start | bytes 36872 | tf_op jit(solution)/shard_map/ppermute | solution.py:646
  111.7 5.4 %collective-permute-start.60 = (f32[8,48]{1,0:T(8,128)S(1)}, f32[8,48]{1,0:T(8,128)S(1)}, u32[]{:S(2)}, u32[]{:S(2)}) collective-permute-start(f32[8,48]{1,0:T(8,128)S(1)} %kernel_sweep.9.y3_ref), channel_id=1, source_target_pairs={{0,6},{2,4},{4,2},{6,0},{1,7},{3,5},{5,3},{7,1},{8,14},{10,12},{12... | collective-permute-start | bytes 4616 | tf_op jit(solution)/shard_map/ppermute | solution.py:646
  127.3 5.4 %collective-permute-start.70 = (f32[8,48]{1,0:T(8,128)S(1)}, f32[8,48]{1,0:T(8,128)S(1)}, u32[]{:S(2)}, u32[]{:S(2)}) collective-permute-start(f32[8,48]{1,0:T(8,128)S(1)} %kernel_sweep.11.y3_ref), channel_id=1, source_target_pairs={{0,6},{2,4},{4,2},{6,0},{1,7},{3,5},{5,3},{7,1},{8,14},{10,12},{12... | collective-permute-start | bytes 4616 | tf_op jit(solution)/shard_map/ppermute | solution.py:646
  135.3 5.5 %collective-permute-start.75 = (f32[3,8,128]{2,1,0:T(8,128)S(1)}, f32[3,8,128]{2,1,0:T(8,128)S(1)}, u32[]{:S(2)}, u32[]{:S(2)}) collective-permute-start(f32[3,8,128]{2,1,0:T(8,128)S(1)} %kernel_sweep_up.3.y2_ref), channel_id=1, source_target_pairs={{0,6},{2,4},{4,2},{6,0},{1,7},{3,5},{5,3},{7,1},{8,14},{10,12},{12... | collective-permute-start | bytes 36872 | tf_op jit(solution)/shard_map/ppermute | solution.py:646
  142.8 7.7 %collective-permute-start.82 = (f32[12,8,128]{2,1,0:T(8,128)S(1)}, f32[12,8,128]{2,1,0:T(8,128)S(1)}, u32[]{:S(2)}, u32[]{:S(2)}) collective-permute-start(f32[12,8,128]{2,1,0:T(8,128)S(1)} %get-tuple-element.96), channel_id=1, source_target_pairs={{1,0},{0,1},{3,2},{2,3},{5,4},{4,5},{7,6},{6,7},{9,8},{8,9},{11,10... | collective-permute-start | bytes 147464 | tf_op jit(solution)/shard_map/ppermute | solution.py:641
  144.3 5.6 %collective-permute-start.80 = (f32[6,8,128]{2,1,0:T(8,128)S(1)}, f32[6,8,128]{2,1,0:T(8,128)S(1)}, u32[]{:S(2)}, u32[]{:S(2)}) collective-permute-start(f32[6,8,128]{2,1,0:T(8,128)S(1)} %get-tuple-element.94), channel_id=1, source_target_pairs={{0,6},{2,4},{4,2},{6,0},{1,7},{3,5},{5,3},{7,1},{8,14},{10,12},{12... | collective-permute-start | bytes 73736 | tf_op jit(solution)/shard_map/ppermute | solution.py:646
  151.3 6.8 %collective-permute-start.87 = (f32[12,8,128]{2,1,0:T(8,128)S(1)}, f32[12,8,128]{2,1,0:T(8,128)S(1)}, u32[]{:S(2)}, u32[]{:S(2)}) collective-permute-start(f32[12,8,128]{2,1,0:T(8,128)S(1)} %get-tuple-element.103), channel_id=1, source_target_pairs={{1,0},{0,1},{3,2},{2,3},{5,4},{4,5},{7,6},{6,7},{9,8},{8,9},{11,10... | collective-permute-start | bytes 147464 | tf_op jit(solution)/shard_map/ppermute | solution.py:641
  151.9 5.6 %collective-permute-start.85 = (f32[6,8,128]{2,1,0:T(8,128)S(1)}, f32[6,8,128]{2,1,0:T(8,128)S(1)}, u32[]{:S(2)}, u32[]{:S(2)}) collective-permute-start(f32[6,8,128]{2,1,0:T(8,128)S(1)} %get-tuple-element.101), channel_id=1, source_target_pairs={{0,6},{2,4},{4,2},{6,0},{1,7},{3,5},{5,3},{7,1},{8,14},{10,12},{12... | collective-permute-start | bytes 73736 | tf_op jit(solution)/shard_map/ppermute | solution.py:646
  (72 other events, 308.1 us)

commit v2 on v1

--- a/solution.py
+++ b/solution.py
@@ -135,10 +135,10 @@
         acc = sub(acc, [shift_y(site, x, -reach) for x in back])
     sent = []
     for direction in range(3):
-        near = [cyclic(site, x, direction, -1) for x in link_adjoint(links_ref, direction, 0, field)]
-        far = link_adjoint(links_ref, direction, 1, field)
+        near, far = backward(site, links_ref, field, direction)
         first, last = site.first(direction), site.last(direction)
-        sent.append([jnp.where(first, n, f) for n, f in zip(near, far)])
+        if direction < 2:
+            sent.append([jnp.where(first, n, f) for n, f in zip(near, far)])
         acc = [
             a - jnp.where(first, 0.0, n) - jnp.where(last, cyclic(site, f, direction, 1), 0.0)
             for a, n, f in zip(acc, near, far)
@@ -146,6 +146,20 @@
     for i in range(6):
         acc_ref[i] = acc[i]
     return sent
+
+
+class PairedLinks:
+    def __init__(self, ref):
+        self.ref = ref
+
+    def __getitem__(self, i):
+        i -= 72
+        return self.ref[i // 2].astype(F32)[8 * (i % 2) : 8 * (i % 2) + 8]
+
+
+def backward(site, links_ref, field, direction):
+    near = [cyclic(site, x, direction, -1) for x in link_adjoint(links_ref, direction, 0, field)]
+    return near, link_adjoint(links_ref, direction, 1, field)
 
 
 def fine_receive(site, links_ref, field, acc, ahead, behind):
@@ -444,11 +458,9 @@
     return lax.rem(lax.axis_index(axis), 2) == 1
 
 
-def finish_fine(site, links_ref, solution, sol_ref, acc_ref, z0_ref, z1_ref, t0_ref, t1_ref, x_ref):
+def finish_fine(site, links_ref, solution, sol_ref, acc_ref, z0_ref, z1_ref, t0_ref, t1_ref):
     store(sol_ref, solution)
-    store(x_ref, solution)
-    back_t, back_z, back_x = fine_send(site, links_ref, solution, acc_ref)
-    store(x_ref, back_x, 6)
+    back_t, back_z = fine_send(site, links_ref, solution, acc_ref)
     for axis, back, ref0, ref1 in (("gz", back_z, z0_ref, z1_ref), ("ta", back_t, t0_ref, t1_ref)):
         odd = is_odd(axis)
         store(ref0, [jnp.where(odd, s, b) for s, b in zip(solution, back)])
@@ -462,12 +474,14 @@
 
 
 def begin_fine(site, links_ref, refs):
-    sol_ref, acc_ref, z1, t1, x, z0, t0 = refs
+    sol_ref, acc_ref, t0, z1, z0, t1, x, gx_ref = refs
     solution = load(sol_ref, 6)
     ahead_t, behind_t = by_parity("ta", load(t0, 6), load(t1, 6))
     ahead_z, behind_z = by_parity("gz", load(z0, 6), load(z1, 6))
     ahead = [ahead_t, ahead_z, load(x, 6)]
-    behind = [behind_t, behind_z, load(x, 6, 6)]
+    near, far = backward(site, PairedLinks(gx_ref), ahead[2], 2)
+    first = site.first(2)
+    behind = [behind_t, behind_z, [jnp.where(first, n, f) for n, f in zip(near, far)]]
     return solution, fine_receive(site, links_ref, solution, load(acc_ref, 6), ahead, behind)
 
 
@@ -487,24 +501,31 @@
     if transposed:
         m, n = n, m
     fine = (((n & 7) << 1) | ((n >> 3) & 1)) | (n & 112)
-    return m == (fine & (min(rows, columns) - 1))
-
-
-def exact_dot(a, b):
-    return jnp.dot(a, b, precision=HIGHEST, preferred_element_type=F32)
-
-
-def prepare_links(site, links_ref, g_ref):
+    return (m == (fine & (min(rows, columns) - 1))).astype(BF16)
+
+
+def dot(a, b):
+    return jnp.dot(a, b, preferred_element_type=F32)
+
+
+def three_parts(x):
+    high = x.astype(BF16)
+    rest = x - high.astype(F32)
+    mid = rest.astype(BF16)
+    return high, mid, (rest - mid.astype(F32)).astype(BF16)
+
+
+def prepare_links(site, links_ref, g_ref, gx_ref):
     rows = row_order(False).astype(BF16)
-    lanes = y_order(128, 128, False).astype(BF16)
+    lanes = y_order(128, 128, False)
     signs = [jnp.full((8, 128), 0.5, F32)]
     for d in LANE_BITS:
         signs.append(jnp.where(site.lane_bit(d), -signs[-1], signs[-1]))
     for rc in range(9):
-        block = links_ref[pl.ds(64 * rc, 64), :]
-        block = jnp.dot(rows, block, preferred_element_type=F32).astype(BF16)
+        parts = [links_ref[rc // 3, rc % 3, t, z].astype(F32) for t in range(4) for z in range(4)]
+        block = dot(rows, jnp.concatenate(parts, axis=0).astype(BF16)).astype(BF16)
         for h in range(2):
-            half = jnp.dot(block[:, 128 * h : 128 * h + 128], lanes, preferred_element_type=F32)
+            half = dot(block[:, 128 * h : 128 * h + 128], lanes)
             v = [half[8 * w : 8 * w + 8] for w in range(8)]
             for d, k in zip(LANE_BITS, (4, 2, 1)):
                 bit = site.lane_bit(d)
@@ -515,75 +536,86 @@
                         v[w | k] = jnp.where(bit, hi, left(lo, d))
             for m in range(8):
                 g_ref[(8 * h + m) * 9 + rc] = v[m] * signs[2 * h + m // 4]
+    for i in range(0, 36, 2):
+        gx_ref[i // 2] = jnp.concatenate([g_ref[72 + i], g_ref[73 + i]], axis=0).astype(BF16)
 
 
 def gather_fine(site, field_ref):
-    rows = row_order(False).astype(F32)
-    lanes = y_order(16, 128, False).astype(F32)
+    rows = row_order(False).astype(BF16)
+    lanes = y_order(16, 128, False)
     group = site.lane >> 4
     out = []
     for p in range(2):
         for c in range(3):
             parts = [field_ref[p, c, t, z] for t in range(4) for z in range(4)]
-            spread_out = exact_dot(rows, exact_dot(jnp.concatenate(parts, axis=0), lanes))
-            total = spread_out[:8]
-            for w in range(1, 8):
-                total = jnp.where(group == w, spread_out[8 * w : 8 * w + 8], total)
+            moved = [dot(rows, x) for x in three_parts(jnp.concatenate(parts, axis=0))]
+            wide = dot(jnp.concatenate(moved, axis=0).astype(BF16), lanes)
+            total = None
+            for w in range(8):
+                own = wide[8 * w : 8 * w + 8] + wide[64 + 8 * w : 72 + 8 * w] + wide[128 + 8 * w : 136 + 8 * w]
+                total = own if w == 0 else jnp.where(group == w, own, total)
             out.append(total)
     return out
 
 
 def scatter_fine(site, field, out_ref):
     rows = row_order(True).astype(F32)
-    lanes = y_order(128, 16, True).astype(F32)
+    rows = jnp.concatenate([rows, rows, rows], axis=1).astype(BF16)
+    lanes = y_order(128, 16, True)
     group = site.lane >> 4
     for p in range(2):
         for c in range(3):
-            x = field[3 * p + c]
-            tall = jnp.concatenate([jnp.where(group == w, x, 0.0) for w in range(8)], axis=0)
-            value = exact_dot(rows, exact_dot(tall, lanes))
+            parts = [x.astype(F32) for x in three_parts(field[3 * p + c])]
+            tall = jnp.concatenate([jnp.where(group == w, x, 0.0) for x in parts for w in range(8)], axis=0)
+            value = dot(rows, dot(tall.astype(BF16), lanes).astype(BF16))
             for t in range(4):
                 for z in range(4):
                     out_ref[p, c, t, z] = value[16 * t + 4 * z : 16 * t + 4 * z + 4]
 
 
-def kernel_first(links_ref, block_ref, source_ref, g_ref, rhs_ref, *outs):
+def kernel_links(block_ref, links_ref, g_ref, gx_ref):
+    prepare_links(Site(), links_ref, g_ref, gx_ref)
+
+
+def kernel_first(g_ref, block_ref, source_ref, rhs_ref, *outs):
     site = Site()
     rhs = gather_fine(site, source_ref)
     store(rhs_ref, rhs)
-    prepare_links(site, links_ref, g_ref)
     finish_fine(site, g_ref, fine_matrix(site, block_ref, rhs), *outs)
 
 
 def kernel_smooth(links_ref, block_ref, rhs_ref, *refs):
     site = Site()
-    solution, applied = begin_fine(site, links_ref, refs[:7])
+    solution, applied = begin_fine(site, links_ref, refs[:8])
     residual = sub(load(rhs_ref, 6), applied)
     solution = add(solution, fine_matrix(site, block_ref, residual))
-    finish_fine(site, links_ref, solution, *refs[7:])
+    finish_fine(site, links_ref, solution, *refs[8:])
 
 
 def kernel_last(links_ref, rhs_ref, *refs):
     site = Site()
-    solution, applied = begin_fine(site, links_ref, refs[:7])
-    scatter_fine(site, solution, refs[7])
+    _, applied = begin_fine(site, links_ref, refs[:8])
     scatter_fine(site, sub(load(rhs_ref, 6), applied), refs[8])
+
+
+def kernel_scatter(field_ref, out_ref):
+    scatter_fine(Site(), load(field_ref, 6), out_ref)
 
 
 def kernel_restrict(links_ref, near_ref, jacobi_ref, rhs_ref, *refs):
     site = Site()
-    _, applied = begin_fine(site, links_ref, refs[:7])
+    _, applied = begin_fine(site, links_ref, refs[:8])
     residual = sub(load(rhs_ref, 6), applied)
     mid_res = restrict_fine(site, near_ref, residual)
-    store(refs[7], mid_res)
-    store(refs[8], mid_matrix(site, jacobi_ref, mid_res))
+    store(refs[8], mid_res)
+    store(refs[9], mid_matrix(site, jacobi_ref, mid_res))
 
 
 def neighbours(refs, get):
-    z1, t1, nx, z0, t0 = refs[:5]
+    nx, t1, z0, z1, t0 = refs
     ahead_t, behind_t = by_parity("ta", get(t0), get(t1))
     ahead_z, behind_z = by_parity("gz", get(z0), get(z1))
-    return [ahead_t, ahead_z, get(nx)], [behind_t, behind_z, get(refs[-1] if len(refs) > 5 else nx)]
+    return [ahead_t, ahead_z, get(nx)], [behind_t, behind_z, get(nx)]
 
 
 def kernel_mid_down(stencil_ref, near_ref, jacobi_ref, res_ref, sol_ref, *refs):
@@ -617,7 +649,7 @@
 
 def kernel_mid_up(links_ref, stencil_ref, jacobi_ref, near_ref, old_ref, res_ref, y2_ref, *refs):
     site = Site()
-    around, outs, spread_ref = refs[:-8], refs[-8:-1], refs[-1]
+    around, outs, spread_ref = refs[:-7], refs[-7:-1], refs[-1]
     ahead, behind = neighbours(around, lambda r: load(r, 3))
     y2 = load(y2_ref, 3)
     rest = sub(load(res_ref, 3), mid_stencil_apply(site, stencil_ref, y2, ahead, behind))
@@ -626,10 +658,14 @@
     finish_fine(site, links_ref, solution, *outs)
 
 
-def call(kernel, outs, scratch, *args):
+def call(kernel, outs, scratch, *args, first_any=False):
+    specs = [pl.BlockSpec(memory_space=pltpu.VMEM)] * len(args)
+    if first_any:
+        specs[0] = pl.BlockSpec(memory_space=pl.ANY)
     return pl.pallas_call(
         kernel,
-        out_shape=[jax.ShapeDtypeStruct(s, F32) for s in outs],
+        out_shape=[jax.ShapeDtypeStruct(*s) if s[1] == BF16 else jax.ShapeDtypeStruct(s, F32) for s in outs],
+        in_specs=specs,
         scratch_shapes=[pltpu.VMEM(s, F32) for s in scratch],
         compiler_params=pltpu.CompilerParams(vmem_limit_bytes=VMEM_BYTES),
         name=kernel.__name__,
@@ -647,26 +683,24 @@
 
 
 def exchange(v):
+    x = from_behind(v, "xy", 1)
+    t1 = swap(v, "ta", 1)
+    z0 = swap(v, "gz", 0)
     z1 = swap(v, "gz", 1)
-    t1 = swap(v, "ta", 1)
-    x = from_behind(v, "xy", -1)
-    z0 = swap(v, "gz", 0)
-    t0 = swap(v, "ta", 0)
-    return [z1, t1, x, z0, t0] + ([from_behind(v, "xy", 1)] if lax.axis_size("xy") > 2 else [])
-
-
-def exchange_fine(sol, acc, z0, z1, t0, t1, x):
+    return [x, t1, z0, z1, swap(v, "ta", 0)]
+
+
+def exchange_fine(gx, sol, acc, z0, z1, t0, t1):
+    x = from_behind(sol, "xy", 1)
+    t1 = swap(t1, "ta", 1)
+    z0 = swap(z0, "gz", 0)
     z1 = swap(z1, "gz", 1)
-    t1 = swap(t1, "ta", 1)
-    if lax.axis_size("xy") == 2:
-        x = from_behind(x, "xy", 1)
-    else:
-        x = jnp.concatenate([from_behind(x[:6], "xy", -1), from_behind(x[6:], "xy", 1)])
-    return [sol, acc, z1, t1, x, swap(z0, "gz", 0), swap(t0, "ta", 0)]
+    t0 = swap(t0, "ta", 0)
+    return [sol, acc, t0, z1, z0, t1, x, gx]
 
 
 TILE6 = (6, 8, 128)
-FINE_OUT = [TILE6] * 6 + [(12, 8, 128)]
+FINE_OUT = [TILE6] * 6
 
 
 def local(
@@ -680,7 +714,6 @@
     coarse_stencil,
     coarse_jacobi,
 ):
-    links_flat = links.reshape(576, 256)
     block = block_inverse.reshape(384, 768)
     near1 = near_fine.reshape(192, 768)
     stencil2 = mid_stencil.reshape(1728, 384)
@@ -691,9 +724,11 @@
     mid = (3, 8, 128)
     coarse = (8, 48)
 
-    g, rhs, *state = call(kernel_first, [(144, 8, 128), TILE6] + FINE_OUT, [], links_flat, block, right_side)
+    g, gx = call(kernel_links, [(144, 8, 128), ((18, 16, 128), BF16)], [], block, links, first_any=True)
+    gx = from_behind(gx, "xy", 1)
+    rhs, *state = call(kernel_first, [TILE6] + FINE_OUT, [], g, block, right_side)
     for cycle_no in range(CYCLES):
-        r2, y2 = call(kernel_restrict, [mid, mid], [], g, near1, jacobi2, rhs, *exchange_fine(*state))
+        r2, y2 = call(kernel_restrict, [mid, mid], [], g, near1, jacobi2, rhs, *exchange_fine(gx, *state))
         r3, y3 = call(
             kernel_mid_down, [coarse, coarse], [(2, 48, 128)], stencil2, near2, jacobi3, r2, y2, *exchange(y2)
         )
@@ -705,10 +740,13 @@
         state = call(
             kernel_mid_up, FINE_OUT, [(48, 8, 128)], g, stencil2, jacobi2, near1, state[0], r2, y2, *exchange(y2)
         )
-        state = call(kernel_smooth, FINE_OUT, [], g, block, rhs, *exchange_fine(*state))
+        state = call(kernel_smooth, FINE_OUT, [], g, block, rhs, *exchange_fine(gx, *state))
         if cycle_no < CYCLES - 1:
-            state = call(kernel_smooth, FINE_OUT, [], g, block, rhs, *exchange_fine(*state))
-    return call(kernel_last, [right_side.shape] * 2, [], g, rhs, *exchange_fine(*state))
+            state = call(kernel_smooth, FINE_OUT, [], g, block, rhs, *exchange_fine(gx, *state))
+    around = exchange_fine(gx, *state)
+    (solution,) = call(kernel_scatter, [right_side.shape], [], state[0])
+    (residual,) = call(kernel_last, [right_side.shape], [], g, rhs, *around)
+    return solution, residual
 
 
 def solution(mesh):

time: 162 us -> 151 us (0.932)
  waiting for transfers between devices: 56.8 us -> 37.2 us
  starting transfers between devices: 74.7 us -> 84.8 us
    ppermute x72, waiting for transfers between devices: 56.2 us -> 23.9 us  [swap(): lax.ppermute(block, axis, [(i, ((i + phase ^ 1) - phase) % n) for i in ra...]
    ppermute x18 -> x19, waiting for transfers between devices: 0.63 us -> 13.2 us  [from_behind(): lax.ppermute(block, axis, [((i - distance) % n, i) for i in range(n)])]
    ppermute x18 -> x19, starting transfers between devices: 20.7 us -> 28 us  [from_behind(): lax.ppermute(block, axis, [((i - distance) % n, i) for i in range(n)])]
    ppermute x72, starting transfers between devices: 54 us -> 56.8 us  [swap(): lax.ppermute(block, axis, [(i, ((i + phase ^ 1) - phase) % n) for i in ra...]
    pallas_call x19 -> x21, Pallas kernels: 23 us -> 22 us  [call(): pl.pallas_call(kernel, out_shape=[jax.ShapeDtypeStruct(*s) if s[1] == BF1...]
  transfers between devices with their start and end apart: 90 -> 91, of which waited for: 42 -> 43; matrix products, arithmetic and copies ran while one was open for 2% -> 2% of each run, Pallas kernels for 0% -> 1%
where the time goes in v2:
time: 151 us
  starting transfers between devices  84.8 us (56%)
  waiting for transfers between devices  37.2 us (25%)
  Pallas kernels  22 us (15%)
  local copies, waits for them, and re-layouts  5.64 us (4%)
    ppermute x72, starting transfers between devices, swap(): lax.ppermute(block, axis, [(i, ((i + phase ^ 1) - phase) % n) for i in ra...  56.8 us
    ppermute x19, starting transfers between devices, from_behind(): lax.ppermute(block, axis, [((i - distance) % n, i) for i in range(n)])  28 us
    ppermute x72, waiting for transfers between devices, swap(): lax.ppermute(block, axis, [(i, ((i + phase ^ 1) - phase) % n) for i in ra...  23.9 us
    pallas_call x21, Pallas kernels, call(): pl.pallas_call(kernel, out_shape=[jax.ShapeDtypeStruct(*s) if s[1] == BF1...  22 us
    ppermute x19, waiting for transfers between devices, from_behind(): lax.ppermute(block, axis, [((i - distance) % n, i) for i in range(n)])  13.2 us
    reshape x1, local copies, waits for them, and re-layouts, local(): stencil2 = mid_stencil.reshape(1728, 384)  3.4 us
  transfers between devices with their start and end apart: 91, of which 43 were waited for; matrix products, arithmetic and copies ran while one was open for 2% of the time, Pallas kernels for 1%

profile of v2, /device:TPU:0, one launch (start us, length us, event | category | flops | bytes accessed | tf_op | source)
XLA Modules:
  0.0 150.6 jit_solution(5252288100598749699)
XLA Ops:
  0.6 2.0 %reshape.25.block_ref = bf16[384,768]{1,0:T(8,128)(2,1)S(1)} reshape(bf16[48,2,2,2,768]{4,3,2,1,0:T(2,128)(2,1)} %param.11) | data formatting | bytes 1179648 | tf_op jit(solution)/shard_map/reshape | solution.py:717
  2.7 1.6 %kernel_links.1 = (f32[144,8,128]{2,1,0:T(8,128)S(1)}, bf16[18,16,128]{2,1,0:T(8,128)(2,1)S(1)}) custom-call(bf16[384,768]{1,0:T(8,128)(2,1)S(1)} %reshape.25.block_ref, bf16[3,3,4,4,4,256]{5,4,3,2,1,0:T(4,128)(2,1)S(1)} %copy-done.3), custom_call_target="tpu_custom_call" | custom-call | tf_op jit(solution)/shard_map/kernel_links/pallas_call | solution.py:665
  4.3 3.0 %collective-permute-start.5 = (bf16[18,16,128]{2,1,0:T(8,128)(2,1)S(1)}, bf16[18,16,128]{2,1,0:T(8,128)(2,1)S(1)}, u32[]{:S(2)}, u32[]{:S(2)}) collective-permute-start(bf16[18,16,128]{2,1,0:T(8,128)(2,1)S(1)} %get-tuple-element.57), channel_id=1, source_target_pairs={{1,0},{0,1},{3,2},{2,3},{5,4},{4,5},{7,6},{6,7},{9,8},{8,9},{11,10... | collective-permute-start | bytes 221192 | tf_op jit(solution)/shard_map/ppermute | solution.py:677
  8.5 3.7 %collective-permute-start.1 = (f32[6,8,128]{2,1,0:T(8,128)S(1)}, f32[6,8,128]{2,1,0:T(8,128)S(1)}, u32[]{:S(2)}, u32[]{:S(2)}) collective-permute-start(f32[6,8,128]{2,1,0:T(8,128)S(1)} %get-tuple-element.54), channel_id=1, source_target_pairs={{0,6},{2,4},{4,2},{6,0},{1,7},{3,5},{5,3},{7,1},{8,14},{10,12},{12... | collective-permute-start | bytes 73736 | tf_op jit(solution)/shard_map/ppermute | solution.py:682
  14.4 1.7 %collective-permute-done.2.refs_4_ = f32[6,8,128]{2,1,0:T(8,128)S(1)} collective-permute-done((f32[6,8,128]{2,1,0:T(8,128)S(1)}, f32[6,8,128]{2,1,0:T(8,128)S(1)}, u32[]{:S(2)}, u32[]{:S(2)}) %collective-permute-start.2) | collective-permute-done | bytes 24608 | tf_op jit(solution)/shard_map/ppermute | solution.py:682
  20.9 3.4 %reshape.26.stencil_ref = bf16[1728,384]{1,0:T(8,128)(2,1)S(1)} reshape(bf16[9,24,2,2,2,384]{5,4,3,2,1,0:T(2,128)(2,1)} %param.13) | data formatting | bytes 2654208 | tf_op jit(solution)/shard_map/reshape | solution.py:719
  24.4 1.7 %kernel_mid_down.2 = (f32[8,48]{1,0:T(8,128)S(1)}, f32[8,48]{1,0:T(8,128)S(1)}) custom-call(bf16[1728,384]{1,0:T(8,128)(2,1)S(1)} %reshape.26.stencil_ref, bf16[48,3072]{1,0:T(8,128)(2,1)S(1)} %bitcast.25, bf16[96,192]{1,0:T(8,128)(2,1)S(1)} %bitcast.15, f32[3,8,128]{2,1,0:T(8,128)S(1)} %get-tuple-element.58.res_ref, ...), custom_call_target="tpu_custom_call" | custom-call | tf_op jit(solution)/shard_map/kernel_mid_down/pallas_call | solution.py:665
  26.3 2.8 %collective-permute-start.14 = (f32[8,48]{1,0:T(8,128)S(1)}, f32[8,48]{1,0:T(8,128)S(1)}, u32[]{:S(2)}, u32[]{:S(2)}) collective-permute-start(f32[8,48]{1,0:T(8,128)S(1)} %get-tuple-element.61.y3_ref), channel_id=1, source_target_pairs={{0,6},{2,4},{4,2},{6,0},{1,7},{3,5},{5,3},{7,1},{8,14},{10,12},{12... | collective-permute-start | bytes 4616 | tf_op jit(solution)/shard_map/ppermute | solution.py:682
  38.1 1.5 %collective-permute-done.19.refs_3_ = f32[8,48]{1,0:T(8,128)S(1)} collective-permute-done((f32[8,48]{1,0:T(8,128)S(1)}, f32[8,48]{1,0:T(8,128)S(1)}, u32[]{:S(2)}, u32[]{:S(2)}) %collective-permute-start.19) | collective-permute-done | bytes 1568 | tf_op jit(solution)/shard_map/ppermute | solution.py:682
  40.7 2.6 %collective-permute-start.24 = (f32[8,48]{1,0:T(8,128)S(1)}, f32[8,48]{1,0:T(8,128)S(1)}, u32[]{:S(2)}, u32[]{:S(2)}) collective-permute-start(f32[8,48]{1,0:T(8,128)S(1)} %kernel_sweep.7.y3_ref), channel_id=1, source_target_pairs={{0,6},{2,4},{4,2},{6,0},{1,7},{3,5},{5,3},{7,1},{8,14},{10,12},{12... | collective-permute-start | bytes 4616 | tf_op jit(solution)/shard_map/ppermute | solution.py:682
  52.4 1.5 %collective-permute-done.29.refs_3_ = f32[8,48]{1,0:T(8,128)S(1)} collective-permute-done((f32[8,48]{1,0:T(8,128)S(1)}, f32[8,48]{1,0:T(8,128)S(1)}, u32[]{:S(2)}, u32[]{:S(2)}) %collective-permute-start.29) | collective-permute-done | bytes 1568 | tf_op jit(solution)/shard_map/ppermute | solution.py:682
  55.9 2.7 %collective-permute-start.34 = (f32[3,8,128]{2,1,0:T(8,128)S(1)}, f32[3,8,128]{2,1,0:T(8,128)S(1)}, u32[]{:S(2)}, u32[]{:S(2)}) collective-permute-start(f32[3,8,128]{2,1,0:T(8,128)S(1)} %kernel_sweep_up.2.y2_ref), channel_id=1, source_target_pairs={{0,6},{2,4},{4,2},{6,0},{1,7},{3,5},{5,3},{7,1},{8,14},{10,12},{12... | collective-permute-start | bytes 36872 | tf_op jit(solution)/shard_map/ppermute | solution.py:682
  63.3 1.8 %kernel_mid_up.2 = (f32[6,8,128]{2,1,0:T(8,128)S(1)}, f32[6,8,128]{2,1,0:T(8,128)S(1)}, f32[6,8,128]{2,1,0:T(8,128)S(1)}, f32[6,8,128]{2,1,0:T(8,128)S(1)}, f32[...) custom-call(f32[144,8,128]{2,1,0:T(8,128)S(1)} %get-tuple-element.49.g_ref.links_ref, ...), custom_call_target="tpu_custom_call" | custom-call | tf_op jit(solution)/shard_map/kernel_mid_up/pallas_call | solution.py:665
  69.0 2.0 %collective-permute-done.37.refs_3_ = f32[6,8,128]{2,1,0:T(8,128)S(1)} collective-permute-done((f32[6,8,128]{2,1,0:T(8,128)S(1)}, f32[6,8,128]{2,1,0:T(8,128)S(1)}, u32[]{:S(2)}, u32[]{:S(2)}) %collective-permute-start.37) | collective-permute-done | bytes 24608 | tf_op jit(solution)/shard_map/ppermute | solution.py:682
  72.3 2.7 %collective-permute-start.42 = (f32[6,8,128]{2,1,0:T(8,128)S(1)}, f32[6,8,128]{2,1,0:T(8,128)S(1)}, u32[]{:S(2)}, u32[]{:S(2)}) collective-permute-start(f32[6,8,128]{2,1,0:T(8,128)S(1)} %get-tuple-element.71), channel_id=1, source_target_pairs={{0,6},{2,4},{4,2},{6,0},{1,7},{3,5},{5,3},{7,1},{8,14},{10,12},{12... | collective-permute-start | bytes 73736 | tf_op jit(solution)/shard_map/ppermute | solution.py:682
  84.6 2.0 %collective-permute-done.47.refs_3_ = f32[6,8,128]{2,1,0:T(8,128)S(1)} collective-permute-done((f32[6,8,128]{2,1,0:T(8,128)S(1)}, f32[6,8,128]{2,1,0:T(8,128)S(1)}, u32[]{:S(2)}, u32[]{:S(2)}) %collective-permute-start.47) | collective-permute-done | bytes 24608 | tf_op jit(solution)/shard_map/ppermute | solution.py:682
  87.9 2.7 %collective-permute-start.54 = (f32[3,8,128]{2,1,0:T(8,128)S(1)}, f32[3,8,128]{2,1,0:T(8,128)S(1)}, u32[]{:S(2)}, u32[]{:S(2)}) collective-permute-start(f32[3,8,128]{2,1,0:T(8,128)S(1)} %get-tuple-element.81.sol_ref.y2_ref), channel_id=1, source_target_pairs={{0,6},{2,4},{4,2},{6,0},{1,7},{3,5},{5,3},{7,1},{8,14},{10,12},{12... | collective-permute-start | bytes 36872 | tf_op jit(solution)/shard_map/ppermute | solution.py:682
  95.3 1.7 %kernel_mid_down.3 = (f32[8,48]{1,0:T(8,128)S(1)}, f32[8,48]{1,0:T(8,128)S(1)}) custom-call(bf16[1728,384]{1,0:T(8,128)(2,1)S(1)} %reshape.26.stencil_ref, bf16[48,3072]{1,0:T(8,128)(2,1)S(1)} %bitcast.27, bf16[96,192]{1,0:T(8,128)(2,1)S(1)} %bitcast.20, f32[3,8,128]{2,1,0:T(8,128)S(1)} %get-tuple-element.80.res_ref, ...), custom_call_target="tpu_custom_call" | custom-call | tf_op jit(solution)/shard_map/kernel_mid_down/pallas_call | solution.py:665
  103.5 2.6 %collective-permute-start.64 = (f32[8,48]{1,0:T(8,128)S(1)}, f32[8,48]{1,0:T(8,128)S(1)}, u32[]{:S(2)}, u32[]{:S(2)}) collective-permute-start(f32[8,48]{1,0:T(8,128)S(1)} %kernel_sweep.9.y3_ref), channel_id=1, source_target_pairs={{0,6},{2,4},{4,2},{6,0},{1,7},{3,5},{5,3},{7,1},{8,14},{10,12},{12... | collective-permute-start | bytes 4616 | tf_op jit(solution)/shard_map/ppermute | solution.py:682
  115.2 1.5 %collective-permute-done.69.refs_3_ = f32[8,48]{1,0:T(8,128)S(1)} collective-permute-done((f32[8,48]{1,0:T(8,128)S(1)}, f32[8,48]{1,0:T(8,128)S(1)}, u32[]{:S(2)}, u32[]{:S(2)}) %collective-permute-start.69) | collective-permute-done | bytes 1568 | tf_op jit(solution)/shard_map/ppermute | solution.py:682
  117.8 2.6 %collective-permute-start.74 = (f32[8,48]{1,0:T(8,128)S(1)}, f32[8,48]{1,0:T(8,128)S(1)}, u32[]{:S(2)}, u32[]{:S(2)}) collective-permute-start(f32[8,48]{1,0:T(8,128)S(1)} %kernel_sweep.11.y3_ref), channel_id=1, source_target_pairs={{0,6},{2,4},{4,2},{6,0},{1,7},{3,5},{5,3},{7,1},{8,14},{10,12},{12... | collective-permute-start | bytes 4616 | tf_op jit(solution)/shard_map/ppermute | solution.py:682
  130.3 1.8 %collective-permute-done.79.refs_3_ = f32[3,8,128]{2,1,0:T(8,128)S(1)} collective-permute-done((f32[3,8,128]{2,1,0:T(8,128)S(1)}, f32[3,8,128]{2,1,0:T(8,128)S(1)}, u32[]{:S(2)}, u32[]{:S(2)}) %collective-permute-start.79) | collective-permute-done | bytes 12320 | tf_op jit(solution)/shard_map/ppermute | solution.py:682
  132.5 2.0 %kernel_mid_up.3 = (f32[6,8,128]{2,1,0:T(8,128)S(1)}, f32[6,8,128]{2,1,0:T(8,128)S(1)}, f32[6,8,128]{2,1,0:T(8,128)S(1)}, f32[6,8,128]{2,1,0:T(8,128)S(1)}, f32[...) custom-call(f32[144,8,128]{2,1,0:T(8,128)S(1)} %get-tuple-element.49.g_ref.links_ref, ...), custom_call_target="tpu_custom_call" | custom-call | tf_op jit(solution)/shard_map/kernel_mid_up/pallas_call | solution.py:665
  134.6 2.7 %collective-permute-start.82 = (f32[6,8,128]{2,1,0:T(8,128)S(1)}, f32[6,8,128]{2,1,0:T(8,128)S(1)}, u32[]{:S(2)}, u32[]{:S(2)}) collective-permute-start(f32[6,8,128]{2,1,0:T(8,128)S(1)} %get-tuple-element.87), channel_id=1, source_target_pairs={{0,6},{2,4},{4,2},{6,0},{1,7},{3,5},{5,3},{7,1},{8,14},{10,12},{12... | collective-permute-start | bytes 73736 | tf_op jit(solution)/shard_map/ppermute | solution.py:682
  (197 shorter events, 95.4 us)
Async XLA Ops:
  4.3 13.0 %collective-permute-start.5 = (bf16[18,16,128]{2,1,0:T(8,128)(2,1)S(1)}, bf16[18,16,128]{2,1,0:T(8,128)(2,1)S(1)}, u32[]{:S(2)}, u32[]{:S(2)}) collective-permute-start(bf16[18,16,128]{2,1,0:T(8,128)(2,1)S(1)} %get-tuple-element.57), channel_id=1, source_target_pairs={{1,0},{0,1},{3,2},{2,3},{5,4},{4,5},{7,6},{6,7},{9,8},{8,9},{11,10... | collective-permute-start | bytes 221192 | tf_op jit(solution)/shard_map/ppermute | solution.py:677
  8.5 5.8 %collective-permute-start.1 = (f32[6,8,128]{2,1,0:T(8,128)S(1)}, f32[6,8,128]{2,1,0:T(8,128)S(1)}, u32[]{:S(2)}, u32[]{:S(2)}) collective-permute-start(f32[6,8,128]{2,1,0:T(8,128)S(1)} %get-tuple-element.54), channel_id=1, source_target_pairs={{0,6},{2,4},{4,2},{6,0},{1,7},{3,5},{5,3},{7,1},{8,14},{10,12},{12... | collective-permute-start | bytes 73736 | tf_op jit(solution)/shard_map/ppermute | solution.py:682
  18.3 6.1 %collective-permute-start.10 = (f32[3,8,128]{2,1,0:T(8,128)S(1)}, f32[3,8,128]{2,1,0:T(8,128)S(1)}, u32[]{:S(2)}, u32[]{:S(2)}) collective-permute-start(f32[3,8,128]{2,1,0:T(8,128)S(1)} %get-tuple-element.59.sol_ref.y2_ref), channel_id=1, source_target_pairs={{0,8},{8,0},{16,24},{24,16},{1,9},{9,1},{17,25},{25,17},{2,10},{10... | collective-permute-start | bytes 36872 | tf_op jit(solution)/shard_map/ppermute | solution.py:682
  18.3 6.0 %collective-permute-start.9 = (f32[3,8,128]{2,1,0:T(8,128)S(1)}, f32[3,8,128]{2,1,0:T(8,128)S(1)}, u32[]{:S(2)}, u32[]{:S(2)}) collective-permute-start(f32[3,8,128]{2,1,0:T(8,128)S(1)} %get-tuple-element.59.sol_ref.y2_ref), channel_id=1, source_target_pairs={{0,6},{2,4},{4,2},{6,0},{1,7},{3,5},{5,3},{7,1},{8,14},{10,12},{12... | collective-permute-start | bytes 36872 | tf_op jit(solution)/shard_map/ppermute | solution.py:682
  19.0 5.4 %collective-permute-start.8 = (f32[3,8,128]{2,1,0:T(8,128)S(1)}, f32[3,8,128]{2,1,0:T(8,128)S(1)}, u32[]{:S(2)}, u32[]{:S(2)}) collective-permute-start(f32[3,8,128]{2,1,0:T(8,128)S(1)} %get-tuple-element.59.sol_ref.y2_ref), channel_id=1, source_target_pairs={{0,2},{2,0},{4,6},{6,4},{1,3},{3,1},{5,7},{7,5},{8,10},{10,8},{12,... | collective-permute-start | bytes 36872 | tf_op jit(solution)/shard_map/ppermute | solution.py:682
  26.1 5.6 %collective-permute-start.15 = (f32[8,48]{1,0:T(8,128)S(1)}, f32[8,48]{1,0:T(8,128)S(1)}, u32[]{:S(2)}, u32[]{:S(2)}) collective-permute-start(f32[8,48]{1,0:T(8,128)S(1)} %get-tuple-element.61.y3_ref), channel_id=1, source_target_pairs={{0,8},{8,0},{16,24},{24,16},{1,9},{9,1},{17,25},{25,17},{2,10},{10... | collective-permute-start | bytes 4616 | tf_op jit(solution)/shard_map/ppermute | solution.py:682
  26.3 5.4 %collective-permute-start.14 = (f32[8,48]{1,0:T(8,128)S(1)}, f32[8,48]{1,0:T(8,128)S(1)}, u32[]{:S(2)}, u32[]{:S(2)}) collective-permute-start(f32[8,48]{1,0:T(8,128)S(1)} %get-tuple-element.61.y3_ref), channel_id=1, source_target_pairs={{0,6},{2,4},{4,2},{6,0},{1,7},{3,5},{5,3},{7,1},{8,14},{10,12},{12... | collective-permute-start | bytes 4616 | tf_op jit(solution)/shard_map/ppermute | solution.py:682
  34.2 5.4 %collective-permute-start.19 = (f32[8,48]{1,0:T(8,128)S(1)}, f32[8,48]{1,0:T(8,128)S(1)}, u32[]{:S(2)}, u32[]{:S(2)}) collective-permute-start(f32[8,48]{1,0:T(8,128)S(1)} %kernel_sweep.6.y3_ref), channel_id=1, source_target_pairs={{0,6},{2,4},{4,2},{6,0},{1,7},{3,5},{5,3},{7,1},{8,14},{10,12},{12... | collective-permute-start | bytes 4616 | tf_op jit(solution)/shard_map/ppermute | solution.py:682
  40.7 5.4 %collective-permute-start.24 = (f32[8,48]{1,0:T(8,128)S(1)}, f32[8,48]{1,0:T(8,128)S(1)}, u32[]{:S(2)}, u32[]{:S(2)}) collective-permute-start(f32[8,48]{1,0:T(8,128)S(1)} %kernel_sweep.7.y3_ref), channel_id=1, source_target_pairs={{0,6},{2,4},{4,2},{6,0},{1,7},{3,5},{5,3},{7,1},{8,14},{10,12},{12... | collective-permute-start | bytes 4616 | tf_op jit(solution)/shard_map/ppermute | solution.py:682
  48.5 5.4 %collective-permute-start.29 = (f32[8,48]{1,0:T(8,128)S(1)}, f32[8,48]{1,0:T(8,128)S(1)}, u32[]{:S(2)}, u32[]{:S(2)}) collective-permute-start(f32[8,48]{1,0:T(8,128)S(1)} %kernel_sweep.8.y3_ref), channel_id=1, source_target_pairs={{0,6},{2,4},{4,2},{6,0},{1,7},{3,5},{5,3},{7,1},{8,14},{10,12},{12... | collective-permute-start | bytes 4616 | tf_op jit(solution)/shard_map/ppermute | solution.py:682
  55.8 5.3 %collective-permute-start.35 = (f32[3,8,128]{2,1,0:T(8,128)S(1)}, f32[3,8,128]{2,1,0:T(8,128)S(1)}, u32[]{:S(2)}, u32[]{:S(2)}) collective-permute-start(f32[3,8,128]{2,1,0:T(8,128)S(1)} %kernel_sweep_up.2.y2_ref), channel_id=1, source_target_pairs={{0,8},{8,0},{16,24},{24,16},{1,9},{9,1},{17,25},{25,17},{2,10},{10... | collective-permute-start | bytes 36872 | tf_op jit(solution)/shard_map/ppermute | solution.py:682
  55.9 5.6 %collective-permute-start.34 = (f32[3,8,128]{2,1,0:T(8,128)S(1)}, f32[3,8,128]{2,1,0:T(8,128)S(1)}, u32[]{:S(2)}, u32[]{:S(2)}) collective-permute-start(f32[3,8,128]{2,1,0:T(8,128)S(1)} %kernel_sweep_up.2.y2_ref), channel_id=1, source_target_pairs={{0,6},{2,4},{4,2},{6,0},{1,7},{3,5},{5,3},{7,1},{8,14},{10,12},{12... | collective-permute-start | bytes 36872 | tf_op jit(solution)/shard_map/ppermute | solution.py:682
  65.1 5.9 %collective-permute-start.37 = (f32[6,8,128]{2,1,0:T(8,128)S(1)}, f32[6,8,128]{2,1,0:T(8,128)S(1)}, u32[]{:S(2)}, u32[]{:S(2)}) collective-permute-start(f32[6,8,128]{2,1,0:T(8,128)S(1)} %get-tuple-element.65), channel_id=1, source_target_pairs={{0,6},{2,4},{4,2},{6,0},{1,7},{3,5},{5,3},{7,1},{8,14},{10,12},{12... | collective-permute-start | bytes 73736 | tf_op jit(solution)/shard_map/ppermute | solution.py:682
  72.3 5.9 %collective-permute-start.42 = (f32[6,8,128]{2,1,0:T(8,128)S(1)}, f32[6,8,128]{2,1,0:T(8,128)S(1)}, u32[]{:S(2)}, u32[]{:S(2)}) collective-permute-start(f32[6,8,128]{2,1,0:T(8,128)S(1)} %get-tuple-element.71), channel_id=1, source_target_pairs={{0,6},{2,4},{4,2},{6,0},{1,7},{3,5},{5,3},{7,1},{8,14},{10,12},{12... | collective-permute-start | bytes 73736 | tf_op jit(solution)/shard_map/ppermute | solution.py:682
  80.7 5.9 %collective-permute-start.47 = (f32[6,8,128]{2,1,0:T(8,128)S(1)}, f32[6,8,128]{2,1,0:T(8,128)S(1)}, u32[]{:S(2)}, u32[]{:S(2)}) collective-permute-start(f32[6,8,128]{2,1,0:T(8,128)S(1)} %get-tuple-element.77), channel_id=1, source_target_pairs={{0,6},{2,4},{4,2},{6,0},{1,7},{3,5},{5,3},{7,1},{8,14},{10,12},{12... | collective-permute-start | bytes 73736 | tf_op jit(solution)/shard_map/ppermute | solution.py:682
  87.9 5.6 %collective-permute-start.54 = (f32[3,8,128]{2,1,0:T(8,128)S(1)}, f32[3,8,128]{2,1,0:T(8,128)S(1)}, u32[]{:S(2)}, u32[]{:S(2)}) collective-permute-start(f32[3,8,128]{2,1,0:T(8,128)S(1)} %get-tuple-element.81.sol_ref.y2_ref), channel_id=1, source_target_pairs={{0,6},{2,4},{4,2},{6,0},{1,7},{3,5},{5,3},{7,1},{8,14},{10,12},{12... | collective-permute-start | bytes 36872 | tf_op jit(solution)/shard_map/ppermute | solution.py:682
  97.0 5.5 %collective-permute-start.59 = (f32[8,48]{1,0:T(8,128)S(1)}, f32[8,48]{1,0:T(8,128)S(1)}, u32[]{:S(2)}, u32[]{:S(2)}) collective-permute-start(f32[8,48]{1,0:T(8,128)S(1)} %get-tuple-element.83.y3_ref), channel_id=1, source_target_pairs={{0,6},{2,4},{4,2},{6,0},{1,7},{3,5},{5,3},{7,1},{8,14},{10,12},{12... | collective-permute-start | bytes 4616 | tf_op jit(solution)/shard_map/ppermute | solution.py:682
  103.5 5.4 %collective-permute-start.64 = (f32[8,48]{1,0:T(8,128)S(1)}, f32[8,48]{1,0:T(8,128)S(1)}, u32[]{:S(2)}, u32[]{:S(2)}) collective-permute-start(f32[8,48]{1,0:T(8,128)S(1)} %kernel_sweep.9.y3_ref), channel_id=1, source_target_pairs={{0,6},{2,4},{4,2},{6,0},{1,7},{3,5},{5,3},{7,1},{8,14},{10,12},{12... | collective-permute-start | bytes 4616 | tf_op jit(solution)/shard_map/ppermute | solution.py:682
  111.3 5.4 %collective-permute-start.69 = (f32[8,48]{1,0:T(8,128)S(1)}, f32[8,48]{1,0:T(8,128)S(1)}, u32[]{:S(2)}, u32[]{:S(2)}) collective-permute-start(f32[8,48]{1,0:T(8,128)S(1)} %kernel_sweep.10.y3_ref), channel_id=1, source_target_pairs={{0,6},{2,4},{4,2},{6,0},{1,7},{3,5},{5,3},{7,1},{8,14},{10,12},{12... | collective-permute-start | bytes 4616 | tf_op jit(solution)/shard_map/ppermute | solution.py:682
  117.8 5.4 %collective-permute-start.74 = (f32[8,48]{1,0:T(8,128)S(1)}, f32[8,48]{1,0:T(8,128)S(1)}, u32[]{:S(2)}, u32[]{:S(2)}) collective-permute-start(f32[8,48]{1,0:T(8,128)S(1)} %kernel_sweep.11.y3_ref), channel_id=1, source_target_pairs={{0,6},{2,4},{4,2},{6,0},{1,7},{3,5},{5,3},{7,1},{8,14},{10,12},{12... | collective-permute-start | bytes 4616 | tf_op jit(solution)/shard_map/ppermute | solution.py:682
  126.4 5.7 %collective-permute-start.79 = (f32[3,8,128]{2,1,0:T(8,128)S(1)}, f32[3,8,128]{2,1,0:T(8,128)S(1)}, u32[]{:S(2)}, u32[]{:S(2)}) collective-permute-start(f32[3,8,128]{2,1,0:T(8,128)S(1)} %kernel_sweep_up.3.y2_ref), channel_id=1, source_target_pairs={{0,6},{2,4},{4,2},{6,0},{1,7},{3,5},{5,3},{7,1},{8,14},{10,12},{12... | collective-permute-start | bytes 36872 | tf_op jit(solution)/shard_map/ppermute | solution.py:682
  134.5 5.3 %collective-permute-start.81 = (f32[6,8,128]{2,1,0:T(8,128)S(1)}, f32[6,8,128]{2,1,0:T(8,128)S(1)}, u32[]{:S(2)}, u32[]{:S(2)}) collective-permute-start(f32[6,8,128]{2,1,0:T(8,128)S(1)} %get-tuple-element.86), channel_id=1, source_target_pairs={{0,8},{8,0},{16,24},{24,16},{1,9},{9,1},{17,25},{25,17},{2,10},{10... | collective-permute-start | bytes 73736 | tf_op jit(solution)/shard_map/ppermute | solution.py:682
  134.6 5.9 %collective-permute-start.82 = (f32[6,8,128]{2,1,0:T(8,128)S(1)}, f32[6,8,128]{2,1,0:T(8,128)S(1)}, u32[]{:S(2)}, u32[]{:S(2)}) collective-permute-start(f32[6,8,128]{2,1,0:T(8,128)S(1)} %get-tuple-element.87), channel_id=1, source_target_pairs={{0,6},{2,4},{4,2},{6,0},{1,7},{3,5},{5,3},{7,1},{8,14},{10,12},{12... | collective-permute-start | bytes 73736 | tf_op jit(solution)/shard_map/ppermute | solution.py:682
  143.1 5.9 %collective-permute-start.87 = (f32[6,8,128]{2,1,0:T(8,128)S(1)}, f32[6,8,128]{2,1,0:T(8,128)S(1)}, u32[]{:S(2)}, u32[]{:S(2)}) collective-permute-start(f32[6,8,128]{2,1,0:T(8,128)S(1)} %get-tuple-element.93), channel_id=1, source_target_pairs={{0,6},{2,4},{4,2},{6,0},{1,7},{3,5},{5,3},{7,1},{8,14},{10,12},{12... | collective-permute-start | bytes 73736 | tf_op jit(solution)/shard_map/ppermute | solution.py:682
  (74 other events, 316.3 us)

commit v3 on v2

--- a/solution.py
+++ b/solution.py
@@ -127,25 +127,29 @@
     return [x - y for x, y in zip(xs, ys)]
 
 
-def fine_send(site, links_ref, field, acc_ref):
+def fine_send(site, links_ref, field):
+    sent = []
+    for direction in range(2):
+        near, far = backward(site, links_ref, field, direction)
+        first = site.first(direction)
+        sent.append([jnp.where(first, n, f) for n, f in zip(near, far)])
+    return sent
+
+
+def fine_own(site, links_ref, field):
     acc = list(field)
     for kind, reach in ((0, 1), (1, 3)):
         acc = add(acc, link_apply(links_ref, 3, kind, [shift_y(site, x, reach) for x in field]))
         back = link_adjoint(links_ref, 3, kind, field)
         acc = sub(acc, [shift_y(site, x, -reach) for x in back])
-    sent = []
     for direction in range(3):
         near, far = backward(site, links_ref, field, direction)
         first, last = site.first(direction), site.last(direction)
-        if direction < 2:
-            sent.append([jnp.where(first, n, f) for n, f in zip(near, far)])
         acc = [
             a - jnp.where(first, 0.0, n) - jnp.where(last, cyclic(site, f, direction, 1), 0.0)
             for a, n, f in zip(acc, near, far)
         ]
-    for i in range(6):
-        acc_ref[i] = acc[i]
-    return sent
+    return acc
 
 
 class PairedLinks:
@@ -263,16 +267,19 @@
     return mid_gather(site, [(ref, 0, x_re, x_im)])
 
 
-def mid_stencil_apply(site, ref, v, ahead, behind):
-    shifted = [v]
+def mid_stencil_own(site, ref, v):
+    shifted = ((0, v), (7, [by_roll(site, x, 0, 1) for x in v]), (8, [by_roll(site, x, 0, -1) for x in v]))
+    return mid_gather(site, [(ref, 24 * k) + mid_x(site, s) for k, s in shifted])
+
+
+def mid_stencil_near(site, ref, v, ahead, behind):
+    shifted = []
     for direction in range(3):
         d = ROW_BITS[direction]
         bit = site.row_bit(d)
         shifted.append([flip_row(site, jnp.where(bit, x, n), d) for x, n in zip(v, ahead[direction])])
         shifted.append([flip_row(site, jnp.where(bit, n, x), d) for x, n in zip(v, behind[direction])])
-    shifted.append([by_roll(site, x, 0, 1) for x in v])
-    shifted.append([by_roll(site, x, 0, -1) for x in v])
-    return mid_gather(site, [(ref, 24 * k) + mid_x(site, s) for k, s in enumerate(shifted)])
+    return mid_gather(site, [(ref, 24 * k + 24) + mid_x(site, s) for k, s in enumerate(shifted)])
 
 
 def spread(site, v, ref):
@@ -435,14 +442,19 @@
     return out
 
 
-def coarse_stencil_apply(ref, v, ahead, behind):
+def coarse_stencil_own(ref, v):
     y = iota2((8, 48), 0) & 3
-    shifted = [v]
+    up_y = jnp.where(y == 3, up(v, -3), up(v, 1))
+    down_y = jnp.where(y == 0, up(v, 3), up(v, -1))
+    return coarse_matrix([(ref, 0, v), (ref, 96 * 7, up_y), (ref, 96 * 8, down_y)])
+
+
+def coarse_stencil_near(ref, ahead, behind):
+    terms = []
     for direction in range(3):
-        shifted += [ahead[direction], behind[direction]]
-    shifted.append(jnp.where(y == 3, up(v, -3), up(v, 1)))
-    shifted.append(jnp.where(y == 0, up(v, 3), up(v, -1)))
-    return coarse_matrix([(ref, 96 * k, s) for k, s in enumerate(shifted)])
+        terms.append((ref, 96 * (2 * direction + 1), ahead[direction]))
+        terms.append((ref, 96 * (2 * direction + 2), behind[direction]))
+    return coarse_matrix(terms)
 
 
 def load(ref, n, base=0):
@@ -458,9 +470,9 @@
     return lax.rem(lax.axis_index(axis), 2) == 1
 
 
-def finish_fine(site, links_ref, solution, sol_ref, acc_ref, z0_ref, z1_ref, t0_ref, t1_ref):
+def finish_fine(site, links_ref, solution, sol_ref, z0_ref, z1_ref, t0_ref, t1_ref):
     store(sol_ref, solution)
-    back_t, back_z = fine_send(site, links_ref, solution, acc_ref)
+    back_t, back_z = fine_send(site, links_ref, solution)
     for axis, back, ref0, ref1 in (("gz", back_z, z0_ref, z1_ref), ("ta", back_t, t0_ref, t1_ref)):
         odd = is_odd(axis)
         store(ref0, [jnp.where(odd, s, b) for s, b in zip(solution, back)])
@@ -573,7 +585,7 @@
                     out_ref[p, c, t, z] = value[16 * t + 4 * z : 16 * t + 4 * z + 4]
 
 
-def kernel_links(block_ref, links_ref, g_ref, gx_ref):
+def kernel_links(links_ref, g_ref, gx_ref):
     prepare_links(Site(), links_ref, g_ref, gx_ref)
 
 
@@ -596,6 +608,10 @@
     site = Site()
     _, applied = begin_fine(site, links_ref, refs[:8])
     scatter_fine(site, sub(load(rhs_ref, 6), applied), refs[8])
+
+
+def kernel_own(links_ref, field_ref, acc_ref):
+    store(acc_ref, fine_own(Site(), links_ref, load(field_ref, 6)))
 
 
 def kernel_scatter(field_ref, out_ref):
@@ -618,58 +634,70 @@
     return [ahead_t, ahead_z, get(nx)], [behind_t, behind_z, get(nx)]
 
 
-def kernel_mid_down(stencil_ref, near_ref, jacobi_ref, res_ref, sol_ref, *refs):
+def kernel_mid_own(stencil_ref, v_ref, out_ref):
+    site = Site()
+    store(out_ref, mid_stencil_own(site, stencil_ref, load(v_ref, 3)))
+
+
+def mid_rest(site, stencil_ref, res_ref, y2_ref, own_ref, around):
+    ahead, behind = neighbours(around, lambda r: load(r, 3))
+    applied = mid_stencil_near(site, stencil_ref, load(y2_ref, 3), ahead, behind)
+    return sub(load(res_ref, 3), add(load(own_ref, 3), applied))
+
+
+def kernel_mid_down(stencil_ref, near_ref, jacobi_ref, res_ref, y2_ref, own_ref, *refs):
     site = Site()
     around, (r3_ref, y3_ref, tile_ref) = refs[:-3], refs[-3:]
-    ahead, behind = neighbours(around, lambda r: load(r, 3))
-    applied = mid_stencil_apply(site, stencil_ref, load(sol_ref, 3), ahead, behind)
-    r3 = restrict_mid(site, near_ref, sub(load(res_ref, 3), applied), tile_ref)
+    rest = mid_rest(site, stencil_ref, res_ref, y2_ref, own_ref, around)
+    r3 = restrict_mid(site, near_ref, rest, tile_ref)
     r3_ref[...] = r3
     y3_ref[...] = coarse_matrix([(jacobi_ref, 0, r3)])
 
 
-def sweep(stencil_ref, jacobi_ref, r3_ref, y3_ref, around):
+def kernel_sweep_own(stencil_ref, r3_ref, y3_ref, out_ref):
+    out_ref[...] = r3_ref[...] - coarse_stencil_own(stencil_ref, y3_ref[...])
+
+
+def sweep(stencil_ref, jacobi_ref, own_ref, y3_ref, around):
     ahead, behind = neighbours(around, lambda r: [r[...]])
     ahead, behind = [x[0] for x in ahead], [x[0] for x in behind]
-    y3 = y3_ref[...]
-    rest = r3_ref[...] - coarse_stencil_apply(stencil_ref, y3, ahead, behind)
-    return y3 + coarse_matrix([(jacobi_ref, 0, rest)])
-
-
-def kernel_sweep(stencil_ref, jacobi_ref, r3_ref, y3_ref, *refs):
-    refs[-1][...] = sweep(stencil_ref, jacobi_ref, r3_ref, y3_ref, refs[:-1])
-
-
-def kernel_sweep_up(stencil_ref, jacobi_ref, near_ref, y2_ref, r3_ref, y3_ref, *refs):
+    rest = own_ref[...] - coarse_stencil_near(stencil_ref, ahead, behind)
+    return y3_ref[...] + coarse_matrix([(jacobi_ref, 0, rest)])
+
+
+def kernel_sweep(stencil_ref, jacobi_ref, own_ref, y3_ref, *refs):
+    refs[-1][...] = sweep(stencil_ref, jacobi_ref, own_ref, y3_ref, refs[:-1])
+
+
+def kernel_sweep_up(stencil_ref, jacobi_ref, near_ref, y2_ref, own_ref, y3_ref, *refs):
     site = Site()
     around, (out_ref, row_ref) = refs[:-2], refs[-2:]
-    y3 = sweep(stencil_ref, jacobi_ref, r3_ref, y3_ref, around)
+    y3 = sweep(stencil_ref, jacobi_ref, own_ref, y3_ref, around)
     store(out_ref, add(load(y2_ref, 3), prolong_mid(site, near_ref, y3, row_ref)))
 
 
-def kernel_mid_up(links_ref, stencil_ref, jacobi_ref, near_ref, old_ref, res_ref, y2_ref, *refs):
+def kernel_mid_up(links_ref, stencil_ref, jacobi_ref, near_ref, old_ref, res_ref, y2_ref, own_ref, *refs):
     site = Site()
-    around, outs, spread_ref = refs[:-7], refs[-7:-1], refs[-1]
-    ahead, behind = neighbours(around, lambda r: load(r, 3))
-    y2 = load(y2_ref, 3)
-    rest = sub(load(res_ref, 3), mid_stencil_apply(site, stencil_ref, y2, ahead, behind))
-    y2 = add(y2, mid_matrix(site, jacobi_ref, rest))
+    around, outs, spread_ref = refs[:-6], refs[-6:-1], refs[-1]
+    rest = mid_rest(site, stencil_ref, res_ref, y2_ref, own_ref, around)
+    y2 = add(load(y2_ref, 3), mid_matrix(site, jacobi_ref, rest))
     solution = add(load(old_ref, 6), prolong_fine(site, near_ref, y2, spread_ref))
     finish_fine(site, links_ref, solution, *outs)
 
 
-def call(kernel, outs, scratch, *args, first_any=False):
-    specs = [pl.BlockSpec(memory_space=pltpu.VMEM)] * len(args)
-    if first_any:
-        specs[0] = pl.BlockSpec(memory_space=pl.ANY)
+def call(kernel, outs, scratch, *args, after=()):
+    def body(*refs):
+        kernel(*refs[len(after) :])
+
+    specs = [pl.BlockSpec(memory_space=pl.ANY)] * len(after)
     return pl.pallas_call(
-        kernel,
+        body,
         out_shape=[jax.ShapeDtypeStruct(*s) if s[1] == BF16 else jax.ShapeDtypeStruct(s, F32) for s in outs],
-        in_specs=specs,
+        in_specs=specs + [pl.BlockSpec(memory_space=pltpu.VMEM)] * len(args),
         scratch_shapes=[pltpu.VMEM(s, F32) for s in scratch],
         compiler_params=pltpu.CompilerParams(vmem_limit_bytes=VMEM_BYTES),
         name=kernel.__name__,
-    )(*args)
+    )(*after, *args)
 
 
 def from_behind(block, axis, distance):
@@ -687,20 +715,22 @@
     t1 = swap(v, "ta", 1)
     z0 = swap(v, "gz", 0)
     z1 = swap(v, "gz", 1)
-    return [x, t1, z0, z1, swap(v, "ta", 0)]
-
-
-def exchange_fine(gx, sol, acc, z0, z1, t0, t1):
+    t0 = swap(v, "ta", 0)
+    return [x, t1, z0, z1, t0]
+
+
+def exchange_fine(g, gx, sol, z0, z1, t0, t1):
     x = from_behind(sol, "xy", 1)
     t1 = swap(t1, "ta", 1)
     z0 = swap(z0, "gz", 0)
     z1 = swap(z1, "gz", 1)
     t0 = swap(t0, "ta", 0)
+    (acc,) = call(kernel_own, [TILE6], [], g, sol)
     return [sol, acc, t0, z1, z0, t1, x, gx]
 
 
 TILE6 = (6, 8, 128)
-FINE_OUT = [TILE6] * 6
+FINE_OUT = [TILE6] * 5
 
 
 def local(
@@ -724,26 +754,46 @@
     mid = (3, 8, 128)
     coarse = (8, 48)
 
-    g, gx = call(kernel_links, [(144, 8, 128), ((18, 16, 128), BF16)], [], block, links, first_any=True)
+    g, gx = call(kernel_links, [(144, 8, 128), ((18, 16, 128), BF16)], [], links, after=(block,))
     gx = from_behind(gx, "xy", 1)
     rhs, *state = call(kernel_first, [TILE6] + FINE_OUT, [], g, block, right_side)
     for cycle_no in range(CYCLES):
-        r2, y2 = call(kernel_restrict, [mid, mid], [], g, near1, jacobi2, rhs, *exchange_fine(gx, *state))
+        around = exchange_fine(g, gx, *state)
+        r2, y2 = call(kernel_restrict, [mid, mid], [], g, near1, jacobi2, rhs, *around)
+        around = exchange(y2)
+        (own,) = call(kernel_mid_own, [mid], [], stencil2, y2)
         r3, y3 = call(
-            kernel_mid_down, [coarse, coarse], [(2, 48, 128)], stencil2, near2, jacobi3, r2, y2, *exchange(y2)
+            kernel_mid_down, [coarse, coarse], [(2, 48, 128)], stencil2, near2, jacobi3, r2, y2, own, *around
         )
         for _ in range(SWEEPS - 1):
-            (y3,) = call(kernel_sweep, [coarse], [], stencil3, jacobi3, r3, y3, *exchange(y3))
+            around = exchange(y3)
+            (own,) = call(kernel_sweep_own, [coarse], [], stencil3, r3, y3)
+            (y3,) = call(kernel_sweep, [coarse], [], stencil3, jacobi3, own, y3, *around)
+        around = exchange(y3)
+        (own,) = call(kernel_sweep_own, [coarse], [], stencil3, r3, y3)
         (y2,) = call(
-            kernel_sweep_up, [mid], [(2, 48, 128)], stencil3, jacobi3, near2, y2, r3, y3, *exchange(y3)
+            kernel_sweep_up, [mid], [(2, 48, 128)], stencil3, jacobi3, near2, y2, own, y3, *around
         )
+        around = exchange(y2)
+        (own,) = call(kernel_mid_own, [mid], [], stencil2, y2)
         state = call(
-            kernel_mid_up, FINE_OUT, [(48, 8, 128)], g, stencil2, jacobi2, near1, state[0], r2, y2, *exchange(y2)
+            kernel_mid_up,
+            FINE_OUT,
+            [(48, 8, 128)],
+            g,
+            stencil2,
+            jacobi2,
+            near1,
+            state[0],
+            r2,
+            y2,
+            own,
+            *around,
         )
-        state = call(kernel_smooth, FINE_OUT, [], g, block, rhs, *exchange_fine(gx, *state))
+        state = call(kernel_smooth, FINE_OUT, [], g, block, rhs, *exchange_fine(g, gx, *state))
         if cycle_no < CYCLES - 1:
-            state = call(kernel_smooth, FINE_OUT, [], g, block, rhs, *exchange_fine(gx, *state))
-    around = exchange_fine(gx, *state)
+            state = call(kernel_smooth, FINE_OUT, [], g, block, rhs, *exchange_fine(g, gx, *state))
+    around = exchange_fine(g, gx, *state)
     (solution,) = call(kernel_scatter, [right_side.shape], [], state[0])
     (residual,) = call(kernel_last, [right_side.shape], [], g, rhs, *around)
     return solution, residual

time: 151 us -> 150 us (level)
  waiting for transfers between devices: 37.2 us -> 32.6 us
  Pallas kernels: 22 us -> 25.3 us
    ppermute x72, waiting for transfers between devices: 23.9 us -> 19.3 us  [swap(): lax.ppermute(block, axis, [(i, ((i + phase ^ 1) - phase) % n) for i in ra...]
    pallas_call x21 -> x39, Pallas kernels: 22 us -> 25.3 us  [call(): pl.pallas_call(body, out_shape=[jax.ShapeDtypeStruct(*s) if s[1] == BF16...]
  transfers between devices with their start and end apart: 91 -> 91, of which waited for: 43 -> 36; matrix products, arithmetic and copies ran while one was open for 2% -> 2% of each run, Pallas kernels for 1% -> 5%
where the time goes in v3:
time: 150 us
  starting transfers between devices  84.8 us (57%)
  waiting for transfers between devices  32.6 us (22%)
  Pallas kernels  25.3 us (17%)
  local copies, waits for them, and re-layouts  6.06 us (4%)
    ppermute x72, starting transfers between devices, swap(): lax.ppermute(block, axis, [(i, ((i + phase ^ 1) - phase) % n) for i in ra...  56.8 us
    ppermute x19, starting transfers between devices, from_behind(): lax.ppermute(block, axis, [((i - distance) % n, i) for i in range(n)])  27.9 us
    pallas_call x39, Pallas kernels, call(): pl.pallas_call(body, out_shape=[jax.ShapeDtypeStruct(*s) if s[1] == BF16...  25.3 us
    ppermute x72, waiting for transfers between devices, swap(): lax.ppermute(block, axis, [(i, ((i + phase ^ 1) - phase) % n) for i in ra...  19.3 us
    ppermute x19, waiting for transfers between devices, from_behind(): lax.ppermute(block, axis, [((i - distance) % n, i) for i in range(n)])  13.3 us
    reshape x1, local copies, waits for them, and re-layouts, local(): stencil2 = mid_stencil.reshape(1728, 384)  3.4 us
  transfers between devices with their start and end apart: 91, of which 36 were waited for; matrix products, arithmetic and copies ran while one was open for 2% of the time, Pallas kernels for 5%

profile of v3, /device:TPU:0, one launch (start us, length us, event | category | flops | bytes accessed | tf_op | source)
XLA Modules:
  0.0 149.8 jit_solution(14507913956770291010)
XLA Ops:
  0.6 2.0 %reshape.25.refs_0_.refs_1_ = bf16[384,768]{1,0:T(8,128)(2,1)S(1)} reshape(bf16[48,2,2,2,768]{4,3,2,1,0:T(2,128)(2,1)} %param.11) | data formatting | bytes 1179648 | tf_op jit(solution)/shard_map/reshape | solution.py:747
  2.7 1.6 %kernel_links.1 = (f32[144,8,128]{2,1,0:T(8,128)S(1)}, bf16[18,16,128]{2,1,0:T(8,128)(2,1)S(1)}) custom-call(bf16[384,768]{1,0:T(8,128)(2,1)S(1)} %reshape.25.refs_0_.refs_1_, bf16[3,3,4,4,4,256]{5,4,3,2,1,0:T(4,128)(2,1)S(1)} %copy-done.3), custom_call_target="tpu_custom_call" | custom-call | tf_op jit(solution)/shard_map/kernel_links/pallas_call | solution.py:693
  4.3 3.0 %collective-permute-start.5 = (bf16[18,16,128]{2,1,0:T(8,128)(2,1)S(1)}, bf16[18,16,128]{2,1,0:T(8,128)(2,1)S(1)}, u32[]{:S(2)}, u32[]{:S(2)}) collective-permute-start(bf16[18,16,128]{2,1,0:T(8,128)(2,1)S(1)} %get-tuple-element.50), channel_id=1, source_target_pairs={{1,0},{0,1},{3,2},{2,3},{5,4},{4,5},{7,6},{6,7},{9,8},{8,9},{11,10... | collective-permute-start | bytes 221192 | tf_op jit(solution)/shard_map/ppermute | solution.py:705
  8.4 3.7 %collective-permute-start.1 = (f32[6,8,128]{2,1,0:T(8,128)S(1)}, f32[6,8,128]{2,1,0:T(8,128)S(1)}, u32[]{:S(2)}, u32[]{:S(2)}) collective-permute-start(f32[6,8,128]{2,1,0:T(8,128)S(1)} %get-tuple-element.47), channel_id=1, source_target_pairs={{0,6},{2,4},{4,2},{6,0},{1,7},{3,5},{5,3},{7,1},{8,14},{10,12},{12... | collective-permute-start | bytes 73736 | tf_op jit(solution)/shard_map/ppermute | solution.py:710
  14.4 1.6 %collective-permute-done.2.refs_8_ = f32[6,8,128]{2,1,0:T(8,128)S(1)} collective-permute-done((f32[6,8,128]{2,1,0:T(8,128)S(1)}, f32[6,8,128]{2,1,0:T(8,128)S(1)}, u32[]{:S(2)}, u32[]{:S(2)}) %collective-permute-start.2) | collective-permute-done | bytes 24608 | tf_op jit(solution)/shard_map/ppermute | solution.py:710
  20.8 3.4 %reshape.26.refs_0_.refs_1_ = bf16[1728,384]{1,0:T(8,128)(2,1)S(1)} reshape(bf16[9,24,2,2,2,384]{5,4,3,2,1,0:T(2,128)(2,1)} %param.13) | data formatting | bytes 2654208 | tf_op jit(solution)/shard_map/reshape | solution.py:749
  26.9 2.8 %collective-permute-start.14 = (f32[8,48]{1,0:T(8,128)S(1)}, f32[8,48]{1,0:T(8,128)S(1)}, u32[]{:S(2)}, u32[]{:S(2)}) collective-permute-start(f32[8,48]{1,0:T(8,128)S(1)} %get-tuple-element.54.refs_2_.refs_3_), channel_id=1, source_target_pairs={{0,6},{2,4},{4,2},{6,0},{1,7},{3,5},{5,3},{7,1},{8,14},{10,12},{12... | collective-permute-start | bytes 4616 | tf_op jit(solution)/shard_map/ppermute | solution.py:710
  37.2 1.5 %collective-permute-start.16 = (f32[8,48]{1,0:T(8,128)S(1)}, f32[8,48]{1,0:T(8,128)S(1)}, u32[]{:S(2)}, u32[]{:S(2)}) collective-permute-start(f32[8,48]{1,0:T(8,128)S(1)} %kernel_sweep.6.refs_2_.refs_3_), channel_id=1, source_target_pairs={{1,0},{0,1},{3,2},{2,3},{5,4},{4,5},{7,6},{6,7},{9,8},{8,9},{11,10... | collective-permute-start | bytes 4616 | tf_op jit(solution)/shard_map/ppermute | solution.py:705
  41.3 2.6 %collective-permute-start.24 = (f32[8,48]{1,0:T(8,128)S(1)}, f32[8,48]{1,0:T(8,128)S(1)}, u32[]{:S(2)}, u32[]{:S(2)}) collective-permute-start(f32[8,48]{1,0:T(8,128)S(1)} %kernel_sweep.7.refs_2_.refs_3_), channel_id=1, source_target_pairs={{0,6},{2,4},{4,2},{6,0},{1,7},{3,5},{5,3},{7,1},{8,14},{10,12},{12... | collective-permute-start | bytes 4616 | tf_op jit(solution)/shard_map/ppermute | solution.py:710
  51.5 1.5 collective-permute-start.26
  56.4 2.7 %collective-permute-start.34 = (f32[3,8,128]{2,1,0:T(8,128)S(1)}, f32[3,8,128]{2,1,0:T(8,128)S(1)}, u32[]{:S(2)}, u32[]{:S(2)}) collective-permute-start(f32[3,8,128]{2,1,0:T(8,128)S(1)} %kernel_sweep_up.2.refs_1_.refs_6_), channel_id=1, source_target_pairs={{0,6},{2,4},{4,2},{6,0},{1,7},{3,5},{5,3},{7,1},{8,14},{10,12},{12... | collective-permute-start | bytes 36872 | tf_op jit(solution)/shard_map/ppermute | solution.py:710
  67.7 1.5 collective-permute-start.40
  69.4 1.8 %collective-permute-done.37.refs_6_ = f32[6,8,128]{2,1,0:T(8,128)S(1)} collective-permute-done((f32[6,8,128]{2,1,0:T(8,128)S(1)}, f32[6,8,128]{2,1,0:T(8,128)S(1)}, u32[]{:S(2)}, u32[]{:S(2)}) %collective-permute-start.37) | collective-permute-done | bytes 24608 | tf_op jit(solution)/shard_map/ppermute | solution.py:710
  72.3 2.7 %collective-permute-start.42 = (f32[6,8,128]{2,1,0:T(8,128)S(1)}, f32[6,8,128]{2,1,0:T(8,128)S(1)}, u32[]{:S(2)}, u32[]{:S(2)}) collective-permute-start(f32[6,8,128]{2,1,0:T(8,128)S(1)} %get-tuple-element.62), channel_id=1, source_target_pairs={{0,6},{2,4},{4,2},{6,0},{1,7},{3,5},{5,3},{7,1},{8,14},{10,12},{12... | collective-permute-start | bytes 73736 | tf_op jit(solution)/shard_map/ppermute | solution.py:710
  83.1 1.5 collective-permute-start.50
  84.8 1.8 %collective-permute-done.47.refs_7_ = f32[6,8,128]{2,1,0:T(8,128)S(1)} collective-permute-done((f32[6,8,128]{2,1,0:T(8,128)S(1)}, f32[6,8,128]{2,1,0:T(8,128)S(1)}, u32[]{:S(2)}, u32[]{:S(2)}) %collective-permute-start.47) | collective-permute-done | bytes 24608 | tf_op jit(solution)/shard_map/ppermute | solution.py:710
  87.9 2.7 %collective-permute-start.54 = (f32[3,8,128]{2,1,0:T(8,128)S(1)}, f32[3,8,128]{2,1,0:T(8,128)S(1)}, u32[]{:S(2)}, u32[]{:S(2)}) collective-permute-start(f32[3,8,128]{2,1,0:T(8,128)S(1)} %get-tuple-element.71.refs_1_.refs_4_.refs_3_), channel_id=1, source_target_pairs={{0,6},{2,4},{4,2},{6,0},{1,7},{3,5},{5,3},{7,1},{8,14},{10,12},{12... | collective-permute-start | bytes 36872 | tf_op jit(solution)/shard_map/ppermute | solution.py:710
  99.2 1.5 collective-permute-start.56
  103.3 2.6 %collective-permute-start.64 = (f32[8,48]{1,0:T(8,128)S(1)}, f32[8,48]{1,0:T(8,128)S(1)}, u32[]{:S(2)}, u32[]{:S(2)}) collective-permute-start(f32[8,48]{1,0:T(8,128)S(1)} %kernel_sweep.9.refs_2_.refs_3_), channel_id=1, source_target_pairs={{0,6},{2,4},{4,2},{6,0},{1,7},{3,5},{5,3},{7,1},{8,14},{10,12},{12... | collective-permute-start | bytes 4616 | tf_op jit(solution)/shard_map/ppermute | solution.py:710
  113.4 1.5 collective-permute-start.66
  117.5 2.6 %collective-permute-start.74 = (f32[8,48]{1,0:T(8,128)S(1)}, f32[8,48]{1,0:T(8,128)S(1)}, u32[]{:S(2)}, u32[]{:S(2)}) collective-permute-start(f32[8,48]{1,0:T(8,128)S(1)} %kernel_sweep.11.refs_2_.refs_5_), channel_id=1, source_target_pairs={{0,6},{2,4},{4,2},{6,0},{1,7},{3,5},{5,3},{7,1},{8,14},{10,12},{12... | collective-permute-start | bytes 4616 | tf_op jit(solution)/shard_map/ppermute | solution.py:710
  128.7 1.5 collective-permute-start.76
  134.0 2.7 %collective-permute-start.82 = (f32[6,8,128]{2,1,0:T(8,128)S(1)}, f32[6,8,128]{2,1,0:T(8,128)S(1)}, u32[]{:S(2)}, u32[]{:S(2)}) collective-permute-start(f32[6,8,128]{2,1,0:T(8,128)S(1)} %get-tuple-element.76), channel_id=1, source_target_pairs={{0,6},{2,4},{4,2},{6,0},{1,7},{3,5},{5,3},{7,1},{8,14},{10,12},{12... | collective-permute-start | bytes 73736 | tf_op jit(solution)/shard_map/ppermute | solution.py:710
  144.7 1.5 collective-permute-start.90
  (215 shorter events, 96.6 us)
Async XLA Ops:
  4.3 12.9 %collective-permute-start.5 = (bf16[18,16,128]{2,1,0:T(8,128)(2,1)S(1)}, bf16[18,16,128]{2,1,0:T(8,128)(2,1)S(1)}, u32[]{:S(2)}, u32[]{:S(2)}) collective-permute-start(bf16[18,16,128]{2,1,0:T(8,128)(2,1)S(1)} %get-tuple-element.50), channel_id=1, source_target_pairs={{1,0},{0,1},{3,2},{2,3},{5,4},{4,5},{7,6},{6,7},{9,8},{8,9},{11,10... | collective-permute-start | bytes 221192 | tf_op jit(solution)/shard_map/ppermute | solution.py:705
  8.4 5.9 %collective-permute-start.1 = (f32[6,8,128]{2,1,0:T(8,128)S(1)}, f32[6,8,128]{2,1,0:T(8,128)S(1)}, u32[]{:S(2)}, u32[]{:S(2)}) collective-permute-start(f32[6,8,128]{2,1,0:T(8,128)S(1)} %get-tuple-element.47), channel_id=1, source_target_pairs={{0,6},{2,4},{4,2},{6,0},{1,7},{3,5},{5,3},{7,1},{8,14},{10,12},{12... | collective-permute-start | bytes 73736 | tf_op jit(solution)/shard_map/ppermute | solution.py:710
  18.2 6.6 %collective-permute-start.10 = (f32[3,8,128]{2,1,0:T(8,128)S(1)}, f32[3,8,128]{2,1,0:T(8,128)S(1)}, u32[]{:S(2)}, u32[]{:S(2)}) collective-permute-start(f32[3,8,128]{2,1,0:T(8,128)S(1)} %get-tuple-element.52.refs_1_.refs_4_.refs_3_), channel_id=1, source_target_pairs={{0,8},{8,0},{16,24},{24,16},{1,9},{9,1},{17,25},{25,17},{2,10},{10... | collective-permute-start | bytes 36872 | tf_op jit(solution)/shard_map/ppermute | solution.py:710
  18.2 6.6 %collective-permute-start.9 = (f32[3,8,128]{2,1,0:T(8,128)S(1)}, f32[3,8,128]{2,1,0:T(8,128)S(1)}, u32[]{:S(2)}, u32[]{:S(2)}) collective-permute-start(f32[3,8,128]{2,1,0:T(8,128)S(1)} %get-tuple-element.52.refs_1_.refs_4_.refs_3_), channel_id=1, source_target_pairs={{0,6},{2,4},{4,2},{6,0},{1,7},{3,5},{5,3},{7,1},{8,14},{10,12},{12... | collective-permute-start | bytes 36872 | tf_op jit(solution)/shard_map/ppermute | solution.py:710
  18.8 5.9 %collective-permute-start.8 = (f32[3,8,128]{2,1,0:T(8,128)S(1)}, f32[3,8,128]{2,1,0:T(8,128)S(1)}, u32[]{:S(2)}, u32[]{:S(2)}) collective-permute-start(f32[3,8,128]{2,1,0:T(8,128)S(1)} %get-tuple-element.52.refs_1_.refs_4_.refs_3_), channel_id=1, source_target_pairs={{0,2},{2,0},{4,6},{6,4},{1,3},{3,1},{5,7},{7,5},{8,10},{10,8},{12,... | collective-permute-start | bytes 36872 | tf_op jit(solution)/shard_map/ppermute | solution.py:710
  26.7 5.7 %collective-permute-start.15 = (f32[8,48]{1,0:T(8,128)S(1)}, f32[8,48]{1,0:T(8,128)S(1)}, u32[]{:S(2)}, u32[]{:S(2)}) collective-permute-start(f32[8,48]{1,0:T(8,128)S(1)} %get-tuple-element.54.refs_2_.refs_3_), channel_id=1, source_target_pairs={{0,8},{8,0},{16,24},{24,16},{1,9},{9,1},{17,25},{25,17},{2,10},{10... | collective-permute-start | bytes 4616 | tf_op jit(solution)/shard_map/ppermute | solution.py:710
  26.9 5.5 %collective-permute-start.14 = (f32[8,48]{1,0:T(8,128)S(1)}, f32[8,48]{1,0:T(8,128)S(1)}, u32[]{:S(2)}, u32[]{:S(2)}) collective-permute-start(f32[8,48]{1,0:T(8,128)S(1)} %get-tuple-element.54.refs_2_.refs_3_), channel_id=1, source_target_pairs={{0,6},{2,4},{4,2},{6,0},{1,7},{3,5},{5,3},{7,1},{8,14},{10,12},{12... | collective-permute-start | bytes 4616 | tf_op jit(solution)/shard_map/ppermute | solution.py:710
  34.8 5.4 %collective-permute-start.19 = (f32[8,48]{1,0:T(8,128)S(1)}, f32[8,48]{1,0:T(8,128)S(1)}, u32[]{:S(2)}, u32[]{:S(2)}) collective-permute-start(f32[8,48]{1,0:T(8,128)S(1)} %kernel_sweep.6.refs_2_.refs_3_), channel_id=1, source_target_pairs={{0,6},{2,4},{4,2},{6,0},{1,7},{3,5},{5,3},{7,1},{8,14},{10,12},{12... | collective-permute-start | bytes 4616 | tf_op jit(solution)/shard_map/ppermute | solution.py:710
  41.3 5.4 %collective-permute-start.24 = (f32[8,48]{1,0:T(8,128)S(1)}, f32[8,48]{1,0:T(8,128)S(1)}, u32[]{:S(2)}, u32[]{:S(2)}) collective-permute-start(f32[8,48]{1,0:T(8,128)S(1)} %kernel_sweep.7.refs_2_.refs_3_), channel_id=1, source_target_pairs={{0,6},{2,4},{4,2},{6,0},{1,7},{3,5},{5,3},{7,1},{8,14},{10,12},{12... | collective-permute-start | bytes 4616 | tf_op jit(solution)/shard_map/ppermute | solution.py:710
  49.0 5.4 %collective-permute-start.29 = (f32[8,48]{1,0:T(8,128)S(1)}, f32[8,48]{1,0:T(8,128)S(1)}, u32[]{:S(2)}, u32[]{:S(2)}) collective-permute-start(f32[8,48]{1,0:T(8,128)S(1)} %kernel_sweep.8.refs_2_.refs_5_), channel_id=1, source_target_pairs={{0,6},{2,4},{4,2},{6,0},{1,7},{3,5},{5,3},{7,1},{8,14},{10,12},{12... | collective-permute-start | bytes 4616 | tf_op jit(solution)/shard_map/ppermute | solution.py:710
  56.3 5.7 %collective-permute-start.35 = (f32[3,8,128]{2,1,0:T(8,128)S(1)}, f32[3,8,128]{2,1,0:T(8,128)S(1)}, u32[]{:S(2)}, u32[]{:S(2)}) collective-permute-start(f32[3,8,128]{2,1,0:T(8,128)S(1)} %kernel_sweep_up.2.refs_1_.refs_6_), channel_id=1, source_target_pairs={{0,8},{8,0},{16,24},{24,16},{1,9},{9,1},{17,25},{25,17},{2,10},{10... | collective-permute-start | bytes 36872 | tf_op jit(solution)/shard_map/ppermute | solution.py:710
  56.4 5.7 %collective-permute-start.34 = (f32[3,8,128]{2,1,0:T(8,128)S(1)}, f32[3,8,128]{2,1,0:T(8,128)S(1)}, u32[]{:S(2)}, u32[]{:S(2)}) collective-permute-start(f32[3,8,128]{2,1,0:T(8,128)S(1)} %kernel_sweep_up.2.refs_1_.refs_6_), channel_id=1, source_target_pairs={{0,6},{2,4},{4,2},{6,0},{1,7},{3,5},{5,3},{7,1},{8,14},{10,12},{12... | collective-permute-start | bytes 36872 | tf_op jit(solution)/shard_map/ppermute | solution.py:710
  65.3 5.9 %collective-permute-start.37 = (f32[6,8,128]{2,1,0:T(8,128)S(1)}, f32[6,8,128]{2,1,0:T(8,128)S(1)}, u32[]{:S(2)}, u32[]{:S(2)}) collective-permute-start(f32[6,8,128]{2,1,0:T(8,128)S(1)} %get-tuple-element.57), channel_id=1, source_target_pairs={{0,6},{2,4},{4,2},{6,0},{1,7},{3,5},{5,3},{7,1},{8,14},{10,12},{12... | collective-permute-start | bytes 73736 | tf_op jit(solution)/shard_map/ppermute | solution.py:710
  72.3 5.5 %collective-permute-start.41 = (f32[6,8,128]{2,1,0:T(8,128)S(1)}, f32[6,8,128]{2,1,0:T(8,128)S(1)}, u32[]{:S(2)}, u32[]{:S(2)}) collective-permute-start(f32[6,8,128]{2,1,0:T(8,128)S(1)} %get-tuple-element.61), channel_id=1, source_target_pairs={{0,8},{8,0},{16,24},{24,16},{1,9},{9,1},{17,25},{25,17},{2,10},{10... | collective-permute-start | bytes 73736 | tf_op jit(solution)/shard_map/ppermute | solution.py:710
  72.3 5.8 %collective-permute-start.42 = (f32[6,8,128]{2,1,0:T(8,128)S(1)}, f32[6,8,128]{2,1,0:T(8,128)S(1)}, u32[]{:S(2)}, u32[]{:S(2)}) collective-permute-start(f32[6,8,128]{2,1,0:T(8,128)S(1)} %get-tuple-element.62), channel_id=1, source_target_pairs={{0,6},{2,4},{4,2},{6,0},{1,7},{3,5},{5,3},{7,1},{8,14},{10,12},{12... | collective-permute-start | bytes 73736 | tf_op jit(solution)/shard_map/ppermute | solution.py:710
  80.7 5.9 %collective-permute-start.47 = (f32[6,8,128]{2,1,0:T(8,128)S(1)}, f32[6,8,128]{2,1,0:T(8,128)S(1)}, u32[]{:S(2)}, u32[]{:S(2)}) collective-permute-start(f32[6,8,128]{2,1,0:T(8,128)S(1)} %get-tuple-element.67), channel_id=1, source_target_pairs={{0,6},{2,4},{4,2},{6,0},{1,7},{3,5},{5,3},{7,1},{8,14},{10,12},{12... | collective-permute-start | bytes 73736 | tf_op jit(solution)/shard_map/ppermute | solution.py:710
  87.9 5.7 %collective-permute-start.55 = (f32[3,8,128]{2,1,0:T(8,128)S(1)}, f32[3,8,128]{2,1,0:T(8,128)S(1)}, u32[]{:S(2)}, u32[]{:S(2)}) collective-permute-start(f32[3,8,128]{2,1,0:T(8,128)S(1)} %get-tuple-element.71.refs_1_.refs_4_.refs_3_), channel_id=1, source_target_pairs={{0,8},{8,0},{16,24},{24,16},{1,9},{9,1},{17,25},{25,17},{2,10},{10... | collective-permute-start | bytes 36872 | tf_op jit(solution)/shard_map/ppermute | solution.py:710
  87.9 5.7 %collective-permute-start.54 = (f32[3,8,128]{2,1,0:T(8,128)S(1)}, f32[3,8,128]{2,1,0:T(8,128)S(1)}, u32[]{:S(2)}, u32[]{:S(2)}) collective-permute-start(f32[3,8,128]{2,1,0:T(8,128)S(1)} %get-tuple-element.71.refs_1_.refs_4_.refs_3_), channel_id=1, source_target_pairs={{0,6},{2,4},{4,2},{6,0},{1,7},{3,5},{5,3},{7,1},{8,14},{10,12},{12... | collective-permute-start | bytes 36872 | tf_op jit(solution)/shard_map/ppermute | solution.py:710
  96.7 5.5 %collective-permute-start.59 = (f32[8,48]{1,0:T(8,128)S(1)}, f32[8,48]{1,0:T(8,128)S(1)}, u32[]{:S(2)}, u32[]{:S(2)}) collective-permute-start(f32[8,48]{1,0:T(8,128)S(1)} %get-tuple-element.73.refs_2_.refs_3_), channel_id=1, source_target_pairs={{0,6},{2,4},{4,2},{6,0},{1,7},{3,5},{5,3},{7,1},{8,14},{10,12},{12... | collective-permute-start | bytes 4616 | tf_op jit(solution)/shard_map/ppermute | solution.py:710
  103.3 5.4 %collective-permute-start.64 = (f32[8,48]{1,0:T(8,128)S(1)}, f32[8,48]{1,0:T(8,128)S(1)}, u32[]{:S(2)}, u32[]{:S(2)}) collective-permute-start(f32[8,48]{1,0:T(8,128)S(1)} %kernel_sweep.9.refs_2_.refs_3_), channel_id=1, source_target_pairs={{0,6},{2,4},{4,2},{6,0},{1,7},{3,5},{5,3},{7,1},{8,14},{10,12},{12... | collective-permute-start | bytes 4616 | tf_op jit(solution)/shard_map/ppermute | solution.py:710
  126.3 5.7 %collective-permute-start.79 = (f32[3,8,128]{2,1,0:T(8,128)S(1)}, f32[3,8,128]{2,1,0:T(8,128)S(1)}, u32[]{:S(2)}, u32[]{:S(2)}) collective-permute-start(f32[3,8,128]{2,1,0:T(8,128)S(1)} %kernel_sweep_up.3.refs_1_.refs_6_), channel_id=1, source_target_pairs={{0,6},{2,4},{4,2},{6,0},{1,7},{3,5},{5,3},{7,1},{8,14},{10,12},{12... | collective-permute-start | bytes 36872 | tf_op jit(solution)/shard_map/ppermute | solution.py:710
  133.9 5.5 %collective-permute-start.81 = (f32[6,8,128]{2,1,0:T(8,128)S(1)}, f32[6,8,128]{2,1,0:T(8,128)S(1)}, u32[]{:S(2)}, u32[]{:S(2)}) collective-permute-start(f32[6,8,128]{2,1,0:T(8,128)S(1)} %get-tuple-element.75), channel_id=1, source_target_pairs={{0,8},{8,0},{16,24},{24,16},{1,9},{9,1},{17,25},{25,17},{2,10},{10... | collective-permute-start | bytes 73736 | tf_op jit(solution)/shard_map/ppermute | solution.py:710
  134.0 5.8 %collective-permute-start.82 = (f32[6,8,128]{2,1,0:T(8,128)S(1)}, f32[6,8,128]{2,1,0:T(8,128)S(1)}, u32[]{:S(2)}, u32[]{:S(2)}) collective-permute-start(f32[6,8,128]{2,1,0:T(8,128)S(1)} %get-tuple-element.76), channel_id=1, source_target_pairs={{0,6},{2,4},{4,2},{6,0},{1,7},{3,5},{5,3},{7,1},{8,14},{10,12},{12... | collective-permute-start | bytes 73736 | tf_op jit(solution)/shard_map/ppermute | solution.py:710
  142.3 5.9 %collective-permute-start.87 = (f32[6,8,128]{2,1,0:T(8,128)S(1)}, f32[6,8,128]{2,1,0:T(8,128)S(1)}, u32[]{:S(2)}, u32[]{:S(2)}) collective-permute-start(f32[6,8,128]{2,1,0:T(8,128)S(1)} %get-tuple-element.81), channel_id=1, source_target_pairs={{0,6},{2,4},{4,2},{6,0},{1,7},{3,5},{5,3},{7,1},{8,14},{10,12},{12... | collective-permute-start | bytes 73736 | tf_op jit(solution)/shard_map/ppermute | solution.py:710
  (74 other events, 307.2 us)

commit v4 on v3

--- a/solution.py
+++ b/solution.py
@@ -759,7 +759,7 @@
     rhs, *state = call(kernel_first, [TILE6] + FINE_OUT, [], g, block, right_side)
     for cycle_no in range(CYCLES):
         around = exchange_fine(g, gx, *state)
-        r2, y2 = call(kernel_restrict, [mid, mid], [], g, near1, jacobi2, rhs, *around)
+        r2, y2 = call(kernel_restrict, [mid, mid], [], g, near1, jacobi2, rhs, *around, after=(stencil2,))
         around = exchange(y2)
         (own,) = call(kernel_mid_own, [mid], [], stencil2, y2)
         r3, y3 = call(

time: 150 us -> 149 us (level)
  no operation moved by 1% of the time
where the time goes in v4:
time: 149 us
  starting transfers between devices  85.8 us (58%)
  waiting for transfers between devices  31.4 us (21%)
  Pallas kernels  25.1 us (17%)
  local copies, waits for them, and re-layouts  5.64 us (4%)
    ppermute x72, starting transfers between devices, swap(): lax.ppermute(block, axis, [(i, ((i + phase ^ 1) - phase) % n) for i in ra...  56.9 us
    ppermute x19, starting transfers between devices, from_behind(): lax.ppermute(block, axis, [((i - distance) % n, i) for i in range(n)])  28.9 us
    pallas_call x39, Pallas kernels, call(): pl.pallas_call(body, out_shape=[jax.ShapeDtypeStruct(*s) if s[1] == BF16...  25.1 us
    ppermute x72, waiting for transfers between devices, swap(): lax.ppermute(block, axis, [(i, ((i + phase ^ 1) - phase) % n) for i in ra...  19.3 us
    ppermute x19, waiting for transfers between devices, from_behind(): lax.ppermute(block, axis, [((i - distance) % n, i) for i in range(n)])  12.1 us
    reshape x1, local copies, waits for them, and re-layouts, local(): stencil2 = mid_stencil.reshape(1728, 384)  3.41 us
  transfers between devices with their start and end apart: 91, of which 36 were waited for; matrix products, arithmetic and copies ran while one was open for 2% of the time, Pallas kernels for 5%

profile of v4, /device:TPU:0, one launch (start us, length us, event | category | flops | bytes accessed | tf_op | source)
XLA Modules:
  0.0 149.0 jit_solution(9535865914026934676)
XLA Ops:
  0.6 2.0 %reshape.25.refs_0_.refs_1_ = bf16[384,768]{1,0:T(8,128)(2,1)S(1)} reshape(bf16[48,2,2,2,768]{4,3,2,1,0:T(2,128)(2,1)} %param.11) | data formatting | bytes 1179648 | tf_op jit(solution)/shard_map/reshape | solution.py:747
  2.7 1.6 %kernel_links.1 = (f32[144,8,128]{2,1,0:T(8,128)S(1)}, bf16[18,16,128]{2,1,0:T(8,128)(2,1)S(1)}) custom-call(bf16[384,768]{1,0:T(8,128)(2,1)S(1)} %reshape.25.refs_0_.refs_1_, bf16[3,3,4,4,4,256]{5,4,3,2,1,0:T(4,128)(2,1)S(1)} %copy-done.3), custom_call_target="tpu_custom_call" | custom-call | tf_op jit(solution)/shard_map/kernel_links/pallas_call | solution.py:693
  4.3 3.0 %collective-permute-start.5 = (bf16[18,16,128]{2,1,0:T(8,128)(2,1)S(1)}, bf16[18,16,128]{2,1,0:T(8,128)(2,1)S(1)}, u32[]{:S(2)}, u32[]{:S(2)}) collective-permute-start(bf16[18,16,128]{2,1,0:T(8,128)(2,1)S(1)} %get-tuple-element.50), channel_id=1, source_target_pairs={{1,0},{0,1},{3,2},{2,3},{5,4},{4,5},{7,6},{6,7},{9,8},{8,9},{11,10... | collective-permute-start | bytes 221192 | tf_op jit(solution)/shard_map/ppermute | solution.py:705
  8.4 3.7 %collective-permute-start.1 = (f32[6,8,128]{2,1,0:T(8,128)S(1)}, f32[6,8,128]{2,1,0:T(8,128)S(1)}, u32[]{:S(2)}, u32[]{:S(2)}) collective-permute-start(f32[6,8,128]{2,1,0:T(8,128)S(1)} %get-tuple-element.47), channel_id=1, source_target_pairs={{0,6},{2,4},{4,2},{6,0},{1,7},{3,5},{5,3},{7,1},{8,14},{10,12},{12... | collective-permute-start | bytes 73736 | tf_op jit(solution)/shard_map/ppermute | solution.py:710
  14.4 3.4 %reshape.26.refs_0_.refs_1_ = bf16[1728,384]{1,0:T(8,128)(2,1)S(1)} reshape(bf16[9,24,2,2,2,384]{5,4,3,2,1,0:T(2,128)(2,1)} %param.13) | data formatting | bytes 2654208 | tf_op jit(solution)/shard_map/reshape | solution.py:749
  22.9 1.6 %collective-permute-done.9.refs_9_ = f32[3,8,128]{2,1,0:T(8,128)S(1)} collective-permute-done((f32[3,8,128]{2,1,0:T(8,128)S(1)}, f32[3,8,128]{2,1,0:T(8,128)S(1)}, u32[]{:S(2)}, u32[]{:S(2)}) %collective-permute-start.9) | collective-permute-done | bytes 12320 | tf_op jit(solution)/shard_map/ppermute | solution.py:710
  26.1 3.0 %collective-permute-start.14 = (f32[8,48]{1,0:T(8,128)S(1)}, f32[8,48]{1,0:T(8,128)S(1)}, u32[]{:S(2)}, u32[]{:S(2)}) collective-permute-start(f32[8,48]{1,0:T(8,128)S(1)} %get-tuple-element.54.refs_2_.refs_3_), channel_id=1, source_target_pairs={{0,6},{2,4},{4,2},{6,0},{1,7},{3,5},{5,3},{7,1},{8,14},{10,12},{12... | collective-permute-start | bytes 4616 | tf_op jit(solution)/shard_map/ppermute | solution.py:710
  36.6 1.5 %collective-permute-start.16 = (f32[8,48]{1,0:T(8,128)S(1)}, f32[8,48]{1,0:T(8,128)S(1)}, u32[]{:S(2)}, u32[]{:S(2)}) collective-permute-start(f32[8,48]{1,0:T(8,128)S(1)} %kernel_sweep.6.refs_2_.refs_3_), channel_id=1, source_target_pairs={{1,0},{0,1},{3,2},{2,3},{5,4},{4,5},{7,6},{6,7},{9,8},{8,9},{11,10... | collective-permute-start | bytes 4616 | tf_op jit(solution)/shard_map/ppermute | solution.py:705
  40.7 2.6 %collective-permute-start.24 = (f32[8,48]{1,0:T(8,128)S(1)}, f32[8,48]{1,0:T(8,128)S(1)}, u32[]{:S(2)}, u32[]{:S(2)}) collective-permute-start(f32[8,48]{1,0:T(8,128)S(1)} %kernel_sweep.7.refs_2_.refs_3_), channel_id=1, source_target_pairs={{0,6},{2,4},{4,2},{6,0},{1,7},{3,5},{5,3},{7,1},{8,14},{10,12},{12... | collective-permute-start | bytes 4616 | tf_op jit(solution)/shard_map/ppermute | solution.py:710
  44.5 1.5 %collective-permute-start.21 = (f32[8,48]{1,0:T(8,128)S(1)}, f32[8,48]{1,0:T(8,128)S(1)}, u32[]{:S(2)}, u32[]{:S(2)}) collective-permute-start(f32[8,48]{1,0:T(8,128)S(1)} %kernel_sweep.7.refs_2_.refs_3_), channel_id=1, source_target_pairs={{1,0},{0,1},{3,2},{2,3},{5,4},{4,5},{7,6},{6,7},{9,8},{8,9},{11,10... | collective-permute-start | bytes 4616 | tf_op jit(solution)/shard_map/ppermute | solution.py:705
  55.8 2.7 %collective-permute-start.34 = (f32[3,8,128]{2,1,0:T(8,128)S(1)}, f32[3,8,128]{2,1,0:T(8,128)S(1)}, u32[]{:S(2)}, u32[]{:S(2)}) collective-permute-start(f32[3,8,128]{2,1,0:T(8,128)S(1)} %kernel_sweep_up.2.refs_1_.refs_6_), channel_id=1, source_target_pairs={{0,6},{2,4},{4,2},{6,0},{1,7},{3,5},{5,3},{7,1},{8,14},{10,12},{12... | collective-permute-start | bytes 36872 | tf_op jit(solution)/shard_map/ppermute | solution.py:710
  59.5 1.5 %collective-permute-start.31 = (f32[3,8,128]{2,1,0:T(8,128)S(1)}, f32[3,8,128]{2,1,0:T(8,128)S(1)}, u32[]{:S(2)}, u32[]{:S(2)}) collective-permute-start(f32[3,8,128]{2,1,0:T(8,128)S(1)} %kernel_sweep_up.2.refs_1_.refs_6_), channel_id=1, source_target_pairs={{1,0},{0,1},{3,2},{2,3},{5,4},{4,5},{7,6},{6,7},{9,8},{8,9},{11,10... | collective-permute-start | bytes 36872 | tf_op jit(solution)/shard_map/ppermute | solution.py:705
  68.8 1.8 %collective-permute-done.37.refs_6_ = f32[6,8,128]{2,1,0:T(8,128)S(1)} collective-permute-done((f32[6,8,128]{2,1,0:T(8,128)S(1)}, f32[6,8,128]{2,1,0:T(8,128)S(1)}, u32[]{:S(2)}, u32[]{:S(2)}) %collective-permute-start.37) | collective-permute-done | bytes 24608 | tf_op jit(solution)/shard_map/ppermute | solution.py:710
  71.8 2.7 %collective-permute-start.42 = (f32[6,8,128]{2,1,0:T(8,128)S(1)}, f32[6,8,128]{2,1,0:T(8,128)S(1)}, u32[]{:S(2)}, u32[]{:S(2)}) collective-permute-start(f32[6,8,128]{2,1,0:T(8,128)S(1)} %get-tuple-element.62), channel_id=1, source_target_pairs={{0,6},{2,4},{4,2},{6,0},{1,7},{3,5},{5,3},{7,1},{8,14},{10,12},{12... | collective-permute-start | bytes 73736 | tf_op jit(solution)/shard_map/ppermute | solution.py:710
  75.5 1.5 %collective-permute-start.45 = (f32[6,8,128]{2,1,0:T(8,128)S(1)}, f32[6,8,128]{2,1,0:T(8,128)S(1)}, u32[]{:S(2)}, u32[]{:S(2)}) collective-permute-start(f32[6,8,128]{2,1,0:T(8,128)S(1)} %get-tuple-element.60.refs_1_.refs_3_), channel_id=1, source_target_pairs={{1,0},{0,1},{3,2},{2,3},{5,4},{4,5},{7,6},{6,7},{9,8},{8,9},{11,10... | collective-permute-start | bytes 73736 | tf_op jit(solution)/shard_map/ppermute | solution.py:705
  84.2 1.8 %collective-permute-done.47.refs_8_ = f32[6,8,128]{2,1,0:T(8,128)S(1)} collective-permute-done((f32[6,8,128]{2,1,0:T(8,128)S(1)}, f32[6,8,128]{2,1,0:T(8,128)S(1)}, u32[]{:S(2)}, u32[]{:S(2)}) %collective-permute-start.47) | collective-permute-done | bytes 24608 | tf_op jit(solution)/shard_map/ppermute | solution.py:710
  87.3 2.7 %collective-permute-start.54 = (f32[3,8,128]{2,1,0:T(8,128)S(1)}, f32[3,8,128]{2,1,0:T(8,128)S(1)}, u32[]{:S(2)}, u32[]{:S(2)}) collective-permute-start(f32[3,8,128]{2,1,0:T(8,128)S(1)} %get-tuple-element.71.refs_1_.refs_4_.refs_3_), channel_id=1, source_target_pairs={{0,6},{2,4},{4,2},{6,0},{1,7},{3,5},{5,3},{7,1},{8,14},{10,12},{12... | collective-permute-start | bytes 36872 | tf_op jit(solution)/shard_map/ppermute | solution.py:710
  91.0 1.5 %collective-permute-start.51 = (f32[3,8,128]{2,1,0:T(8,128)S(1)}, f32[3,8,128]{2,1,0:T(8,128)S(1)}, u32[]{:S(2)}, u32[]{:S(2)}) collective-permute-start(f32[3,8,128]{2,1,0:T(8,128)S(1)} %get-tuple-element.71.refs_1_.refs_4_.refs_3_), channel_id=1, source_target_pairs={{1,0},{0,1},{3,2},{2,3},{5,4},{4,5},{7,6},{6,7},{9,8},{8,9},{11,10... | collective-permute-start | bytes 36872 | tf_op jit(solution)/shard_map/ppermute | solution.py:705
  102.7 2.6 %collective-permute-start.64 = (f32[8,48]{1,0:T(8,128)S(1)}, f32[8,48]{1,0:T(8,128)S(1)}, u32[]{:S(2)}, u32[]{:S(2)}) collective-permute-start(f32[8,48]{1,0:T(8,128)S(1)} %kernel_sweep.9.refs_2_.refs_3_), channel_id=1, source_target_pairs={{0,6},{2,4},{4,2},{6,0},{1,7},{3,5},{5,3},{7,1},{8,14},{10,12},{12... | collective-permute-start | bytes 4616 | tf_op jit(solution)/shard_map/ppermute | solution.py:710
  106.4 1.5 %collective-permute-start.61 = (f32[8,48]{1,0:T(8,128)S(1)}, f32[8,48]{1,0:T(8,128)S(1)}, u32[]{:S(2)}, u32[]{:S(2)}) collective-permute-start(f32[8,48]{1,0:T(8,128)S(1)} %kernel_sweep.9.refs_2_.refs_3_), channel_id=1, source_target_pairs={{1,0},{0,1},{3,2},{2,3},{5,4},{4,5},{7,6},{6,7},{9,8},{8,9},{11,10... | collective-permute-start | bytes 4616 | tf_op jit(solution)/shard_map/ppermute | solution.py:705
  116.9 2.6 %collective-permute-start.74 = (f32[8,48]{1,0:T(8,128)S(1)}, f32[8,48]{1,0:T(8,128)S(1)}, u32[]{:S(2)}, u32[]{:S(2)}) collective-permute-start(f32[8,48]{1,0:T(8,128)S(1)} %kernel_sweep.11.refs_2_.refs_5_), channel_id=1, source_target_pairs={{0,6},{2,4},{4,2},{6,0},{1,7},{3,5},{5,3},{7,1},{8,14},{10,12},{12... | collective-permute-start | bytes 4616 | tf_op jit(solution)/shard_map/ppermute | solution.py:710
  120.7 1.5 %collective-permute-start.71 = (f32[8,48]{1,0:T(8,128)S(1)}, f32[8,48]{1,0:T(8,128)S(1)}, u32[]{:S(2)}, u32[]{:S(2)}) collective-permute-start(f32[8,48]{1,0:T(8,128)S(1)} %kernel_sweep.11.refs_2_.refs_5_), channel_id=1, source_target_pairs={{1,0},{0,1},{3,2},{2,3},{5,4},{4,5},{7,6},{6,7},{9,8},{8,9},{11,10... | collective-permute-start | bytes 4616 | tf_op jit(solution)/shard_map/ppermute | solution.py:705
  133.2 2.7 %collective-permute-start.82 = (f32[6,8,128]{2,1,0:T(8,128)S(1)}, f32[6,8,128]{2,1,0:T(8,128)S(1)}, u32[]{:S(2)}, u32[]{:S(2)}) collective-permute-start(f32[6,8,128]{2,1,0:T(8,128)S(1)} %get-tuple-element.76), channel_id=1, source_target_pairs={{0,6},{2,4},{4,2},{6,0},{1,7},{3,5},{5,3},{7,1},{8,14},{10,12},{12... | collective-permute-start | bytes 73736 | tf_op jit(solution)/shard_map/ppermute | solution.py:710
  136.9 1.5 %collective-permute-start.85 = (f32[6,8,128]{2,1,0:T(8,128)S(1)}, f32[6,8,128]{2,1,0:T(8,128)S(1)}, u32[]{:S(2)}, u32[]{:S(2)}) collective-permute-start(f32[6,8,128]{2,1,0:T(8,128)S(1)} %get-tuple-element.74.refs_1_.refs_3_), channel_id=1, source_target_pairs={{1,0},{0,1},{3,2},{2,3},{5,4},{4,5},{7,6},{6,7},{9,8},{8,9},{11,10... | collective-permute-start | bytes 73736 | tf_op jit(solution)/shard_map/ppermute | solution.py:705
  (215 shorter events, 95.4 us)
Async XLA Ops:
  4.3 13.5 %collective-permute-start.5 = (bf16[18,16,128]{2,1,0:T(8,128)(2,1)S(1)}, bf16[18,16,128]{2,1,0:T(8,128)(2,1)S(1)}, u32[]{:S(2)}, u32[]{:S(2)}) collective-permute-start(bf16[18,16,128]{2,1,0:T(8,128)(2,1)S(1)} %get-tuple-element.50), channel_id=1, source_target_pairs={{1,0},{0,1},{3,2},{2,3},{5,4},{4,5},{7,6},{6,7},{9,8},{8,9},{11,10... | collective-permute-start | bytes 221192 | tf_op jit(solution)/shard_map/ppermute | solution.py:705
  8.4 9.4 %collective-permute-start.1 = (f32[6,8,128]{2,1,0:T(8,128)S(1)}, f32[6,8,128]{2,1,0:T(8,128)S(1)}, u32[]{:S(2)}, u32[]{:S(2)}) collective-permute-start(f32[6,8,128]{2,1,0:T(8,128)S(1)} %get-tuple-element.47), channel_id=1, source_target_pairs={{0,6},{2,4},{4,2},{6,0},{1,7},{3,5},{5,3},{7,1},{8,14},{10,12},{12... | collective-permute-start | bytes 73736 | tf_op jit(solution)/shard_map/ppermute | solution.py:710
  12.1 5.7 %collective-permute-start.2 = (f32[6,8,128]{2,1,0:T(8,128)S(1)}, f32[6,8,128]{2,1,0:T(8,128)S(1)}, u32[]{:S(2)}, u32[]{:S(2)}) collective-permute-start(f32[6,8,128]{2,1,0:T(8,128)S(1)} %get-tuple-element.48), channel_id=1, source_target_pairs={{0,2},{2,0},{4,6},{6,4},{1,3},{3,1},{5,7},{7,5},{8,10},{10,8},{12,... | collective-permute-start | bytes 73736 | tf_op jit(solution)/shard_map/ppermute | solution.py:710
  12.1 5.7 %collective-permute-start.3 = (f32[6,8,128]{2,1,0:T(8,128)S(1)}, f32[6,8,128]{2,1,0:T(8,128)S(1)}, u32[]{:S(2)}, u32[]{:S(2)}) collective-permute-start(f32[6,8,128]{2,1,0:T(8,128)S(1)} %get-tuple-element.49), channel_id=1, source_target_pairs={{0,24},{8,16},{16,8},{24,0},{1,25},{9,17},{17,9},{25,1},{2,26},{10... | collective-permute-start | bytes 73736 | tf_op jit(solution)/shard_map/ppermute | solution.py:710
  18.9 5.6 %collective-permute-start.9 = (f32[3,8,128]{2,1,0:T(8,128)S(1)}, f32[3,8,128]{2,1,0:T(8,128)S(1)}, u32[]{:S(2)}, u32[]{:S(2)}) collective-permute-start(f32[3,8,128]{2,1,0:T(8,128)S(1)} %get-tuple-element.52.refs_1_.refs_4_.refs_3_), channel_id=1, source_target_pairs={{0,6},{2,4},{4,2},{6,0},{1,7},{3,5},{5,3},{7,1},{8,14},{10,12},{12... | collective-permute-start | bytes 36872 | tf_op jit(solution)/shard_map/ppermute | solution.py:710
  26.1 5.8 %collective-permute-start.15 = (f32[8,48]{1,0:T(8,128)S(1)}, f32[8,48]{1,0:T(8,128)S(1)}, u32[]{:S(2)}, u32[]{:S(2)}) collective-permute-start(f32[8,48]{1,0:T(8,128)S(1)} %get-tuple-element.54.refs_2_.refs_3_), channel_id=1, source_target_pairs={{0,8},{8,0},{16,24},{24,16},{1,9},{9,1},{17,25},{25,17},{2,10},{10... | collective-permute-start | bytes 4616 | tf_op jit(solution)/shard_map/ppermute | solution.py:710
  26.1 5.8 %collective-permute-start.14 = (f32[8,48]{1,0:T(8,128)S(1)}, f32[8,48]{1,0:T(8,128)S(1)}, u32[]{:S(2)}, u32[]{:S(2)}) collective-permute-start(f32[8,48]{1,0:T(8,128)S(1)} %get-tuple-element.54.refs_2_.refs_3_), channel_id=1, source_target_pairs={{0,6},{2,4},{4,2},{6,0},{1,7},{3,5},{5,3},{7,1},{8,14},{10,12},{12... | collective-permute-start | bytes 4616 | tf_op jit(solution)/shard_map/ppermute | solution.py:710
  40.7 5.5 %collective-permute-start.25 = (f32[8,48]{1,0:T(8,128)S(1)}, f32[8,48]{1,0:T(8,128)S(1)}, u32[]{:S(2)}, u32[]{:S(2)}) collective-permute-start(f32[8,48]{1,0:T(8,128)S(1)} %kernel_sweep.7.refs_2_.refs_3_), channel_id=1, source_target_pairs={{0,8},{8,0},{16,24},{24,16},{1,9},{9,1},{17,25},{25,17},{2,10},{10... | collective-permute-start | bytes 4616 | tf_op jit(solution)/shard_map/ppermute | solution.py:710
  40.7 5.5 %collective-permute-start.24 = (f32[8,48]{1,0:T(8,128)S(1)}, f32[8,48]{1,0:T(8,128)S(1)}, u32[]{:S(2)}, u32[]{:S(2)}) collective-permute-start(f32[8,48]{1,0:T(8,128)S(1)} %kernel_sweep.7.refs_2_.refs_3_), channel_id=1, source_target_pairs={{0,6},{2,4},{4,2},{6,0},{1,7},{3,5},{5,3},{7,1},{8,14},{10,12},{12... | collective-permute-start | bytes 4616 | tf_op jit(solution)/shard_map/ppermute | solution.py:710
  55.7 5.8 %collective-permute-start.35 = (f32[3,8,128]{2,1,0:T(8,128)S(1)}, f32[3,8,128]{2,1,0:T(8,128)S(1)}, u32[]{:S(2)}, u32[]{:S(2)}) collective-permute-start(f32[3,8,128]{2,1,0:T(8,128)S(1)} %kernel_sweep_up.2.refs_1_.refs_6_), channel_id=1, source_target_pairs={{0,8},{8,0},{16,24},{24,16},{1,9},{9,1},{17,25},{25,17},{2,10},{10... | collective-permute-start | bytes 36872 | tf_op jit(solution)/shard_map/ppermute | solution.py:710
  55.8 5.7 %collective-permute-start.34 = (f32[3,8,128]{2,1,0:T(8,128)S(1)}, f32[3,8,128]{2,1,0:T(8,128)S(1)}, u32[]{:S(2)}, u32[]{:S(2)}) collective-permute-start(f32[3,8,128]{2,1,0:T(8,128)S(1)} %kernel_sweep_up.2.refs_1_.refs_6_), channel_id=1, source_target_pairs={{0,6},{2,4},{4,2},{6,0},{1,7},{3,5},{5,3},{7,1},{8,14},{10,12},{12... | collective-permute-start | bytes 36872 | tf_op jit(solution)/shard_map/ppermute | solution.py:710
  64.8 5.9 %collective-permute-start.37 = (f32[6,8,128]{2,1,0:T(8,128)S(1)}, f32[6,8,128]{2,1,0:T(8,128)S(1)}, u32[]{:S(2)}, u32[]{:S(2)}) collective-permute-start(f32[6,8,128]{2,1,0:T(8,128)S(1)} %get-tuple-element.57), channel_id=1, source_target_pairs={{0,6},{2,4},{4,2},{6,0},{1,7},{3,5},{5,3},{7,1},{8,14},{10,12},{12... | collective-permute-start | bytes 73736 | tf_op jit(solution)/shard_map/ppermute | solution.py:710
  71.7 5.6 %collective-permute-start.41 = (f32[6,8,128]{2,1,0:T(8,128)S(1)}, f32[6,8,128]{2,1,0:T(8,128)S(1)}, u32[]{:S(2)}, u32[]{:S(2)}) collective-permute-start(f32[6,8,128]{2,1,0:T(8,128)S(1)} %get-tuple-element.61), channel_id=1, source_target_pairs={{0,8},{8,0},{16,24},{24,16},{1,9},{9,1},{17,25},{25,17},{2,10},{10... | collective-permute-start | bytes 73736 | tf_op jit(solution)/shard_map/ppermute | solution.py:710
  71.8 5.7 %collective-permute-start.42 = (f32[6,8,128]{2,1,0:T(8,128)S(1)}, f32[6,8,128]{2,1,0:T(8,128)S(1)}, u32[]{:S(2)}, u32[]{:S(2)}) collective-permute-start(f32[6,8,128]{2,1,0:T(8,128)S(1)} %get-tuple-element.62), channel_id=1, source_target_pairs={{0,6},{2,4},{4,2},{6,0},{1,7},{3,5},{5,3},{7,1},{8,14},{10,12},{12... | collective-permute-start | bytes 73736 | tf_op jit(solution)/shard_map/ppermute | solution.py:710
  80.2 5.9 %collective-permute-start.47 = (f32[6,8,128]{2,1,0:T(8,128)S(1)}, f32[6,8,128]{2,1,0:T(8,128)S(1)}, u32[]{:S(2)}, u32[]{:S(2)}) collective-permute-start(f32[6,8,128]{2,1,0:T(8,128)S(1)} %get-tuple-element.67), channel_id=1, source_target_pairs={{0,6},{2,4},{4,2},{6,0},{1,7},{3,5},{5,3},{7,1},{8,14},{10,12},{12... | collective-permute-start | bytes 73736 | tf_op jit(solution)/shard_map/ppermute | solution.py:710
  87.3 5.8 %collective-permute-start.55 = (f32[3,8,128]{2,1,0:T(8,128)S(1)}, f32[3,8,128]{2,1,0:T(8,128)S(1)}, u32[]{:S(2)}, u32[]{:S(2)}) collective-permute-start(f32[3,8,128]{2,1,0:T(8,128)S(1)} %get-tuple-element.71.refs_1_.refs_4_.refs_3_), channel_id=1, source_target_pairs={{0,8},{8,0},{16,24},{24,16},{1,9},{9,1},{17,25},{25,17},{2,10},{10... | collective-permute-start | bytes 36872 | tf_op jit(solution)/shard_map/ppermute | solution.py:710
  87.3 5.7 %collective-permute-start.54 = (f32[3,8,128]{2,1,0:T(8,128)S(1)}, f32[3,8,128]{2,1,0:T(8,128)S(1)}, u32[]{:S(2)}, u32[]{:S(2)}) collective-permute-start(f32[3,8,128]{2,1,0:T(8,128)S(1)} %get-tuple-element.71.refs_1_.refs_4_.refs_3_), channel_id=1, source_target_pairs={{0,6},{2,4},{4,2},{6,0},{1,7},{3,5},{5,3},{7,1},{8,14},{10,12},{12... | collective-permute-start | bytes 36872 | tf_op jit(solution)/shard_map/ppermute | solution.py:710
  102.7 5.5 %collective-permute-start.64 = (f32[8,48]{1,0:T(8,128)S(1)}, f32[8,48]{1,0:T(8,128)S(1)}, u32[]{:S(2)}, u32[]{:S(2)}) collective-permute-start(f32[8,48]{1,0:T(8,128)S(1)} %kernel_sweep.9.refs_2_.refs_3_), channel_id=1, source_target_pairs={{0,6},{2,4},{4,2},{6,0},{1,7},{3,5},{5,3},{7,1},{8,14},{10,12},{12... | collective-permute-start | bytes 4616 | tf_op jit(solution)/shard_map/ppermute | solution.py:710
  116.9 5.5 %collective-permute-start.75 = (f32[8,48]{1,0:T(8,128)S(1)}, f32[8,48]{1,0:T(8,128)S(1)}, u32[]{:S(2)}, u32[]{:S(2)}) collective-permute-start(f32[8,48]{1,0:T(8,128)S(1)} %kernel_sweep.11.refs_2_.refs_5_), channel_id=1, source_target_pairs={{0,8},{8,0},{16,24},{24,16},{1,9},{9,1},{17,25},{25,17},{2,10},{10... | collective-permute-start | bytes 4616 | tf_op jit(solution)/shard_map/ppermute | solution.py:710
  116.9 5.5 %collective-permute-start.74 = (f32[8,48]{1,0:T(8,128)S(1)}, f32[8,48]{1,0:T(8,128)S(1)}, u32[]{:S(2)}, u32[]{:S(2)}) collective-permute-start(f32[8,48]{1,0:T(8,128)S(1)} %kernel_sweep.11.refs_2_.refs_5_), channel_id=1, source_target_pairs={{0,6},{2,4},{4,2},{6,0},{1,7},{3,5},{5,3},{7,1},{8,14},{10,12},{12... | collective-permute-start | bytes 4616 | tf_op jit(solution)/shard_map/ppermute | solution.py:710
  125.6 5.7 %collective-permute-start.79 = (f32[3,8,128]{2,1,0:T(8,128)S(1)}, f32[3,8,128]{2,1,0:T(8,128)S(1)}, u32[]{:S(2)}, u32[]{:S(2)}) collective-permute-start(f32[3,8,128]{2,1,0:T(8,128)S(1)} %kernel_sweep_up.3.refs_1_.refs_6_), channel_id=1, source_target_pairs={{0,6},{2,4},{4,2},{6,0},{1,7},{3,5},{5,3},{7,1},{8,14},{10,12},{12... | collective-permute-start | bytes 36872 | tf_op jit(solution)/shard_map/ppermute | solution.py:710
  133.1 5.6 %collective-permute-start.81 = (f32[6,8,128]{2,1,0:T(8,128)S(1)}, f32[6,8,128]{2,1,0:T(8,128)S(1)}, u32[]{:S(2)}, u32[]{:S(2)}) collective-permute-start(f32[6,8,128]{2,1,0:T(8,128)S(1)} %get-tuple-element.75), channel_id=1, source_target_pairs={{0,8},{8,0},{16,24},{24,16},{1,9},{9,1},{17,25},{25,17},{2,10},{10... | collective-permute-start | bytes 73736 | tf_op jit(solution)/shard_map/ppermute | solution.py:710
  133.2 5.8 %collective-permute-start.82 = (f32[6,8,128]{2,1,0:T(8,128)S(1)}, f32[6,8,128]{2,1,0:T(8,128)S(1)}, u32[]{:S(2)}, u32[]{:S(2)}) collective-permute-start(f32[6,8,128]{2,1,0:T(8,128)S(1)} %get-tuple-element.76), channel_id=1, source_target_pairs={{0,6},{2,4},{4,2},{6,0},{1,7},{3,5},{5,3},{7,1},{8,14},{10,12},{12... | collective-permute-start | bytes 73736 | tf_op jit(solution)/shard_map/ppermute | solution.py:710
  141.6 5.9 %collective-permute-start.87 = (f32[6,8,128]{2,1,0:T(8,128)S(1)}, f32[6,8,128]{2,1,0:T(8,128)S(1)}, u32[]{:S(2)}, u32[]{:S(2)}) collective-permute-start(f32[6,8,128]{2,1,0:T(8,128)S(1)} %get-tuple-element.81), channel_id=1, source_target_pairs={{0,6},{2,4},{4,2},{6,0},{1,7},{3,5},{5,3},{7,1},{8,14},{10,12},{12... | collective-permute-start | bytes 73736 | tf_op jit(solution)/shard_map/ppermute | solution.py:710
  (74 other events, 321.8 us)

commit v5 on v4

--- a/solution.py
+++ b/solution.py
@@ -486,7 +486,7 @@
 
 
 def begin_fine(site, links_ref, refs):
-    sol_ref, acc_ref, t0, z1, z0, t1, x, gx_ref = refs
+    sol_ref, acc_ref, t0, x, z1, z0, t1, gx_ref = refs
     solution = load(sol_ref, 6)
     ahead_t, behind_t = by_parity("ta", load(t0, 6), load(t1, 6))
     ahead_z, behind_z = by_parity("gz", load(z0, 6), load(z1, 6))
@@ -726,7 +726,7 @@
     z1 = swap(z1, "gz", 1)
     t0 = swap(t0, "ta", 0)
     (acc,) = call(kernel_own, [TILE6], [], g, sol)
-    return [sol, acc, t0, z1, z0, t1, x, gx]
+    return [sol, acc, t0, x, z1, z0, t1, gx]
 
 
 TILE6 = (6, 8, 128)

time: 149 us -> 149 us (level)
  no operation moved by 1% of the time
where the time goes in v5:
time: 149 us
  starting transfers between devices  85.8 us (58%)
  waiting for transfers between devices  31.4 us (21%)
  Pallas kernels  25.1 us (17%)
  local copies, waits for them, and re-layouts  5.64 us (4%)
    ppermute x72, starting transfers between devices, swap(): lax.ppermute(block, axis, [(i, ((i + phase ^ 1) - phase) % n) for i in ra...  56.9 us
    ppermute x19, starting transfers between devices, from_behind(): lax.ppermute(block, axis, [((i - distance) % n, i) for i in range(n)])  28.9 us
    pallas_call x39, Pallas kernels, call(): pl.pallas_call(body, out_shape=[jax.ShapeDtypeStruct(*s) if s[1] == BF16...  25.1 us
    ppermute x72, waiting for transfers between devices, swap(): lax.ppermute(block, axis, [(i, ((i + phase ^ 1) - phase) % n) for i in ra...  19.3 us
    ppermute x19, waiting for transfers between devices, from_behind(): lax.ppermute(block, axis, [((i - distance) % n, i) for i in range(n)])  12.1 us
    reshape x1, local copies, waits for them, and re-layouts, local(): stencil2 = mid_stencil.reshape(1728, 384)  3.41 us
  transfers between devices with their start and end apart: 91, of which 36 were waited for; matrix products, arithmetic and copies ran while one was open for 2% of the time, Pallas kernels for 5%

profile of v5, /device:TPU:0, one launch (start us, length us, event | category | flops | bytes accessed | tf_op | source)
XLA Modules:
  0.0 149.0 jit_solution(5149736465086036102)
XLA Ops:
  0.6 2.0 %reshape.25.refs_0_.refs_1_ = bf16[384,768]{1,0:T(8,128)(2,1)S(1)} reshape(bf16[48,2,2,2,768]{4,3,2,1,0:T(2,128)(2,1)} %param.11) | data formatting | bytes 1179648 | tf_op jit(solution)/shard_map/reshape | solution.py:747
  2.7 1.6 %kernel_links.1 = (f32[144,8,128]{2,1,0:T(8,128)S(1)}, bf16[18,16,128]{2,1,0:T(8,128)(2,1)S(1)}) custom-call(bf16[384,768]{1,0:T(8,128)(2,1)S(1)} %reshape.25.refs_0_.refs_1_, bf16[3,3,4,4,4,256]{5,4,3,2,1,0:T(4,128)(2,1)S(1)} %copy-done.3), custom_call_target="tpu_custom_call" | custom-call | tf_op jit(solution)/shard_map/kernel_links/pallas_call | solution.py:693
  4.3 3.0 %collective-permute-start.5 = (bf16[18,16,128]{2,1,0:T(8,128)(2,1)S(1)}, bf16[18,16,128]{2,1,0:T(8,128)(2,1)S(1)}, u32[]{:S(2)}, u32[]{:S(2)}) collective-permute-start(bf16[18,16,128]{2,1,0:T(8,128)(2,1)S(1)} %get-tuple-element.50), channel_id=1, source_target_pairs={{1,0},{0,1},{3,2},{2,3},{5,4},{4,5},{7,6},{6,7},{9,8},{8,9},{11,10... | collective-permute-start | bytes 221192 | tf_op jit(solution)/shard_map/ppermute | solution.py:705
  8.4 3.7 %collective-permute-start.2 = (f32[6,8,128]{2,1,0:T(8,128)S(1)}, f32[6,8,128]{2,1,0:T(8,128)S(1)}, u32[]{:S(2)}, u32[]{:S(2)}) collective-permute-start(f32[6,8,128]{2,1,0:T(8,128)S(1)} %get-tuple-element.47), channel_id=1, source_target_pairs={{0,6},{2,4},{4,2},{6,0},{1,7},{3,5},{5,3},{7,1},{8,14},{10,12},{12... | collective-permute-start | bytes 73736 | tf_op jit(solution)/shard_map/ppermute | solution.py:710
  14.4 3.4 %reshape.26.refs_0_.refs_1_ = bf16[1728,384]{1,0:T(8,128)(2,1)S(1)} reshape(bf16[9,24,2,2,2,384]{5,4,3,2,1,0:T(2,128)(2,1)} %param.13) | data formatting | bytes 2654208 | tf_op jit(solution)/shard_map/reshape | solution.py:749
  22.9 1.6 %collective-permute-done.9.refs_9_ = f32[3,8,128]{2,1,0:T(8,128)S(1)} collective-permute-done((f32[3,8,128]{2,1,0:T(8,128)S(1)}, f32[3,8,128]{2,1,0:T(8,128)S(1)}, u32[]{:S(2)}, u32[]{:S(2)}) %collective-permute-start.9) | collective-permute-done | bytes 12320 | tf_op jit(solution)/shard_map/ppermute | solution.py:710
  26.1 3.0 %collective-permute-start.14 = (f32[8,48]{1,0:T(8,128)S(1)}, f32[8,48]{1,0:T(8,128)S(1)}, u32[]{:S(2)}, u32[]{:S(2)}) collective-permute-start(f32[8,48]{1,0:T(8,128)S(1)} %get-tuple-element.54.refs_2_.refs_3_), channel_id=1, source_target_pairs={{0,6},{2,4},{4,2},{6,0},{1,7},{3,5},{5,3},{7,1},{8,14},{10,12},{12... | collective-permute-start | bytes 4616 | tf_op jit(solution)/shard_map/ppermute | solution.py:710
  36.6 1.5 %collective-permute-start.16 = (f32[8,48]{1,0:T(8,128)S(1)}, f32[8,48]{1,0:T(8,128)S(1)}, u32[]{:S(2)}, u32[]{:S(2)}) collective-permute-start(f32[8,48]{1,0:T(8,128)S(1)} %kernel_sweep.6.refs_2_.refs_3_), channel_id=1, source_target_pairs={{1,0},{0,1},{3,2},{2,3},{5,4},{4,5},{7,6},{6,7},{9,8},{8,9},{11,10... | collective-permute-start | bytes 4616 | tf_op jit(solution)/shard_map/ppermute | solution.py:705
  40.7 2.6 %collective-permute-start.24 = (f32[8,48]{1,0:T(8,128)S(1)}, f32[8,48]{1,0:T(8,128)S(1)}, u32[]{:S(2)}, u32[]{:S(2)}) collective-permute-start(f32[8,48]{1,0:T(8,128)S(1)} %kernel_sweep.7.refs_2_.refs_3_), channel_id=1, source_target_pairs={{0,6},{2,4},{4,2},{6,0},{1,7},{3,5},{5,3},{7,1},{8,14},{10,12},{12... | collective-permute-start | bytes 4616 | tf_op jit(solution)/shard_map/ppermute | solution.py:710
  44.5 1.5 %collective-permute-start.21 = (f32[8,48]{1,0:T(8,128)S(1)}, f32[8,48]{1,0:T(8,128)S(1)}, u32[]{:S(2)}, u32[]{:S(2)}) collective-permute-start(f32[8,48]{1,0:T(8,128)S(1)} %kernel_sweep.7.refs_2_.refs_3_), channel_id=1, source_target_pairs={{1,0},{0,1},{3,2},{2,3},{5,4},{4,5},{7,6},{6,7},{9,8},{8,9},{11,10... | collective-permute-start | bytes 4616 | tf_op jit(solution)/shard_map/ppermute | solution.py:705
  55.8 2.7 %collective-permute-start.34 = (f32[3,8,128]{2,1,0:T(8,128)S(1)}, f32[3,8,128]{2,1,0:T(8,128)S(1)}, u32[]{:S(2)}, u32[]{:S(2)}) collective-permute-start(f32[3,8,128]{2,1,0:T(8,128)S(1)} %kernel_sweep_up.2.refs_1_.refs_6_), channel_id=1, source_target_pairs={{0,6},{2,4},{4,2},{6,0},{1,7},{3,5},{5,3},{7,1},{8,14},{10,12},{12... | collective-permute-start | bytes 36872 | tf_op jit(solution)/shard_map/ppermute | solution.py:710
  59.5 1.5 %collective-permute-start.31 = (f32[3,8,128]{2,1,0:T(8,128)S(1)}, f32[3,8,128]{2,1,0:T(8,128)S(1)}, u32[]{:S(2)}, u32[]{:S(2)}) collective-permute-start(f32[3,8,128]{2,1,0:T(8,128)S(1)} %kernel_sweep_up.2.refs_1_.refs_6_), channel_id=1, source_target_pairs={{1,0},{0,1},{3,2},{2,3},{5,4},{4,5},{7,6},{6,7},{9,8},{8,9},{11,10... | collective-permute-start | bytes 36872 | tf_op jit(solution)/shard_map/ppermute | solution.py:705
  68.8 1.8 %collective-permute-done.38.refs_7_ = f32[6,8,128]{2,1,0:T(8,128)S(1)} collective-permute-done((f32[6,8,128]{2,1,0:T(8,128)S(1)}, f32[6,8,128]{2,1,0:T(8,128)S(1)}, u32[]{:S(2)}, u32[]{:S(2)}) %collective-permute-start.38) | collective-permute-done | bytes 24608 | tf_op jit(solution)/shard_map/ppermute | solution.py:710
  71.8 2.7 %collective-permute-start.43 = (f32[6,8,128]{2,1,0:T(8,128)S(1)}, f32[6,8,128]{2,1,0:T(8,128)S(1)}, u32[]{:S(2)}, u32[]{:S(2)}) collective-permute-start(f32[6,8,128]{2,1,0:T(8,128)S(1)} %get-tuple-element.62), channel_id=1, source_target_pairs={{0,6},{2,4},{4,2},{6,0},{1,7},{3,5},{5,3},{7,1},{8,14},{10,12},{12... | collective-permute-start | bytes 73736 | tf_op jit(solution)/shard_map/ppermute | solution.py:710
  75.5 1.5 %collective-permute-start.42 = (f32[6,8,128]{2,1,0:T(8,128)S(1)}, f32[6,8,128]{2,1,0:T(8,128)S(1)}, u32[]{:S(2)}, u32[]{:S(2)}) collective-permute-start(f32[6,8,128]{2,1,0:T(8,128)S(1)} %get-tuple-element.60.refs_1_.refs_3_), channel_id=1, source_target_pairs={{1,0},{0,1},{3,2},{2,3},{5,4},{4,5},{7,6},{6,7},{9,8},{8,9},{11,10... | collective-permute-start | bytes 73736 | tf_op jit(solution)/shard_map/ppermute | solution.py:705
  84.2 1.8 %collective-permute-done.48.refs_9_ = f32[6,8,128]{2,1,0:T(8,128)S(1)} collective-permute-done((f32[6,8,128]{2,1,0:T(8,128)S(1)}, f32[6,8,128]{2,1,0:T(8,128)S(1)}, u32[]{:S(2)}, u32[]{:S(2)}) %collective-permute-start.48) | collective-permute-done | bytes 24608 | tf_op jit(solution)/shard_map/ppermute | solution.py:710
  87.3 2.7 %collective-permute-start.54 = (f32[3,8,128]{2,1,0:T(8,128)S(1)}, f32[3,8,128]{2,1,0:T(8,128)S(1)}, u32[]{:S(2)}, u32[]{:S(2)}) collective-permute-start(f32[3,8,128]{2,1,0:T(8,128)S(1)} %get-tuple-element.71.refs_1_.refs_4_.refs_3_), channel_id=1, source_target_pairs={{0,6},{2,4},{4,2},{6,0},{1,7},{3,5},{5,3},{7,1},{8,14},{10,12},{12... | collective-permute-start | bytes 36872 | tf_op jit(solution)/shard_map/ppermute | solution.py:710
  91.0 1.5 %collective-permute-start.51 = (f32[3,8,128]{2,1,0:T(8,128)S(1)}, f32[3,8,128]{2,1,0:T(8,128)S(1)}, u32[]{:S(2)}, u32[]{:S(2)}) collective-permute-start(f32[3,8,128]{2,1,0:T(8,128)S(1)} %get-tuple-element.71.refs_1_.refs_4_.refs_3_), channel_id=1, source_target_pairs={{1,0},{0,1},{3,2},{2,3},{5,4},{4,5},{7,6},{6,7},{9,8},{8,9},{11,10... | collective-permute-start | bytes 36872 | tf_op jit(solution)/shard_map/ppermute | solution.py:705
  102.7 2.6 %collective-permute-start.64 = (f32[8,48]{1,0:T(8,128)S(1)}, f32[8,48]{1,0:T(8,128)S(1)}, u32[]{:S(2)}, u32[]{:S(2)}) collective-permute-start(f32[8,48]{1,0:T(8,128)S(1)} %kernel_sweep.9.refs_2_.refs_3_), channel_id=1, source_target_pairs={{0,6},{2,4},{4,2},{6,0},{1,7},{3,5},{5,3},{7,1},{8,14},{10,12},{12... | collective-permute-start | bytes 4616 | tf_op jit(solution)/shard_map/ppermute | solution.py:710
  106.4 1.5 %collective-permute-start.61 = (f32[8,48]{1,0:T(8,128)S(1)}, f32[8,48]{1,0:T(8,128)S(1)}, u32[]{:S(2)}, u32[]{:S(2)}) collective-permute-start(f32[8,48]{1,0:T(8,128)S(1)} %kernel_sweep.9.refs_2_.refs_3_), channel_id=1, source_target_pairs={{1,0},{0,1},{3,2},{2,3},{5,4},{4,5},{7,6},{6,7},{9,8},{8,9},{11,10... | collective-permute-start | bytes 4616 | tf_op jit(solution)/shard_map/ppermute | solution.py:705
  116.9 2.6 %collective-permute-start.74 = (f32[8,48]{1,0:T(8,128)S(1)}, f32[8,48]{1,0:T(8,128)S(1)}, u32[]{:S(2)}, u32[]{:S(2)}) collective-permute-start(f32[8,48]{1,0:T(8,128)S(1)} %kernel_sweep.11.refs_2_.refs_5_), channel_id=1, source_target_pairs={{0,6},{2,4},{4,2},{6,0},{1,7},{3,5},{5,3},{7,1},{8,14},{10,12},{12... | collective-permute-start | bytes 4616 | tf_op jit(solution)/shard_map/ppermute | solution.py:710
  120.7 1.5 %collective-permute-start.71 = (f32[8,48]{1,0:T(8,128)S(1)}, f32[8,48]{1,0:T(8,128)S(1)}, u32[]{:S(2)}, u32[]{:S(2)}) collective-permute-start(f32[8,48]{1,0:T(8,128)S(1)} %kernel_sweep.11.refs_2_.refs_5_), channel_id=1, source_target_pairs={{1,0},{0,1},{3,2},{2,3},{5,4},{4,5},{7,6},{6,7},{9,8},{8,9},{11,10... | collective-permute-start | bytes 4616 | tf_op jit(solution)/shard_map/ppermute | solution.py:705
  133.2 2.7 %collective-permute-start.83 = (f32[6,8,128]{2,1,0:T(8,128)S(1)}, f32[6,8,128]{2,1,0:T(8,128)S(1)}, u32[]{:S(2)}, u32[]{:S(2)}) collective-permute-start(f32[6,8,128]{2,1,0:T(8,128)S(1)} %get-tuple-element.76), channel_id=1, source_target_pairs={{0,6},{2,4},{4,2},{6,0},{1,7},{3,5},{5,3},{7,1},{8,14},{10,12},{12... | collective-permute-start | bytes 73736 | tf_op jit(solution)/shard_map/ppermute | solution.py:710
  136.9 1.5 %collective-permute-start.82 = (f32[6,8,128]{2,1,0:T(8,128)S(1)}, f32[6,8,128]{2,1,0:T(8,128)S(1)}, u32[]{:S(2)}, u32[]{:S(2)}) collective-permute-start(f32[6,8,128]{2,1,0:T(8,128)S(1)} %get-tuple-element.74.refs_1_.refs_3_), channel_id=1, source_target_pairs={{1,0},{0,1},{3,2},{2,3},{5,4},{4,5},{7,6},{6,7},{9,8},{8,9},{11,10... | collective-permute-start | bytes 73736 | tf_op jit(solution)/shard_map/ppermute | solution.py:705
  (215 shorter events, 95.4 us)
Async XLA Ops:
  4.3 13.5 %collective-permute-start.5 = (bf16[18,16,128]{2,1,0:T(8,128)(2,1)S(1)}, bf16[18,16,128]{2,1,0:T(8,128)(2,1)S(1)}, u32[]{:S(2)}, u32[]{:S(2)}) collective-permute-start(bf16[18,16,128]{2,1,0:T(8,128)(2,1)S(1)} %get-tuple-element.50), channel_id=1, source_target_pairs={{1,0},{0,1},{3,2},{2,3},{5,4},{4,5},{7,6},{6,7},{9,8},{8,9},{11,10... | collective-permute-start | bytes 221192 | tf_op jit(solution)/shard_map/ppermute | solution.py:705
  8.4 9.4 %collective-permute-start.2 = (f32[6,8,128]{2,1,0:T(8,128)S(1)}, f32[6,8,128]{2,1,0:T(8,128)S(1)}, u32[]{:S(2)}, u32[]{:S(2)}) collective-permute-start(f32[6,8,128]{2,1,0:T(8,128)S(1)} %get-tuple-element.47), channel_id=1, source_target_pairs={{0,6},{2,4},{4,2},{6,0},{1,7},{3,5},{5,3},{7,1},{8,14},{10,12},{12... | collective-permute-start | bytes 73736 | tf_op jit(solution)/shard_map/ppermute | solution.py:710
  12.1 5.7 %collective-permute-start.3 = (f32[6,8,128]{2,1,0:T(8,128)S(1)}, f32[6,8,128]{2,1,0:T(8,128)S(1)}, u32[]{:S(2)}, u32[]{:S(2)}) collective-permute-start(f32[6,8,128]{2,1,0:T(8,128)S(1)} %get-tuple-element.48), channel_id=1, source_target_pairs={{0,2},{2,0},{4,6},{6,4},{1,3},{3,1},{5,7},{7,5},{8,10},{10,8},{12,... | collective-permute-start | bytes 73736 | tf_op jit(solution)/shard_map/ppermute | solution.py:710
  12.1 5.7 %collective-permute-start.4 = (f32[6,8,128]{2,1,0:T(8,128)S(1)}, f32[6,8,128]{2,1,0:T(8,128)S(1)}, u32[]{:S(2)}, u32[]{:S(2)}) collective-permute-start(f32[6,8,128]{2,1,0:T(8,128)S(1)} %get-tuple-element.49), channel_id=1, source_target_pairs={{0,24},{8,16},{16,8},{24,0},{1,25},{9,17},{17,9},{25,1},{2,26},{10... | collective-permute-start | bytes 73736 | tf_op jit(solution)/shard_map/ppermute | solution.py:710
  18.9 5.6 %collective-permute-start.9 = (f32[3,8,128]{2,1,0:T(8,128)S(1)}, f32[3,8,128]{2,1,0:T(8,128)S(1)}, u32[]{:S(2)}, u32[]{:S(2)}) collective-permute-start(f32[3,8,128]{2,1,0:T(8,128)S(1)} %get-tuple-element.52.refs_1_.refs_4_.refs_3_), channel_id=1, source_target_pairs={{0,6},{2,4},{4,2},{6,0},{1,7},{3,5},{5,3},{7,1},{8,14},{10,12},{12... | collective-permute-start | bytes 36872 | tf_op jit(solution)/shard_map/ppermute | solution.py:710
  26.1 5.8 %collective-permute-start.15 = (f32[8,48]{1,0:T(8,128)S(1)}, f32[8,48]{1,0:T(8,128)S(1)}, u32[]{:S(2)}, u32[]{:S(2)}) collective-permute-start(f32[8,48]{1,0:T(8,128)S(1)} %get-tuple-element.54.refs_2_.refs_3_), channel_id=1, source_target_pairs={{0,8},{8,0},{16,24},{24,16},{1,9},{9,1},{17,25},{25,17},{2,10},{10... | collective-permute-start | bytes 4616 | tf_op jit(solution)/shard_map/ppermute | solution.py:710
  26.1 5.8 %collective-permute-start.14 = (f32[8,48]{1,0:T(8,128)S(1)}, f32[8,48]{1,0:T(8,128)S(1)}, u32[]{:S(2)}, u32[]{:S(2)}) collective-permute-start(f32[8,48]{1,0:T(8,128)S(1)} %get-tuple-element.54.refs_2_.refs_3_), channel_id=1, source_target_pairs={{0,6},{2,4},{4,2},{6,0},{1,7},{3,5},{5,3},{7,1},{8,14},{10,12},{12... | collective-permute-start | bytes 4616 | tf_op jit(solution)/shard_map/ppermute | solution.py:710
  40.7 5.5 %collective-permute-start.25 = (f32[8,48]{1,0:T(8,128)S(1)}, f32[8,48]{1,0:T(8,128)S(1)}, u32[]{:S(2)}, u32[]{:S(2)}) collective-permute-start(f32[8,48]{1,0:T(8,128)S(1)} %kernel_sweep.7.refs_2_.refs_3_), channel_id=1, source_target_pairs={{0,8},{8,0},{16,24},{24,16},{1,9},{9,1},{17,25},{25,17},{2,10},{10... | collective-permute-start | bytes 4616 | tf_op jit(solution)/shard_map/ppermute | solution.py:710
  40.7 5.5 %collective-permute-start.24 = (f32[8,48]{1,0:T(8,128)S(1)}, f32[8,48]{1,0:T(8,128)S(1)}, u32[]{:S(2)}, u32[]{:S(2)}) collective-permute-start(f32[8,48]{1,0:T(8,128)S(1)} %kernel_sweep.7.refs_2_.refs_3_), channel_id=1, source_target_pairs={{0,6},{2,4},{4,2},{6,0},{1,7},{3,5},{5,3},{7,1},{8,14},{10,12},{12... | collective-permute-start | bytes 4616 | tf_op jit(solution)/shard_map/ppermute | solution.py:710
  55.7 5.8 %collective-permute-start.35 = (f32[3,8,128]{2,1,0:T(8,128)S(1)}, f32[3,8,128]{2,1,0:T(8,128)S(1)}, u32[]{:S(2)}, u32[]{:S(2)}) collective-permute-start(f32[3,8,128]{2,1,0:T(8,128)S(1)} %kernel_sweep_up.2.refs_1_.refs_6_), channel_id=1, source_target_pairs={{0,8},{8,0},{16,24},{24,16},{1,9},{9,1},{17,25},{25,17},{2,10},{10... | collective-permute-start | bytes 36872 | tf_op jit(solution)/shard_map/ppermute | solution.py:710
  55.8 5.7 %collective-permute-start.34 = (f32[3,8,128]{2,1,0:T(8,128)S(1)}, f32[3,8,128]{2,1,0:T(8,128)S(1)}, u32[]{:S(2)}, u32[]{:S(2)}) collective-permute-start(f32[3,8,128]{2,1,0:T(8,128)S(1)} %kernel_sweep_up.2.refs_1_.refs_6_), channel_id=1, source_target_pairs={{0,6},{2,4},{4,2},{6,0},{1,7},{3,5},{5,3},{7,1},{8,14},{10,12},{12... | collective-permute-start | bytes 36872 | tf_op jit(solution)/shard_map/ppermute | solution.py:710
  64.8 5.9 %collective-permute-start.38 = (f32[6,8,128]{2,1,0:T(8,128)S(1)}, f32[6,8,128]{2,1,0:T(8,128)S(1)}, u32[]{:S(2)}, u32[]{:S(2)}) collective-permute-start(f32[6,8,128]{2,1,0:T(8,128)S(1)} %get-tuple-element.57), channel_id=1, source_target_pairs={{0,6},{2,4},{4,2},{6,0},{1,7},{3,5},{5,3},{7,1},{8,14},{10,12},{12... | collective-permute-start | bytes 73736 | tf_op jit(solution)/shard_map/ppermute | solution.py:710
  71.7 5.6 %collective-permute-start.41 = (f32[6,8,128]{2,1,0:T(8,128)S(1)}, f32[6,8,128]{2,1,0:T(8,128)S(1)}, u32[]{:S(2)}, u32[]{:S(2)}) collective-permute-start(f32[6,8,128]{2,1,0:T(8,128)S(1)} %get-tuple-element.61), channel_id=1, source_target_pairs={{0,8},{8,0},{16,24},{24,16},{1,9},{9,1},{17,25},{25,17},{2,10},{10... | collective-permute-start | bytes 73736 | tf_op jit(solution)/shard_map/ppermute | solution.py:710
  71.8 5.7 %collective-permute-start.43 = (f32[6,8,128]{2,1,0:T(8,128)S(1)}, f32[6,8,128]{2,1,0:T(8,128)S(1)}, u32[]{:S(2)}, u32[]{:S(2)}) collective-permute-start(f32[6,8,128]{2,1,0:T(8,128)S(1)} %get-tuple-element.62), channel_id=1, source_target_pairs={{0,6},{2,4},{4,2},{6,0},{1,7},{3,5},{5,3},{7,1},{8,14},{10,12},{12... | collective-permute-start | bytes 73736 | tf_op jit(solution)/shard_map/ppermute | solution.py:710
  80.2 5.9 %collective-permute-start.48 = (f32[6,8,128]{2,1,0:T(8,128)S(1)}, f32[6,8,128]{2,1,0:T(8,128)S(1)}, u32[]{:S(2)}, u32[]{:S(2)}) collective-permute-start(f32[6,8,128]{2,1,0:T(8,128)S(1)} %get-tuple-element.67), channel_id=1, source_target_pairs={{0,6},{2,4},{4,2},{6,0},{1,7},{3,5},{5,3},{7,1},{8,14},{10,12},{12... | collective-permute-start | bytes 73736 | tf_op jit(solution)/shard_map/ppermute | solution.py:710
  87.3 5.8 %collective-permute-start.55 = (f32[3,8,128]{2,1,0:T(8,128)S(1)}, f32[3,8,128]{2,1,0:T(8,128)S(1)}, u32[]{:S(2)}, u32[]{:S(2)}) collective-permute-start(f32[3,8,128]{2,1,0:T(8,128)S(1)} %get-tuple-element.71.refs_1_.refs_4_.refs_3_), channel_id=1, source_target_pairs={{0,8},{8,0},{16,24},{24,16},{1,9},{9,1},{17,25},{25,17},{2,10},{10... | collective-permute-start | bytes 36872 | tf_op jit(solution)/shard_map/ppermute | solution.py:710
  87.3 5.7 %collective-permute-start.54 = (f32[3,8,128]{2,1,0:T(8,128)S(1)}, f32[3,8,128]{2,1,0:T(8,128)S(1)}, u32[]{:S(2)}, u32[]{:S(2)}) collective-permute-start(f32[3,8,128]{2,1,0:T(8,128)S(1)} %get-tuple-element.71.refs_1_.refs_4_.refs_3_), channel_id=1, source_target_pairs={{0,6},{2,4},{4,2},{6,0},{1,7},{3,5},{5,3},{7,1},{8,14},{10,12},{12... | collective-permute-start | bytes 36872 | tf_op jit(solution)/shard_map/ppermute | solution.py:710
  102.7 5.5 %collective-permute-start.64 = (f32[8,48]{1,0:T(8,128)S(1)}, f32[8,48]{1,0:T(8,128)S(1)}, u32[]{:S(2)}, u32[]{:S(2)}) collective-permute-start(f32[8,48]{1,0:T(8,128)S(1)} %kernel_sweep.9.refs_2_.refs_3_), channel_id=1, source_target_pairs={{0,6},{2,4},{4,2},{6,0},{1,7},{3,5},{5,3},{7,1},{8,14},{10,12},{12... | collective-permute-start | bytes 4616 | tf_op jit(solution)/shard_map/ppermute | solution.py:710
  116.9 5.5 %collective-permute-start.75 = (f32[8,48]{1,0:T(8,128)S(1)}, f32[8,48]{1,0:T(8,128)S(1)}, u32[]{:S(2)}, u32[]{:S(2)}) collective-permute-start(f32[8,48]{1,0:T(8,128)S(1)} %kernel_sweep.11.refs_2_.refs_5_), channel_id=1, source_target_pairs={{0,8},{8,0},{16,24},{24,16},{1,9},{9,1},{17,25},{25,17},{2,10},{10... | collective-permute-start | bytes 4616 | tf_op jit(solution)/shard_map/ppermute | solution.py:710
  116.9 5.5 %collective-permute-start.74 = (f32[8,48]{1,0:T(8,128)S(1)}, f32[8,48]{1,0:T(8,128)S(1)}, u32[]{:S(2)}, u32[]{:S(2)}) collective-permute-start(f32[8,48]{1,0:T(8,128)S(1)} %kernel_sweep.11.refs_2_.refs_5_), channel_id=1, source_target_pairs={{0,6},{2,4},{4,2},{6,0},{1,7},{3,5},{5,3},{7,1},{8,14},{10,12},{12... | collective-permute-start | bytes 4616 | tf_op jit(solution)/shard_map/ppermute | solution.py:710
  125.6 5.7 %collective-permute-start.79 = (f32[3,8,128]{2,1,0:T(8,128)S(1)}, f32[3,8,128]{2,1,0:T(8,128)S(1)}, u32[]{:S(2)}, u32[]{:S(2)}) collective-permute-start(f32[3,8,128]{2,1,0:T(8,128)S(1)} %kernel_sweep_up.3.refs_1_.refs_6_), channel_id=1, source_target_pairs={{0,6},{2,4},{4,2},{6,0},{1,7},{3,5},{5,3},{7,1},{8,14},{10,12},{12... | collective-permute-start | bytes 36872 | tf_op jit(solution)/shard_map/ppermute | solution.py:710
  133.1 5.6 %collective-permute-start.81 = (f32[6,8,128]{2,1,0:T(8,128)S(1)}, f32[6,8,128]{2,1,0:T(8,128)S(1)}, u32[]{:S(2)}, u32[]{:S(2)}) collective-permute-start(f32[6,8,128]{2,1,0:T(8,128)S(1)} %get-tuple-element.75), channel_id=1, source_target_pairs={{0,8},{8,0},{16,24},{24,16},{1,9},{9,1},{17,25},{25,17},{2,10},{10... | collective-permute-start | bytes 73736 | tf_op jit(solution)/shard_map/ppermute | solution.py:710
  133.2 5.8 %collective-permute-start.83 = (f32[6,8,128]{2,1,0:T(8,128)S(1)}, f32[6,8,128]{2,1,0:T(8,128)S(1)}, u32[]{:S(2)}, u32[]{:S(2)}) collective-permute-start(f32[6,8,128]{2,1,0:T(8,128)S(1)} %get-tuple-element.76), channel_id=1, source_target_pairs={{0,6},{2,4},{4,2},{6,0},{1,7},{3,5},{5,3},{7,1},{8,14},{10,12},{12... | collective-permute-start | bytes 73736 | tf_op jit(solution)/shard_map/ppermute | solution.py:710
  141.6 5.9 %collective-permute-start.88 = (f32[6,8,128]{2,1,0:T(8,128)S(1)}, f32[6,8,128]{2,1,0:T(8,128)S(1)}, u32[]{:S(2)}, u32[]{:S(2)}) collective-permute-start(f32[6,8,128]{2,1,0:T(8,128)S(1)} %get-tuple-element.81), channel_id=1, source_target_pairs={{0,6},{2,4},{4,2},{6,0},{1,7},{3,5},{5,3},{7,1},{8,14},{10,12},{12... | collective-permute-start | bytes 73736 | tf_op jit(solution)/shard_map/ppermute | solution.py:710
  (74 other events, 321.8 us)
